TPU v7x, 512 devices: a whole 4x8x8 slice. The times are simulated.
512 devices in a mesh: slab: 16 (over y, core), space: 32 (over z, x).
Axes of the slice: x: 4, y: 8, z: 8, core: 2. Of those that a mesh axis runs over, the one named last changes fastest.
Arguments:
- latent: bfloat16 [16, 4, 64, 32, 512], P('slab', None, 'space'), may hold values from -6.5 to 6.5
- gamma: float32 [512], replicated, may hold values from 0.25 to 1.75
- beta: float32 [512], replicated, may hold values from -3 to 3
- smooth: float32 [512], replicated, may hold values from 0.5 to 4
- weights: bfloat16 [3, 3, 3, 512, 256], P(None, None, None, 'space'), may hold values from -127 to 127, as said below
- w_scale: float32 [256], replicated, may hold values from 0.00017010345 to 0.0006804138
- bias: float32 [256], replicated, may hold values from -3 to 3
- lengths: int32 [10], replicated, may hold values from 1 to 8, 64 in all
- order: int32 [64], replicated, may hold values from 0 to 63, each once
Outputs:
- decoded: bfloat16 [16, 4, 64, 32, 256], P(None, None, 'space', 'slab')
Inputs may be any that keep to these rules, and one draw needn't show every extreme that they name: `weights`: whole numbers. `order`: each frame once.
All inputs are finite; a program needn't handle non-finite values.
Results may differ from a plain program's by a relative error of at most 0.00165.
The roundings to bfloat16 on the way count: a program that leaves them out, or rounds other values in their place, can miss the bound.
Values may be sent and summed in bfloat16 or wider, within the bound.
No kernel may reach another device: no remote copies, remote signals or barrier semaphores. Data moves between devices by JAX's collectives and lax.ppermute only.
A program may use at most 64 MiB of HBM per device.

v0:
```python
import jax
import jax.numpy as jnp
from jax import lax
from jax.sharding import PartitionSpec as P

GROUPS = 32


epsilon = 1e-06
highest = lax.Precision.HIGHEST


def entering(value, axis, join, neutral, backward):
    count, mine = (lax.axis_size(axis), lax.axis_index(axis))
    pieces = jax.tree.map(lambda part: lax.all_gather(part, axis), value)
    if backward:
        pieces = jax.tree.map(lambda part: part[::-1], pieces)
        mine = count - 1 - mine
    so_far = jax.tree.map(
        lambda part, zero: jnp.full_like(part, 0) + jnp.asarray(zero, part.dtype), value, neutral
    )

    def step(position, so_far):
        longer = join(so_far, jax.tree.map(lambda part: part[position], pieces))
        return jax.tree.map(lambda new, old: jnp.where(position < mine, new, old), longer, so_far)

    return lax.fori_loop(0, count - 1, step, so_far)


def with_halo(cells, sides, width):
    for axis, dim in sides:
        count = lax.axis_size(axis)
        ends = count - 1
        head = lax.slice_in_dim(cells, 0, width, axis=dim)
        tail = lax.slice_in_dim(cells, cells.shape[dim] - width, cells.shape[dim], axis=dim)
        cells = jnp.concatenate(
            [
                lax.ppermute(tail, axis, [(i, (i + 1) % count) for i in range(ends)]),
                cells,
                lax.ppermute(head, axis, [((i + 1) % count, i) for i in range(ends)]),
            ],
            axis=dim,
        )
    return cells


def from_behind(shard, axis, by):
    devices = lax.axis_size(axis)
    pairs = [(i, i + by) for i in range(devices) if 0 <= i + by < devices]
    return lax.ppermute(shard, axis, pairs)


def clip_index(clip_ends, frame_ids):
    return jnp.sum((clip_ends[None, :] <= frame_ids[:, None]).astype(jnp.int32), axis=1)


def joined_sums(earlier, latter):
    flagged = jnp.maximum(earlier[0], latter[0])
    return (flagged, jnp.where(latter[0] > 0.5, latter[1], earlier[1] + latter[1]))


def clip_totals(frame_sums, clip_local, clip_prev, clip_next):
    row_sums = lax.psum(frame_sums, "space")
    frames_dev = clip_local.shape[0]
    same_clip = (clip_local[:, None] == clip_local[None, :]).astype(jnp.float32)
    local_sums = jnp.dot(same_clip, row_sums, precision=highest)
    first_clip = clip_local[0]
    last_clip = clip_local[frames_dev - 1]
    cut_forward = ((first_clip != last_clip) | (clip_prev != last_clip)).astype(jnp.float32)
    cut_backward = ((first_clip != last_clip) | (clip_next != first_clip)).astype(jnp.float32)
    identity = (jnp.float32(0.0), jnp.zeros_like(local_sums[0]))
    flag_before, sums_before = entering(
        (cut_forward, local_sums[frames_dev - 1]), "slab", joined_sums, identity, False
    )
    flag_after, sums_after = entering(
        (cut_backward, local_sums[0]), "slab", joined_sums, identity, True
    )
    running = local_sums + jnp.where((clip_local == clip_prev)[:, None], sums_before[None, :], 0.0)
    return running + jnp.where((clip_local == clip_next)[:, None], sums_after[None, :], 0.0)


def local(latent, gamma, beta, smooth, weights, w_scale, bias, lengths, order):
    frames_dev = latent.shape[1]
    rows_dev = latent.shape[2]
    width = latent.shape[3]
    channels = latent.shape[4]
    slab_index = lax.axis_index("slab")
    first_frame = slab_index * frames_dev
    clip_ends = jnp.cumsum(lengths)
    clip_starts = clip_ends - lengths
    frame_ids = first_frame + jnp.arange(frames_dev, dtype=jnp.int32)
    clip_local = clip_index(clip_ends, frame_ids)
    border_clips = clip_index(clip_ends, jnp.stack([first_frame - 1, first_frame + frames_dev]))
    clip_prev = jnp.where(slab_index > 0, border_clips[0], -1)
    clip_next = border_clips[1]
    member = clip_local[:, None] == jnp.arange(lengths.shape[0], dtype=jnp.int32)[None, :]
    onehot_local = member.astype(jnp.float32)
    start_local = jnp.sum(jnp.where(member, clip_starts[None, :], 0), axis=1)
    frame_cells = float(rows_dev * lax.axis_size("space") * width * (channels // GROUPS))
    clip_cells = jnp.dot(onehot_local, lengths.astype(jnp.float32), precision=highest) * frame_cells
    values = (
        latent[0]
        .astype(jnp.float32)
        .reshape(frames_dev, rows_dev * width, GROUPS, channels // GROUPS)
    )
    averages = (
        clip_totals(jnp.sum(values, axis=(1, 3)), clip_local, clip_prev, clip_next)
        / clip_cells[:, None]
    )
    centered = values - averages[:, None, :, None]
    variance = (
        clip_totals(jnp.sum(centered * centered, axis=(1, 3)), clip_local, clip_prev, clip_next)
        / clip_cells[:, None]
    )
    inverse_std = lax.rsqrt(variance + epsilon)
    normed = (centered * inverse_std[:, None, :, None]).reshape(
        frames_dev, rows_dev, width, channels
    ) * gamma + beta
    activated = (jax.nn.silu(normed) / smooth).astype(jnp.bfloat16)
    framed_own = with_halo(activated, (("space", 1),), 1)
    carried = from_behind(framed_own[frames_dev - 2 :], "slab", 1)
    framed = jnp.concatenate([carried, framed_own], axis=0)
    framed = jnp.pad(framed, ((0, 0), (0, 0), (1, 1), (0, 0)))
    start_slot = start_local - first_frame + 2
    slot_index = jnp.arange(frames_dev + 2, dtype=jnp.int32)
    picker = (slot_index[None, :] == start_slot[:, None]).astype(jnp.bfloat16)
    start_planes = jnp.einsum(
        "fe,erwc->frwc", picker, framed, preferred_element_type=jnp.float32
    ).astype(jnp.bfloat16)
    local_ids = jnp.arange(frames_dev, dtype=jnp.int32)
    tap_planes = []
    for t_tap in range(3):
        keep_own = local_ids + t_tap >= start_slot
        tap_planes.append(
            jnp.where(
                keep_own[:, None, None, None], framed[t_tap : t_tap + frames_dev], start_planes
            )
        )
    tap_planes = jnp.stack(tap_planes, axis=0)
    out_channels = weights.shape[4]
    empty = jnp.zeros((frames_dev * rows_dev * width, out_channels), jnp.float32)
    running = empty
    piece = lax.all_gather(weights, "space", axis=3, tiled=True)
    piece_width = piece.shape[3]
    for t_tap in range(3):
        for h_tap in range(3):
            for w_tap in range(3):
                tap_rows = tap_planes[
                    t_tap, :, h_tap : h_tap + rows_dev, w_tap : w_tap + width, :
                ].reshape(frames_dev * rows_dev * width, piece_width)
                running = running + jnp.dot(
                    tap_rows, piece[t_tap, h_tap, w_tap], preferred_element_type=jnp.float32
                )
    result = (
        (running * w_scale + bias)
        .astype(jnp.bfloat16)
        .reshape(1, frames_dev, rows_dev, width, out_channels)
    )
    returned = lax.all_to_all(result, "slab", split_axis=3, concat_axis=0, tiled=True)
    slab_count = returned.shape[0]
    column_share = returned.shape[3]
    flat_frames = returned.reshape(slab_count * frames_dev, rows_dev, column_share, out_channels)
    picked = jnp.take(flat_frames, order, axis=0)
    return picked.reshape(slab_count, frames_dev, rows_dev, column_share, out_channels)


def solution(mesh):
    in_specs = (
        P("slab", None, "space", None, None),
        P(),
        P(),
        P(),
        P(None, None, None, "space", None),
        P(),
        P(),
        P(),
        P(),
    )
    out_specs = P(None, None, "space", "slab", None)
    return jax.shard_map(local, mesh=mesh, in_specs=in_specs, out_specs=out_specs, check_vma=False)
```

profile of v0, /device:TPU:1, one launch (start us, length us, event | category | flops | bytes accessed | tf_op | source)
XLA Modules:
  0.0 411.5 jit_solution(2460495483026409674)
XLA Ops:
  15.0 1.2 convert_reduce_fusion
  16.3 67.9 %psum.14 = f32[4,32]{1,0:T(4,128)S(1)} all-reduce(f32[4,32]{1,0:T(4,128)S(1)} %reduce_sum.63), channel_id=1, replica_groups=mesh['slab'=16,'space'=32] {'space'}, use_global_device_ids=true, to_apply=%region_5.6 | all-reduce | flops 128 | bytes 1024 | tf_op jit(solution)/shard_map/psum | solution.py:63
  84.4 1.4 dynamic-slice
  87.4 38.6 %all-reduce.3 = (f32[16]{0:T(128)S(1)}, f32[16]{0:T(128)S(1)}) all-reduce(f32[16]{0:T(128)S(1)} %dynamic-update-slice.1, f32[16]{0:T(128)S(1)} %dynamic-update-slice), channel_id=1, replica_groups=mesh['slab'=16,'space'=32] {'slab'}, use_global_device_ids=true, to_apply=%add.2 | all-reduce | flops 32 | bytes 256
  126.0 15.7 %all-gather.1 = f32[16,1,32]{2,1,0:T(1,128)S(1)} all-gather(f32[1,1,32]{2,1,0:T(1,128)S(1)} %get-tuple-element.536), channel_id=1, replica_groups=mesh['slab'=16,'space'=32] {'slab'}, dimensions={0}, use_global_device_ids=true | all-gather | bytes 2176 | tf_op jit(solution)/shard_map/all_gather | solution.py:15
  141.8 17.4 %while.57 = (s32[]{:T(128)}, f32[32]{0:T(128)S(1)}, s32[]{:T(128)}, f32[16]{0:T(128)S(1)}, f32[16,32]{1,0:T(8,128)S(1)}, /*index=5*/s32[]{:T(128)}, f32[1]{0:T(128)}, s32[]{:T(128)}) while((s32[]{:T(128)}, f32[32]{0:T(128)S(1)}, s32[]{:T(128)}, f32[16]{0:T(128)S(1)}, f32[16,32]{1,0:T(8,128)S(1)}, /*index=5*/s32[]{:T(128)}, ...), condition=%wide.region_10.11_spmd.clone, body=%wide.region_9.10_spmd.clone.sunk | while | flops 133 | bytes 523 | solution.py:27
  159.2 17.2 %all-gather = f32[16,1,32]{2,1,0:T(1,128)S(1)} all-gather(f32[1,1,32]{2,1,0:T(1,128)S(1)} %get-tuple-element.535), channel_id=1, replica_groups=mesh['slab'=16,'space'=32] {'slab'}, dimensions={0}, use_global_device_ids=true | all-gather | bytes 2176 | tf_op jit(solution)/shard_map/all_gather | solution.py:15
  176.4 18.9 %while.56 = (s32[]{:T(128)}, f32[32]{0:T(128)S(1)}, s32[]{:T(128)}, f32[16]{0:T(128)S(1)}, f32[16,32]{1,0:T(8,128)S(1)}, /*index=5*/s32[]{:T(128)}, f32[1]{0:T(128)}, s32[]{:T(128)}) while((s32[]{:T(128)}, f32[32]{0:T(128)S(1)}, s32[]{:T(128)}, f32[16]{0:T(128)S(1)}, f32[16,32]{1,0:T(8,128)S(1)}, /*index=5*/s32[]{:T(128)}, ...), condition=%wide.region_8.9_spmd.clone, body=%wide.region_7.8_spmd.clone.sunk | while | flops 133 | bytes 523 | solution.py:27
  195.6 1.2 fusion.18
  197.0 55.9 %psum.15 = f32[4,32]{1,0:T(4,128)S(1)} all-reduce(f32[4,32]{1,0:T(4,128)S(1)} %reduce_sum.67), channel_id=1, replica_groups=mesh['slab'=16,'space'=32] {'space'}, use_global_device_ids=true, to_apply=%region_13.14 | all-reduce | flops 128 | bytes 1024 | tf_op jit(solution)/shard_map/psum | solution.py:63
  253.0 27.8 %all-gather.3 = f32[16,1,32]{2,1,0:T(1,128)S(1)} all-gather(f32[1,1,32]{2,1,0:T(1,128)S(1)} %get-tuple-element.534), channel_id=1, replica_groups=mesh['slab'=16,'space'=32] {'slab'}, dimensions={0}, use_global_device_ids=true | all-gather | bytes 2176 | tf_op jit(solution)/shard_map/all_gather | solution.py:15
  280.9 16.0 %all-gather.2 = f32[16,1,32]{2,1,0:T(1,128)S(1)} all-gather(f32[1,1,32]{2,1,0:T(1,128)S(1)} %get-tuple-element.533), channel_id=1, replica_groups=mesh['slab'=16,'space'=32] {'slab'}, dimensions={0}, use_global_device_ids=true | all-gather | bytes 2176 | tf_op jit(solution)/shard_map/all_gather | solution.py:15
  296.8 20.8 %while.59 = (s32[]{:T(128)}, f32[32]{0:T(128)S(1)}, s32[]{:T(128)}, f32[16]{0:T(128)S(1)}, f32[16,32]{1,0:T(8,128)S(1)}, /*index=5*/s32[]{:T(128)}, f32[1]{0:T(128)}, s32[]{:T(128)}) while((s32[]{:T(128)}, f32[32]{0:T(128)S(1)}, s32[]{:T(128)}, f32[16]{0:T(128)S(1)}, f32[16,32]{1,0:T(8,128)S(1)}, /*index=5*/s32[]{:T(128)}, ...), condition=%wide.region_17.18_spmd.clone, body=%wide.region_16.17_spmd.clone.sunk | while | flops 133 | bytes 523 | solution.py:27
  317.7 19.1 %while.58 = (s32[]{:T(128)}, f32[32]{0:T(128)S(1)}, s32[]{:T(128)}, f32[16]{0:T(128)S(1)}, f32[16,32]{1,0:T(8,128)S(1)}, /*index=5*/s32[]{:T(128)}, f32[1]{0:T(128)}, s32[]{:T(128)}) while((s32[]{:T(128)}, f32[32]{0:T(128)S(1)}, s32[]{:T(128)}, f32[16]{0:T(128)S(1)}, f32[16,32]{1,0:T(8,128)S(1)}, /*index=5*/s32[]{:T(128)}, ...), condition=%wide.region_15.16_spmd.clone, body=%wide.region_14.15_spmd.clone.sunk | while | flops 133 | bytes 523 | solution.py:27
  337.0 1.5 fusion.20
  338.6 1.3 collective-permute-start.1
  339.9 4.3 %collective-permute-start = (bf16[4,1,32,512]{3,0,2,1:T(4,128)(2,1)S(1)}, bf16[4,1,32,512]{3,0,2,1:T(4,128)(2,1)S(1)}, u32[]{:S(2)}, u32[]{:S(2)}) collective-permute-start(bf16[4,1,32,512]{3,0,2,1:T(4,128)(2,1)S(1)} %get-tuple-element.531), channel_id=1, source_target_pairs={{0,1},{1,2},{2,3},{3,4},{4,5},{5,6},{6,7},{7,8},{8,9},{9,10},{10,1... | collective-permute-start | bytes 393224 | tf_op jit(solution)/shard_map/ppermute | solution.py:38
  345.1 0.9 collective-permute-done.1
  346.0 0.9 collective-permute-done
  347.2 2.8 collective-permute-start.2
  350.7 2.3 collective-permute-done.2
  353.6 1.3 fusion.10
  356.1 2.6 fusion.35
  369.6 1.3 fusion.21
  371.0 1.8 convolution_add_fusion.25
  372.7 1.2 convolution_add_fusion.24
  374.0 1.2 convolution_add_fusion.23
  375.2 1.2 convolution_add_fusion.22
  376.5 1.2 convolution_add_fusion.21
  377.7 1.2 convolution_add_fusion.20
  384.7 8.9 %all-to-all-start = ((bf16[1,4,2,32,256]{4,2,1,0,3:T(2,128)(2,1)}), bf16[1,4,2,32,256]{4,2,1,0,3:T(2,128)(2,1)S(1)}, u32[]{:S(2)}, u32[]{:S(2)}) async-start(bf16[1,4,2,32,256]{4,2,1,0,3:T(2,128)(2,1)} %copy.128), calls=%async_computation | async-start | bytes 262144 | tf_op jit(solution)/shard_map/all_to_all | solution.py:159
  393.6 9.1 %all-to-all-done = bf16[1,4,2,32,256]{4,2,1,0,3:T(2,128)(2,1)S(1)} async-done(((bf16[1,4,2,32,256]{4,2,1,0,3:T(2,128)(2,1)}), bf16[1,4,2,32,256]{4,2,1,0,3:T(2,128)(2,1)S(1)}, u32[]{:S(2)}, u32[]{:S(2)}) %all-to-all-start) | async-done | bytes 131104 | tf_op jit(solution)/shard_map/all_to_all | solution.py:159
  (257 shorter events, 66.8 us)
Async XLA Ops:
  6.5 363.0 %all-gather.6.cloned.1.call-start = ((), (), s32[]{:S(2)}) async-start(), calls=%async_computation.1 | async-start | bytes 7299072 | tf_op jit(solution)/shard_map/all_gather | solution.py:143
  338.6 7.4 %collective-permute-start.1 = (bf16[4,1,32,512]{3,0,2,1:T(4,128)(2,1)S(1)}, bf16[4,1,32,512]{3,0,2,1:T(4,128)(2,1)S(1)}, u32[]{:S(2)}, u32[]{:S(2)}) collective-permute-start(bf16[4,1,32,512]{3,0,2,1:T(4,128)(2,1)S(1)} %get-tuple-element.532), channel_id=1, source_target_pairs={{1,0},{2,1},{3,2},{4,3},{5,4},{6,5},{7,6},{8,7},{9,8},{10,9},{11,1... | collective-permute-start | bytes 393224 | tf_op jit(solution)/shard_map/ppermute | solution.py:40
  339.9 6.9 %collective-permute-start = (bf16[4,1,32,512]{3,0,2,1:T(4,128)(2,1)S(1)}, bf16[4,1,32,512]{3,0,2,1:T(4,128)(2,1)S(1)}, u32[]{:S(2)}, u32[]{:S(2)}) collective-permute-start(bf16[4,1,32,512]{3,0,2,1:T(4,128)(2,1)S(1)} %get-tuple-element.531), channel_id=1, source_target_pairs={{0,1},{1,2},{2,3},{3,4},{4,5},{5,6},{6,7},{7,8},{8,9},{9,10},{10,1... | collective-permute-start | bytes 393224 | tf_op jit(solution)/shard_map/ppermute | solution.py:38
  347.2 5.9 %collective-permute-start.2 = (bf16[2,4,32,512]{3,0,2,1:T(2,128)(2,1)S(1)}, bf16[2,4,32,512]{3,0,2,1:T(2,128)(2,1)S(1)}, u32[]{:S(2)}, u32[]{:S(2)}) collective-permute-start(bf16[2,4,32,512]{3,0,2,1:T(2,128)(2,1)S(1)} %pad_maximum_fusion), channel_id=1, source_target_pairs={{0,32},{32,64},{64,96},{96,128},{128,160},{160,192},{192,224},{224... | collective-permute-start | bytes 786440 | tf_op jit(solution)/shard_map/ppermute | solution.py:50
  369.6 9.4 %copy-start = (bf16[3,3,3,512,256]{4,3,2,1,0:T(8,128)(2,1)S(1)}, bf16[3,3,3,512,256]{4,3,2,1,0:T(8,128)(2,1)}, u32[]{:S(2)}) copy-start(bf16[3,3,3,512,256]{4,3,2,1,0:T(8,128)(2,1)} %all-gather.6.cloned.1.call-done) | copy-start | bytes 21233668
  369.6 9.9 %copy-start.14 = (bf16[1,4,2,32,512]{4,3,2,1,0:T(8,128)(2,1)S(1)}, bf16[1,4,2,32,512]{4,3,2,1,0:T(8,128)(2,1)}, u32[]{:S(2)}) copy-start(bf16[1,4,2,32,512]{4,3,2,1,0:T(8,128)(2,1)} %copy.110) | copy-start | bytes 786436
  369.6 10.1 %copy-start.13 = (bf16[1,4,2,32,512]{4,3,2,1,0:T(8,128)(2,1)S(1)}, bf16[1,4,2,32,512]{4,3,2,1,0:T(8,128)(2,1)}, u32[]{:S(2)}) copy-start(bf16[1,4,2,32,512]{4,3,2,1,0:T(8,128)(2,1)} %copy.111) | copy-start | bytes 786436
  369.6 10.3 %copy-start.12 = (bf16[1,4,2,32,512]{4,3,2,1,0:T(8,128)(2,1)S(1)}, bf16[1,4,2,32,512]{4,3,2,1,0:T(8,128)(2,1)}, u32[]{:S(2)}) copy-start(bf16[1,4,2,32,512]{4,3,2,1,0:T(8,128)(2,1)} %copy.112) | copy-start | bytes 786436
  369.6 10.6 %copy-start.11 = (bf16[1,4,2,32,512]{4,3,2,1,0:T(8,128)(2,1)S(1)}, bf16[1,4,2,32,512]{4,3,2,1,0:T(8,128)(2,1)}, u32[]{:S(2)}) copy-start(bf16[1,4,2,32,512]{4,3,2,1,0:T(8,128)(2,1)} %copy.113) | copy-start | bytes 786436
  369.6 10.8 %copy-start.10 = (bf16[1,4,2,32,512]{4,3,2,1,0:T(8,128)(2,1)S(1)}, bf16[1,4,2,32,512]{4,3,2,1,0:T(8,128)(2,1)}, u32[]{:S(2)}) copy-start(bf16[1,4,2,32,512]{4,3,2,1,0:T(8,128)(2,1)} %copy.114) | copy-start | bytes 786436
  369.6 11.1 %copy-start.9 = (bf16[1,4,2,32,512]{4,3,2,1,0:T(8,128)(2,1)S(1)}, bf16[1,4,2,32,512]{4,3,2,1,0:T(8,128)(2,1)}, u32[]{:S(2)}) copy-start(bf16[1,4,2,32,512]{4,3,2,1,0:T(8,128)(2,1)} %copy.115) | copy-start | bytes 786436
  372.7 8.2 %copy-start.8 = (bf16[1,4,2,32,512]{4,3,2,1,0:T(8,128)(2,1)S(1)}, bf16[1,4,2,32,512]{4,3,2,1,0:T(8,128)(2,1)}, u32[]{:S(2)}) copy-start(bf16[1,4,2,32,512]{4,3,2,1,0:T(8,128)(2,1)} %copy.116) | copy-start | bytes 786436
  374.0 7.2 %copy-start.7 = (bf16[1,4,2,32,512]{4,3,2,1,0:T(8,128)(2,1)S(1)}, bf16[1,4,2,32,512]{4,3,2,1,0:T(8,128)(2,1)}, u32[]{:S(2)}) copy-start(bf16[1,4,2,32,512]{4,3,2,1,0:T(8,128)(2,1)} %copy.117) | copy-start | bytes 786436
  375.2 6.2 %copy-start.6 = (bf16[1,4,2,32,512]{4,3,2,1,0:T(8,128)(2,1)S(1)}, bf16[1,4,2,32,512]{4,3,2,1,0:T(8,128)(2,1)}, u32[]{:S(2)}) copy-start(bf16[1,4,2,32,512]{4,3,2,1,0:T(8,128)(2,1)} %copy.118) | copy-start | bytes 786436
  376.4 5.2 %copy-start.5 = (bf16[1,4,2,32,512]{4,3,2,1,0:T(8,128)(2,1)S(1)}, bf16[1,4,2,32,512]{4,3,2,1,0:T(8,128)(2,1)}, u32[]{:S(2)}) copy-start(bf16[1,4,2,32,512]{4,3,2,1,0:T(8,128)(2,1)} %copy.119) | copy-start | bytes 786436
  377.7 4.2 %copy-start.4 = (bf16[1,4,2,32,512]{4,3,2,1,0:T(8,128)(2,1)S(1)}, bf16[1,4,2,32,512]{4,3,2,1,0:T(8,128)(2,1)}, u32[]{:S(2)}) copy-start(bf16[1,4,2,32,512]{4,3,2,1,0:T(8,128)(2,1)} %copy.120) | copy-start | bytes 786436
  378.9 3.2 copy-start.3
  379.2 3.2 copy-start.2
  379.4 3.2 copy-start.1
  380.4 3.2 copy-start.15
  380.4 3.2 copy-start.16
  380.7 12.9 %copy-start.17 = (s32[64]{0:T(128)S(1)}, s32[64]{0:T(128)}, u32[]{:S(2)}) copy-start(s32[64]{0:T(128)} %param.25) | copy-start | bytes 772
  384.7 18.1 %all-to-all-start = ((bf16[1,4,2,32,256]{4,2,1,0,3:T(2,128)(2,1)}), bf16[1,4,2,32,256]{4,2,1,0,3:T(2,128)(2,1)S(1)}, u32[]{:S(2)}, u32[]{:S(2)}) async-start(bf16[1,4,2,32,256]{4,2,1,0,3:T(2,128)(2,1)} %copy.128), calls=%async_computation | async-start | bytes 262144 | tf_op jit(solution)/shard_map/all_to_all | solution.py:159
Sparse Core Ops, SparseCore 0:
  10.4 105.5 all-gather.5
where the time goes:
time: 413 us; the launch traced here: 411 us
  blocking collectives  239 us (58%)
  local copies, waits for them, and re-layouts  57.6 us (14%)
  loops' own time  38.9 us (9%)
  between operations  17.8 us (4%)
  starting transfers between devices  17.2 us (4%)
  matrix products  16.2 us (4%)
  waiting for transfers between devices  14 us (3%)
  other arithmetic  10.5 us (3%)
    psum x2, blocking collectives, clip_totals(): row_sums = lax.psum(frame_sums, 'space')  124 us
    all_gather x4, blocking collectives, entering(): pieces = jax.tree.map(lambda part: lax.all_gather(part, axis), value)  76.8 us
    another operation x4, loops' own time, entering(): return lax.fori_loop(0, count - 1, step, so_far)  38.9 us
    unnamed x1, blocking collectives  38.6 us
    dynamic_slice x60, local copies, waits for them, and re-layouts, step(): longer = join(so_far, jax.tree.map(lambda part: part[position], pieces))  36.1 us
    slice x29, local copies, waits for them, and re-layouts, local(): tap_planes[t_tap, :, h_tap:h_tap + rows_dev, w_tap:w_tap + width, :]  14.5 us
    dot_general x27, matrix products, local(): jnp.dot(tap_rows, piece[t_tap, h_tap, w_tap], preferred_element_type=jnp....  13.7 us
    all_to_all x1, waiting for transfers between devices, local(): lax.all_to_all(result, 'slab', split_axis=3, concat_axis=0, tiled=True)  9.14 us
  transfers between devices with their start and end apart: 5, of which 4 were waited for; matrix products, arithmetic and copies ran while one was open for 16% of the time, Pallas kernels for 0%

commit v1 on v0

v1 whole, which is shorter than its diff:
```python
import functools
import jax
import jax.numpy as jnp
from jax import lax
from jax.experimental import pallas as pl
from jax.experimental.pallas import tpu as pltpu
from jax.sharding import Mesh, PartitionSpec as P

C = 512
CO = 256
GROUPS = 32
GW = C // GROUPS
FR = 4
W = 32
SLABS = 16
T = FR * SLABS
HALF = C // 2
NY, NC, NZ, NX = 8, 2, 8, 4
AXES = ("y", "core", "z", "x")
HIGH = lax.Precision.HIGHEST
F32 = jnp.float32
BF16 = jnp.bfloat16
CELLS = 64 * GW
FRAME_CELLS = CELLS * NZ * NX
VMEM = pl.BlockSpec(memory_space=pltpu.VMEM)
SMEM = pl.BlockSpec(memory_space=pltpu.SMEM)
ANY = pl.BlockSpec(memory_space=pl.ANY)


def iota(shape, dim):
    return lax.broadcasted_iota(jnp.int32, shape, dim)


def group_of(shape, channel_dim, group_dim):
    return (iota(shape, channel_dim) // GW == iota(shape, group_dim)).astype(F32)


def fdot(a, b):
    return jnp.dot(a, b, precision=HIGH, preferred_element_type=F32)


def bdot(a, b):
    return jnp.dot(a, b, preferred_element_type=F32)


def local_sums(x_ref, out_ref):
    rows = [x_ref[f].reshape(2 * W, C).astype(F32) for f in range(FR)]
    totals = jnp.concatenate([jnp.sum(v, axis=0, keepdims=True) for v in rows], axis=0)
    mean = fdot(totals, group_of((C, 128), 0, 1)) * (1.0 / CELLS)
    spread = fdot(mean, group_of((128, C), 1, 0))
    squares = []
    for f in range(FR):
        d = rows[f] - spread[f : f + 1]
        squares.append(jnp.sum(d * d, axis=0, keepdims=True))
    squares = fdot(jnp.concatenate(squares, axis=0), group_of((C, 128), 0, 1))
    out_ref[...] = jnp.concatenate([mean, squares], axis=0)


def join_space(in_ref, out_ref):
    v = in_ref[...]
    n = NZ * NX
    mean = jnp.sum(v[:, :FR], axis=0) * (1.0 / n)
    d = v[:, :FR] - mean[None]
    squares = jnp.sum(v[:, FR:], axis=0) + CELLS * jnp.sum(d * d, axis=0)
    out_ref[...] = jnp.concatenate([mean, squares], axis=0)


def pack(at_ref, own_ref, up_ref, down_ref, out_ref):
    z = at_ref[2]
    source = jnp.concatenate(
        [up_ref[...].reshape(FR * W, C), own_ref[...].reshape(FR * 2 * W, C), down_ref[...].reshape(FR * W, C)], axis=0
    )
    n = 4 * FR * W
    to, frm = iota((n, n), 0), iota((n, n), 1)
    col, row, frame = to // 16, (to // 4) % 4, to % 4
    want = jnp.where(
        row == 0,
        frame * W + col,
        jnp.where(row == 3, 3 * FR * W + frame * W + col, FR * W + (frame * 2 + row - 1) * W + col),
    )
    order = (want == frm).astype(F32).astype(BF16)
    roll = (iota((C, C), 0) == lax.rem(64 * z + 32 + iota((C, C), 1), C)).astype(F32).astype(BF16)
    sorted_rows = bdot(order, source).astype(BF16)
    rolled = bdot(sorted_rows, roll).astype(BF16)
    for y in range(NY):
        for core in range(NC):
            lanes = slice(HALF, C) if core == 0 else slice(0, HALF)
            lo, hi = max(4 * y - 1, 0), min(4 * y + 5, W)
            first = lo - (4 * y - 1)
            out_ref[2 * y + core, 16 * first : 16 * (first + hi - lo), :] = rolled[16 * lo : 16 * hi, lanes]
            if y == 0:
                out_ref[2 * y + core, 0:16, :] = jnp.zeros((16, HALF), BF16)
            if y == NY - 1:
                out_ref[2 * y + core, 80:96, :] = jnp.zeros((16, HALF), BF16)


def starts(lengths_ref, frame):
    end = lengths_ref[0]
    start = jnp.zeros_like(frame)
    for k in range(1, lengths_ref.shape[0]):
        start = jnp.where(frame >= end, end, start)
        end = end + lengths_ref[k]
    return start


def convolve(
    at_ref, lengths_ref, sums_ref, gamma_ref, beta_ref, smooth_ref, x_ref, own, r1, r2, r3, r4,
    keep_ref, send_ref, w_ref, act_ref, acc_ref, sem,
):
    y, core, z, s = at_ref[0], at_ref[1], at_ref[2], at_ref[3]
    copies = []

    def bring(source, count, first, row):
        for i in range(count):
            at = pl.multiple_of(row + 16 * i, 16)
            copy = pltpu.make_async_copy(
                source.at[first + i], w_ref.at[:, pl.ds(at, 16), :], sem.at[len(copies)]
            )
            copy.start()
            copies.append(copy)

    bring(own, 2, 2 * core, jnp.where(core == 0, 224, 0))
    bring(r1, 4, 0, jnp.where(core == 0, 160, 32))
    bring(r2, 4, 0, 96)
    bring(r3, 4, 0, jnp.where(core == 0, 32, 160))
    bring(r4, 2, 0, jnp.where(core == 0, 0, 224))

    n = 2 * T
    sums = sums_ref[...].reshape(n, 128)
    frame_a = (iota((n, n), 0) // 8) * FR + iota((n, n), 0) % FR
    frame_b = (iota((n, n), 1) // 8) * FR + iota((n, n), 1) % FR
    squares_b = (iota((n, n), 1) // 4) % 2
    same = starts(lengths_ref, frame_a) == starts(lengths_ref, frame_b)
    on_means = (same & (squares_b == 0)).astype(F32)
    on_squares = (same & (squares_b == 1)).astype(F32)
    count = jnp.sum(on_means, axis=1, keepdims=True)
    mean = fdot(on_means, sums) / count
    off = sums - mean
    variance = (fdot(on_squares, sums) + FRAME_CELLS * fdot(on_means, off * off)) / (count * FRAME_CELLS)
    inverse = lax.rsqrt(variance + 1e-6)
    pick = (
        (iota((T, n), 1) // 8 * FR + iota((T, n), 1) % FR == iota((T, n), 0)) & ((iota((T, n), 1) // 4) % 2 == 0)
    ).astype(F32)
    base = 64 * z + jnp.where(core == 0, 32 + HALF, 32)
    mine = (iota((C, HALF), 0) == lax.rem(base + iota((C, HALF), 1), C)).astype(F32)
    to_group = (iota((128, HALF), 0) == lax.rem(base + iota((128, HALF), 1), C) // GW).astype(F32)
    gamma, beta, smooth = fdot(gamma_ref[...], mine), fdot(beta_ref[...], mine), fdot(smooth_ref[...], mine)
    mean = fdot(fdot(pick, mean), to_group)
    scale = fdot(fdot(pick, inverse), to_group) * gamma
    unsmooth = 1.0 / smooth

    m = 16 * 16
    to, frm = iota((m, m), 0), iota((m, m), 1)
    row, t = to // T, to % T
    by_row = (frm == (t // FR) * 16 + row * FR + t % FR).astype(F32).astype(BF16)
    frame, other = iota((T, T), 0), iota((T, T), 1)
    start = starts(lengths_ref, frame)
    before = jnp.maximum(frame - 1, start)
    before2 = jnp.maximum(frame - 2, start)
    earlier = jnp.concatenate([(other == before2).astype(F32), (other == before).astype(F32)], axis=0).astype(BF16)
    for c in range(6):
        rows = x_ref[:, 16 * c : 16 * (c + 1), :].reshape(m, HALF)
        values = bdot(by_row, rows)
        for r in range(4):
            v = (values[T * r : T * (r + 1)] - mean) * scale + beta
            v = v / (1.0 + jnp.exp(-v)) * unsmooth
            inside = None
            if r == 0:
                inside = s > 0
            if r == 3:
                inside = s < NZ * NX - 1
            if c == 0:
                inside = (y > 0) if inside is None else inside & (y > 0)
            if c == 5:
                inside = (y < NY - 1) if inside is None else inside & (y < NY - 1)
            if inside is not None:
                v = v * inside.astype(F32)
            v = v.astype(BF16)
            act_ref[2, r, c] = v
            e = bdot(earlier, v).astype(BF16)
            act_ref[0, r, c] = e[:T]
            act_ref[1, r, c] = e[T:]

    for copy in copies:
        copy.wait()
    total = None
    for j in range(3):
        for a in range(3):
            for b in range(3):
                lhs = act_ref[j, a : a + 2, b : b + 4].reshape(8 * T, HALF)
                term = bdot(lhs, w_ref[9 * j + 3 * a + b])
                total = term if total is None else total + term
    acc_ref[...] = total.reshape(2, 4, T, CO)
    keep_ref[...] = acc_ref[:, pl.ds(2 * core, 2)]
    send_ref[...] = acc_ref[:, pl.ds(2 - 2 * core, 2)]


def finish(order_ref, scale_ref, bias_ref, a_ref, b_ref, out_ref):
    picked = (iota((T, T), 0) == order_ref[...]).astype(F32).astype(BF16)
    for r in range(2):
        for c in range(2):
            v = ((a_ref[r, c] + b_ref[r, c]) * scale_ref[...] + bias_ref[...]).astype(BF16)
            v = lax.dot_general(picked, v, (((0,), (0,)), ((), ())), preferred_element_type=F32)
            at = (2 * r + c) * CO
            out_ref[:, at : at + CO] = v.astype(BF16)


def shift(value, step):
    pairs = []
    for i in range(NY * NC * NZ * NX):
        y, core, z, x = i // 64, i // 32 % 2, i // 4 % 8, i % 4
        to = step(y, core, z, x)
        if to is not None:
            ty, tc, tz, tx = to
            pairs.append((i, ((ty * NC + tc) * NZ + tz % NZ) * NX + tx))
    return lax.ppermute(value, AXES, pairs)


def by_space(y, core, s):
    return (y, core, s // NX, s % NX) if 0 <= s < NZ * NX else None


def struct(shape, dtype):
    return jax.ShapeDtypeStruct(shape, dtype)


def params(mib=48):
    return pltpu.CompilerParams(vmem_limit_bytes=mib * 2**20)


def cost(flops, size):
    return pl.CostEstimate(flops=flops, bytes_accessed=size, transcendentals=0)


def local(latent, gamma, beta, smooth, weights, w_scale, bias, lengths, order):
    y, core, z, x = (lax.axis_index(a) for a in AXES)
    at = jnp.stack([y, core, z, z * NX + x]).astype(jnp.int32)
    latent = latent[0]
    weights = weights.reshape(27, GW, CO)

    own = lax.all_to_all(jnp.broadcast_to(weights[None], (NX, 27, GW, CO)), "x", 0, 0, tiled=True)

    sums = pl.pallas_call(
        local_sums, out_shape=struct((8, 128), F32), in_specs=[VMEM], out_specs=VMEM, compiler_params=params(),
        cost_estimate=cost(2**20, 2**18),
    )(latent)
    up = shift(latent[:, 1], lambda y, core, z, x: by_space(y, core, z * NX + x + 1))
    down = shift(latent[:, 0], lambda y, core, z, x: by_space(y, core, z * NX + x - 1))
    gathered = lax.all_to_all(jnp.broadcast_to(sums[None], (NZ * NX, 8, 128)), ("z", "x"), 0, 0, tiled=True)

    def ring(v):
        return shift(v, lambda y, core, z, x: (y, core, z + 1 - 2 * core, x))

    r1 = ring(own)
    windows = pl.pallas_call(
        pack, out_shape=struct((SLABS, 96, HALF), BF16), in_specs=[SMEM, VMEM, VMEM, VMEM], out_specs=VMEM,
        compiler_params=params(), cost_estimate=cost(2**29, 2**21),
    )(at, latent, up, down)
    columns = lax.all_to_all(windows, ("y", "core"), 0, 0, tiled=True)
    sums = pl.pallas_call(
        join_space, out_shape=struct((8, 128), F32), in_specs=[VMEM], out_specs=VMEM, compiler_params=params(),
        cost_estimate=cost(2**18, 2**17),
    )(gathered)
    sums = lax.all_to_all(jnp.broadcast_to(sums[None], (SLABS, 8, 128)), ("y", "core"), 0, 0, tiled=True)
    r2 = ring(r1)
    r3 = ring(r2)
    r4 = ring(jnp.where(core == 0, r3[2:], r3[:2]))

    part = struct((2, 2, T, CO), F32)
    keep, send = pl.pallas_call(
        convolve, out_shape=(part, part), in_specs=[SMEM, SMEM] + [VMEM] * 5 + [ANY] * 5, out_specs=(VMEM, VMEM),
        scratch_shapes=[
            pltpu.VMEM((27, HALF, CO), BF16),
            pltpu.VMEM((3, 4, 6, T, HALF), BF16),
            pltpu.VMEM((2, 4, T, CO), F32),
            pltpu.SemaphoreType.DMA((16,)),
        ],
        compiler_params=params(), cost_estimate=cost(2**31, 2**22),
    )(at, lengths, sums, gamma[None], beta[None], smooth[None], columns, own, r1, r2, r3, r4)
    other = shift(send, lambda y, core, z, x: (y, 1 - core, z, x))
    out = pl.pallas_call(
        finish, out_shape=struct((T, 4 * CO), BF16), in_specs=[VMEM] * 5, out_specs=VMEM, compiler_params=params(),
        cost_estimate=cost(2**22, 2**20),
    )(order[None], w_scale[None], bias[None], keep, other)
    return out.reshape(SLABS, FR, 2, 2, CO)


def solution(mesh):
    inner = Mesh(mesh.devices.reshape(NY, NC, NZ, NX), AXES)
    slab, space = ("y", "core"), ("z", "x")
    in_specs = (
        P(slab, None, space, None, None), P(), P(), P(), P(None, None, None, space, None), P(), P(), P(), P(),
    )
    out_specs = P(None, None, space, slab, None)
    return jax.shard_map(local, mesh=inner, in_specs=in_specs, out_specs=out_specs, check_vma=False)
```

time: 413 us -> 119 us (0.29)
  blocking collectives: 239 us -> 13.6 us
  local copies, waits for them, and re-layouts: 57.6 us -> 6.5 us
  loops' own time: 38.9 us -> 0 us
  starting transfers between devices: 17.2 us -> 50.3 us
  waiting for transfers between devices: 14 us -> 37.9 us
  between operations: 17.8 us -> 0.17 us
  matrix products: 16.2 us -> 0 us
  other arithmetic: 10.5 us -> 0.91 us
  Pallas kernels: 0 us -> 8.61 us
    psum x2 -> x0, blocking collectives: 124 us -> none  [clip_totals(): row_sums = lax.psum(frame_sums, 'space')]
    all_gather x4 -> x0, blocking collectives: 76.8 us -> none  [entering(): pieces = jax.tree.map(lambda part: lax.all_gather(part, axis), value)]
    another operation x4 -> x0, loops' own time: 38.9 us -> none  [entering(): return lax.fori_loop(0, count - 1, step, so_far)]
    unnamed x1 -> x0, blocking collectives: 38.6 us -> none
    dynamic_slice x60 -> x0, local copies, waits for them, and re-layouts: 36.1 us -> none  [step(): longer = join(so_far, jax.tree.map(lambda part: part[position], pieces))]
    ppermute x3 -> x7, starting transfers between devices: 8.31 us -> 32.2 us  [shift(): return lax.ppermute(value, AXES, pairs)]
    dot_general x31 -> x0, matrix products: 16.2 us -> none  [the longest x27 13.7 us: local(): jnp.dot(tap_rows, piece[t_tap, h_tap, w_tap], preferred_element_type=jnp....]
    slice x32 -> x0, local copies, waits for them, and re-layouts: 15.9 us -> none  [the longest x29 14.5 us: local(): tap_planes[t_tap, :, h_tap:h_tap + rows_dev, w_tap:w_tap + width, :]]
  transfers between devices with their start and end apart: 5 -> 10, of which waited for: 4 -> 6; matrix products, arithmetic and copies ran while one was open for 16% -> 2% of each run, Pallas kernels for 0% -> 2%
where the time goes in v1:
time: 119 us; the launch traced here: 118 us
  starting transfers between devices  50.3 us (42%)
  waiting for transfers between devices  37.9 us (32%)
  blocking collectives  13.6 us (11%)
  Pallas kernels  8.61 us (7%)
  local copies, waits for them, and re-layouts  6.5 us (5%)
    ppermute x7, starting transfers between devices, shift(): return lax.ppermute(value, AXES, pairs)  32.2 us
    all_to_all x1, waiting for transfers between devices, local(): columns = lax.all_to_all(windows, ('y', 'core'), 0, 0, tiled=True)  16.8 us
    all_to_all x1, blocking collectives, local(): lax.all_to_all(jnp.broadcast_to(weights[None], (NX, 27, GW, CO)), 'x', 0,...  13.6 us
    ppermute x7, waiting for transfers between devices, shift(): return lax.ppermute(value, AXES, pairs)  13.1 us
    all_to_all x1, starting transfers between devices, local(): lax.all_to_all(jnp.broadcast_to(sums[None], (SLABS, 8, 128)), ('y', 'core...  9.38 us
    pallas_call x1, Pallas kernels, local(): pl.pallas_call(convolve, out_shape=(part, part), in_specs=[SMEM, SMEM] +...  6.26 us
    all_to_all x1, starting transfers between devices, local(): columns = lax.all_to_all(windows, ('y', 'core'), 0, 0, tiled=True)  4.84 us
    all_to_all x1, waiting for transfers between devices, local(): lax.all_to_all(jnp.broadcast_to(sums[None], (NZ * NX, 8, 128)), ('z', 'x'...  4.81 us
  transfers between devices with their start and end apart: 10, of which 6 were waited for; matrix products, arithmetic and copies ran while one was open for 2% of the time, Pallas kernels for 2%

profile of v1, /device:TPU:1, one launch (start us, length us, event | category | flops | bytes accessed | tf_op | source)
XLA Modules:
  0.0 118.0 jit_solution(9632934291275414368)
XLA Ops:
  0.0 1.0 broadcast_in_dim.46
  1.0 13.6 %all_to_all.20.own = bf16[4,27,16,256]{3,2,1,0:T(8,128)(2,1)S(1)} all-to-all(bf16[4,27,16,256]{3,2,1,0:T(8,128)(2,1)S(1)} %broadcast_in_dim.46), channel_id=1, replica_groups=mesh['y'=8,'core'=2,'z'=8,'x'=4] {'x'}, dimensions={0} | all-to-all | bytes 1769472 | tf_op jit(solution)/shard_map/all_to_all | solution.py:241
  14.6 14.2 %collective-permute-start.2 = (bf16[4,27,16,256]{3,2,1,0:T(8,128)(2,1)S(1)}, bf16[4,27,16,256]{3,2,1,0:T(8,128)(2,1)S(1)}, u32[]{:S(2)}, u32[]{:S(2)}) collective-permute-start(bf16[4,27,16,256]{3,2,1,0:T(8,128)(2,1)S(1)} %all_to_all.20.own), channel_id=1, source_target_pairs={{0,4},{1,5},{2,6},{3,7},{4,8},{5,9},{6,10},{7,11},{8,12},{9,13},{1... | collective-permute-start | bytes 2654216 | tf_op jit(solution)/shard_map/ppermute | solution.py:216
  28.9 10.0 %collective-permute-done.2.r1 = bf16[4,27,16,256]{3,2,1,0:T(8,128)(2,1)S(1)} collective-permute-done((bf16[4,27,16,256]{3,2,1,0:T(8,128)(2,1)S(1)}, bf16[4,27,16,256]{3,2,1,0:T(8,128)(2,1)S(1)}, u32[]{:S(2)}, u32[]{:S(2)}) %collective-permute-start.2) | collective-permute-done | bytes 884768 | tf_op jit(solution)/shard_map/ppermute | solution.py:216
  38.8 5.0 %collective-permute-start.3 = (bf16[4,27,16,256]{3,2,1,0:T(8,128)(2,1)S(1)}, bf16[4,27,16,256]{3,2,1,0:T(8,128)(2,1)}, u32[]{:S(2)}, u32[]{:S(2)}) collective-permute-start(bf16[4,27,16,256]{3,2,1,0:T(8,128)(2,1)S(1)} %collective-permute-done.2.r1), channel_id=1, source_target_pairs={{0,4},{1,5},{2,6},{3,7},{4,8},{5,9},{6,10},{7,11},{8,12},{9,13},{1... | collective-permute-start | bytes 2654216 | tf_op jit(solution)/shard_map/ppermute | solution.py:216
  43.9 0.8 shard_map.91
  44.7 0.7 broadcast_in_dim.40
  45.4 3.9 %all-to-all-start = ((f32[32,8,128]{2,1,0:T(8,128)}), f32[32,8,128]{2,1,0:T(8,128)S(1)}, u32[]{:S(2)}, u32[]{:S(2)}) async-start(f32[32,8,128]{2,1,0:T(8,128)} %broadcast_in_dim.40), calls=%async_computation | async-start | bytes 262144 | tf_op jit(solution)/shard_map/all_to_all | solution.py:249
  49.3 1.3 %collective-permute-start.1 = (bf16[4,32,512]{2,1,0:T(8,128)(2,1)S(1)}, bf16[4,32,512]{2,1,0:T(8,128)(2,1)S(1)}, u32[]{:S(2)}, u32[]{:S(2)}) collective-permute-start(bf16[4,32,512]{2,1,0:T(8,128)(2,1)S(1)} %get-tuple-element.9), channel_id=1, source_target_pairs={{1,0},{2,1},{3,2},{4,3},{5,4},{6,5},{7,6},{8,7},{9,8},{10,9},{11,1... | collective-permute-start | bytes 393224 | tf_op jit(solution)/shard_map/ppermute | solution.py:216
  50.6 4.0 %collective-permute-start = (bf16[4,32,512]{2,1,0:T(8,128)(2,1)S(1)}, bf16[4,32,512]{2,1,0:T(8,128)(2,1)S(1)}, u32[]{:S(2)}, u32[]{:S(2)}) collective-permute-start(bf16[4,32,512]{2,1,0:T(8,128)(2,1)S(1)} %get-tuple-element.10), channel_id=1, source_target_pairs={{0,1},{1,2},{2,3},{3,4},{4,5},{5,6},{6,7},{7,8},{8,9},{9,10},{10,1... | collective-permute-start | bytes 393224 | tf_op jit(solution)/shard_map/ppermute | solution.py:216
  54.6 4.8 %all-to-all-done.in_ref = f32[32,8,128]{2,1,0:T(8,128)S(1)} async-done(((f32[32,8,128]{2,1,0:T(8,128)}), f32[32,8,128]{2,1,0:T(8,128)S(1)}, u32[]{:S(2)}, u32[]{:S(2)}) %all-to-all-start) | async-done | bytes 131104 | tf_op jit(solution)/shard_map/all_to_all | solution.py:249
  59.4 0.1 shard_map.92
  59.5 0.6 broadcast_in_dim.41
  60.1 9.4 %all-to-all-start.1 = ((f32[16,8,128]{2,1,0:T(8,128)}), f32[16,8,128]{2,1,0:T(8,128)S(1)}, u32[]{:S(2)}, u32[]{:S(2)}) async-start(f32[16,8,128]{2,1,0:T(8,128)} %broadcast_in_dim.41), calls=%async_computation.1 | async-start | bytes 131072 | tf_op jit(solution)/shard_map/all_to_all | solution.py:264
  69.5 2.4 %collective-permute-start.4 = (bf16[4,27,16,256]{3,2,1,0:T(8,128)(2,1)}, bf16[4,27,16,256]{3,2,1,0:T(8,128)(2,1)S(1)}, u32[]{:S(2)}, u32[]{:S(2)}) collective-permute-start(bf16[4,27,16,256]{3,2,1,0:T(8,128)(2,1)} %collective-permute-done.3.r2), channel_id=1, source_target_pairs={{0,4},{1,5},{2,6},{3,7},{4,8},{5,9},{6,10},{7,11},{8,12},{9,13},{1... | collective-permute-start | bytes 2654216 | tf_op jit(solution)/shard_map/ppermute | solution.py:216
  71.9 0.1 pad_add_fusion.at_ref
  72.0 1.3 %shard_map.93 = bf16[16,96,256]{2,1,0:T(8,128)(2,1)S(1)} custom-call(s32[4]{0:T(128)S(1)} %pad_add_fusion.at_ref, bf16[4,2,32,512]{3,2,1,0:T(8,128)(2,1)S(1)} %bitcast.20, bf16[4,32,512]{2,1,0:T(8,128)(2,1)S(1)} %collective-permute-done.up_ref, bf16[4,32,512]{2,1,0:T(8,128)(2,1)S(1)} %collective-permute-done.1.down_ref), custom_call_target="tpu_custom_call" | custom-call | flops 536870912 | bytes 2097152 | tf_op jit(solution)/shard_map/pallas_call | solution.py:255
  73.3 0.9 copy-done.1
  74.2 3.1 %all-to-all-done.1.sums_ref = f32[16,8,128]{2,1,0:T(8,128)S(1)} async-done(((f32[16,8,128]{2,1,0:T(8,128)}), f32[16,8,128]{2,1,0:T(8,128)S(1)}, u32[]{:S(2)}, u32[]{:S(2)}) %all-to-all-start.1) | async-done | bytes 65568 | tf_op jit(solution)/shard_map/all_to_all | solution.py:264
  77.3 4.8 %all-to-all-start.2 = ((bf16[16,96,256]{2,1,0:T(8,128)(2,1)}), bf16[16,96,256]{2,1,0:T(8,128)(2,1)S(1)}, u32[]{:S(2)}, u32[]{:S(2)}) async-start(bf16[16,96,256]{2,1,0:T(8,128)(2,1)} %copy-done.1), calls=%async_computation.2 | async-start | bytes 1572864 | tf_op jit(solution)/shard_map/all_to_all | solution.py:259
  82.1 1.6 %collective-permute-done.4.r3 = bf16[4,27,16,256]{3,2,1,0:T(8,128)(2,1)S(1)} collective-permute-done((bf16[4,27,16,256]{3,2,1,0:T(8,128)(2,1)}, bf16[4,27,16,256]{3,2,1,0:T(8,128)(2,1)S(1)}, u32[]{:S(2)}, u32[]{:S(2)}) %collective-permute-start.4) | collective-permute-done | bytes 884768 | tf_op jit(solution)/shard_map/ppermute | solution.py:216
  83.8 0.8 slice_select_fusion
  84.6 3.3 %collective-permute-start.5 = (bf16[2,27,16,256]{3,2,1,0:T(8,128)(2,1)}, bf16[2,27,16,256]{3,2,1,0:T(8,128)(2,1)S(1)}, u32[]{:S(2)}, u32[]{:S(2)}) collective-permute-start(bf16[2,27,16,256]{3,2,1,0:T(8,128)(2,1)} %slice_select_fusion), channel_id=1, source_target_pairs={{0,4},{1,5},{2,6},{3,7},{4,8},{5,9},{6,10},{7,11},{8,12},{9,13},{1... | collective-permute-start | bytes 1327112 | tf_op jit(solution)/shard_map/ppermute | solution.py:216
  88.0 16.8 %all-to-all-done.2.x_ref = bf16[16,96,256]{2,1,0:T(8,128)(2,1)S(1)} async-done(((bf16[16,96,256]{2,1,0:T(8,128)(2,1)}), bf16[16,96,256]{2,1,0:T(8,128)(2,1)S(1)}, u32[]{:S(2)}, u32[]{:S(2)}) %all-to-all-start.2) | async-done | bytes 786464 | tf_op jit(solution)/shard_map/all_to_all | solution.py:259
  104.8 0.7 copy-done.7
  105.5 1.2 copy-done.6
  106.7 6.3 %shard_map.94 = (f32[2,2,64,256]{3,2,1,0:T(8,128)S(1)}, f32[2,2,64,256]{3,2,1,0:T(8,128)S(1)}) custom-call(s32[4]{0:T(128)S(1)} %pad_add_fusion.at_ref, s32[10]{0:T(128)S(1)} %copy-done.10, f32[16,8,128]{2,1,0:T(8,128)S(1)} %all-to-all-done.1.sums_ref, f32[1,512]{1,0:T(1,128)S(1)} %bitcast.24, f32[1,512]{1,0:T(1,128)S(1)} %bitcast.25, ...), custom_call_target="tpu_custom_call" | custom-call | flops 2147483648 | bytes 4194304 | tf_op jit(solution)/shard_map/pallas_call | solution.py:270
  112.9 1.9 %collective-permute-start.6 = (f32[2,2,64,256]{3,2,1,0:T(8,128)S(1)}, f32[2,2,64,256]{3,2,1,0:T(8,128)S(1)}, u32[]{:S(2)}, u32[]{:S(2)}) collective-permute-start(f32[2,2,64,256]{3,2,1,0:T(8,128)S(1)} %get-tuple-element.8), channel_id=1, source_target_pairs={{0,32},{1,33},{2,34},{3,35},{4,36},{5,37},{6,38},{7,39},{8,40},{9,... | collective-permute-start | bytes 786440 | tf_op jit(solution)/shard_map/ppermute | solution.py:216
  114.9 1.5 %collective-permute-done.6.b_ref = f32[2,2,64,256]{3,2,1,0:T(8,128)S(1)} collective-permute-done((f32[2,2,64,256]{3,2,1,0:T(8,128)S(1)}, f32[2,2,64,256]{3,2,1,0:T(8,128)S(1)}, u32[]{:S(2)}, u32[]{:S(2)}) %collective-permute-start.6) | collective-permute-done | bytes 262176 | tf_op jit(solution)/shard_map/ppermute | solution.py:216
  116.4 0.7 copy-done.2
  117.0 0.2 shard_map.95
  117.3 0.7 reshape.6
  (24 shorter events, 0.1 us)
Async XLA Ops:
  1.0 42.9 %copy-start = (bf16[1,4,2,32,512]{4,3,2,1,0:T(8,128)(2,1)S(1)}, bf16[1,4,2,32,512]{4,3,2,1,0:T(8,128)(2,1)}, u32[]{:S(2)}) copy-start(bf16[1,4,2,32,512]{4,3,2,1,0:T(8,128)(2,1)} %param.9) | copy-start | bytes 786436
  14.6 24.2 %collective-permute-start.2 = (bf16[4,27,16,256]{3,2,1,0:T(8,128)(2,1)S(1)}, bf16[4,27,16,256]{3,2,1,0:T(8,128)(2,1)S(1)}, u32[]{:S(2)}, u32[]{:S(2)}) collective-permute-start(bf16[4,27,16,256]{3,2,1,0:T(8,128)(2,1)S(1)} %all_to_all.20.own), channel_id=1, source_target_pairs={{0,4},{1,5},{2,6},{3,7},{4,8},{5,9},{6,10},{7,11},{8,12},{9,13},{1... | collective-permute-start | bytes 2654216 | tf_op jit(solution)/shard_map/ppermute | solution.py:216
  38.8 20.6 %copy-start.5 = (bf16[4,27,16,256]{3,2,1,0:T(8,128)(2,1)}, bf16[4,27,16,256]{3,2,1,0:T(8,128)(2,1)S(1)}, u32[]{:S(2)}) copy-start(bf16[4,27,16,256]{3,2,1,0:T(8,128)(2,1)S(1)} %collective-permute-done.2.r1) | copy-start | bytes 2654212
  38.8 30.6 %collective-permute-start.3 = (bf16[4,27,16,256]{3,2,1,0:T(8,128)(2,1)S(1)}, bf16[4,27,16,256]{3,2,1,0:T(8,128)(2,1)}, u32[]{:S(2)}, u32[]{:S(2)}) collective-permute-start(bf16[4,27,16,256]{3,2,1,0:T(8,128)(2,1)S(1)} %collective-permute-done.2.r1), channel_id=1, source_target_pairs={{0,4},{1,5},{2,6},{3,7},{4,8},{5,9},{6,10},{7,11},{8,12},{9,13},{1... | collective-permute-start | bytes 2654216 | tf_op jit(solution)/shard_map/ppermute | solution.py:216
  45.4 14.0 %all-to-all-start = ((f32[32,8,128]{2,1,0:T(8,128)}), f32[32,8,128]{2,1,0:T(8,128)S(1)}, u32[]{:S(2)}, u32[]{:S(2)}) async-start(f32[32,8,128]{2,1,0:T(8,128)} %broadcast_in_dim.40), calls=%async_computation | async-start | bytes 262144 | tf_op jit(solution)/shard_map/all_to_all | solution.py:249
  49.3 22.7 %collective-permute-start.1 = (bf16[4,32,512]{2,1,0:T(8,128)(2,1)S(1)}, bf16[4,32,512]{2,1,0:T(8,128)(2,1)S(1)}, u32[]{:S(2)}, u32[]{:S(2)}) collective-permute-start(bf16[4,32,512]{2,1,0:T(8,128)(2,1)S(1)} %get-tuple-element.9), channel_id=1, source_target_pairs={{1,0},{2,1},{3,2},{4,3},{5,4},{6,5},{7,6},{8,7},{9,8},{10,9},{11,1... | collective-permute-start | bytes 393224 | tf_op jit(solution)/shard_map/ppermute | solution.py:216
  50.6 21.4 %collective-permute-start = (bf16[4,32,512]{2,1,0:T(8,128)(2,1)S(1)}, bf16[4,32,512]{2,1,0:T(8,128)(2,1)S(1)}, u32[]{:S(2)}, u32[]{:S(2)}) collective-permute-start(bf16[4,32,512]{2,1,0:T(8,128)(2,1)S(1)} %get-tuple-element.10), channel_id=1, source_target_pairs={{0,1},{1,2},{2,3},{3,4},{4,5},{5,6},{6,7},{7,8},{8,9},{9,10},{10,1... | collective-permute-start | bytes 393224 | tf_op jit(solution)/shard_map/ppermute | solution.py:216
  60.1 17.2 %all-to-all-start.1 = ((f32[16,8,128]{2,1,0:T(8,128)}), f32[16,8,128]{2,1,0:T(8,128)S(1)}, u32[]{:S(2)}, u32[]{:S(2)}) async-start(f32[16,8,128]{2,1,0:T(8,128)} %broadcast_in_dim.41), calls=%async_computation.1 | async-start | bytes 131072 | tf_op jit(solution)/shard_map/all_to_all | solution.py:264
  69.5 14.3 %collective-permute-start.4 = (bf16[4,27,16,256]{3,2,1,0:T(8,128)(2,1)}, bf16[4,27,16,256]{3,2,1,0:T(8,128)(2,1)S(1)}, u32[]{:S(2)}, u32[]{:S(2)}) collective-permute-start(bf16[4,27,16,256]{3,2,1,0:T(8,128)(2,1)} %collective-permute-done.3.r2), channel_id=1, source_target_pairs={{0,4},{1,5},{2,6},{3,7},{4,8},{5,9},{6,10},{7,11},{8,12},{9,13},{1... | collective-permute-start | bytes 2654216 | tf_op jit(solution)/shard_map/ppermute | solution.py:216
  73.3 0.9 copy-start.1
  77.3 27.5 %all-to-all-start.2 = ((bf16[16,96,256]{2,1,0:T(8,128)(2,1)}), bf16[16,96,256]{2,1,0:T(8,128)(2,1)S(1)}, u32[]{:S(2)}, u32[]{:S(2)}) async-start(bf16[16,96,256]{2,1,0:T(8,128)(2,1)} %copy-done.1), calls=%async_computation.2 | async-start | bytes 1572864 | tf_op jit(solution)/shard_map/all_to_all | solution.py:259
  83.8 21.0 %copy-start.8 = (f32[512]{0:T(512)S(1)}, f32[512]{0:T(512)}, u32[]{:S(2)}) copy-start(f32[512]{0:T(512)} %param.11) | copy-start | bytes 6148
  83.8 21.0 %copy-start.9 = (f32[512]{0:T(512)S(1)}, f32[512]{0:T(512)}, u32[]{:S(2)}) copy-start(f32[512]{0:T(512)} %param.12) | copy-start | bytes 6148
  84.6 20.2 %collective-permute-start.5 = (bf16[2,27,16,256]{3,2,1,0:T(8,128)(2,1)}, bf16[2,27,16,256]{3,2,1,0:T(8,128)(2,1)S(1)}, u32[]{:S(2)}, u32[]{:S(2)}) collective-permute-start(bf16[2,27,16,256]{3,2,1,0:T(8,128)(2,1)} %slice_select_fusion), channel_id=1, source_target_pairs={{0,4},{1,5},{2,6},{3,7},{4,8},{5,9},{6,10},{7,11},{8,12},{9,13},{1... | collective-permute-start | bytes 1327112 | tf_op jit(solution)/shard_map/ppermute | solution.py:216
  104.8 0.7 copy-start.7
  104.8 0.7 copy-start.10
  105.5 1.2 copy-start.6
  106.7 9.7 %copy-start.3 = (f32[256]{0:T(256)S(1)}, f32[256]{0:T(256)}, u32[]{:S(2)}) copy-start(f32[256]{0:T(256)} %param.15) | copy-start | bytes 3076
  112.9 3.4 %collective-permute-start.6 = (f32[2,2,64,256]{3,2,1,0:T(8,128)S(1)}, f32[2,2,64,256]{3,2,1,0:T(8,128)S(1)}, u32[]{:S(2)}, u32[]{:S(2)}) collective-permute-start(f32[2,2,64,256]{3,2,1,0:T(8,128)S(1)} %get-tuple-element.8), channel_id=1, source_target_pairs={{0,32},{1,33},{2,34},{3,35},{4,36},{5,37},{6,38},{7,39},{8,40},{9,... | collective-permute-start | bytes 786440 | tf_op jit(solution)/shard_map/ppermute | solution.py:216
  116.4 0.7 copy-start.2
  116.4 0.7 copy-start.4

commit v2 on v1

--- a/solution.py
+++ b/solution.py
@@ -43,8 +43,14 @@
     return jnp.dot(a, b, preferred_element_type=F32)
 
 
-def local_sums(x_ref, out_ref):
-    rows = [x_ref[f].reshape(2 * W, C).astype(F32) for f in range(FR)]
+def local_sums(x_hbm, sums_ref, x_ref, sem):
+    loads = [pltpu.make_async_copy(x_hbm.at[f], x_ref.at[f], sem.at[f]) for f in range(FR)]
+    for copy in loads:
+        copy.start()
+    rows = []
+    for f in range(FR):
+        loads[f].wait()
+        rows.append(x_ref[f].reshape(2 * W, C).astype(F32))
     totals = jnp.concatenate([jnp.sum(v, axis=0, keepdims=True) for v in rows], axis=0)
     mean = fdot(totals, group_of((C, 128), 0, 1)) * (1.0 / CELLS)
     spread = fdot(mean, group_of((128, C), 1, 0))
@@ -53,20 +59,32 @@
         d = rows[f] - spread[f : f + 1]
         squares.append(jnp.sum(d * d, axis=0, keepdims=True))
     squares = fdot(jnp.concatenate(squares, axis=0), group_of((C, 128), 0, 1))
-    out_ref[...] = jnp.concatenate([mean, squares], axis=0)
-
-
-def join_space(in_ref, out_ref):
-    v = in_ref[...]
+    sums_ref[...] = jnp.broadcast_to(jnp.concatenate([mean, squares], axis=0)[None], sums_ref.shape)
+
+
+def join_space(v):
     n = NZ * NX
     mean = jnp.sum(v[:, :FR], axis=0) * (1.0 / n)
     d = v[:, :FR] - mean[None]
     squares = jnp.sum(v[:, FR:], axis=0) + CELLS * jnp.sum(d * d, axis=0)
-    out_ref[...] = jnp.concatenate([mean, squares], axis=0)
-
-
-def pack(at_ref, own_ref, up_ref, down_ref, out_ref):
-    z = at_ref[2]
+    return jnp.concatenate([mean, squares], axis=0)
+
+
+def in_three(v):
+    high = v.astype(BF16)
+    rest = v - high.astype(F32)
+    middle = rest.astype(BF16)
+    return high, middle, (rest - middle.astype(F32)).astype(BF16)
+
+
+def channel_at(z, x, place):
+    u = place + 32
+    block, shard = lax.rem(z + u // (GW * NX), NZ), lax.rem(x + u // GW, NX)
+    return block * (GW * NX) + shard * GW + u % GW
+
+
+def pack(at_ref, own_ref, up_ref, down_ref, sums_ref, out_ref):
+    z, x = at_ref[2], at_ref[4]
     source = jnp.concatenate(
         [up_ref[...].reshape(FR * W, C), own_ref[...].reshape(FR * 2 * W, C), down_ref[...].reshape(FR * W, C)], axis=0
     )
@@ -79,15 +97,20 @@
         jnp.where(row == 3, 3 * FR * W + frame * W + col, FR * W + (frame * 2 + row - 1) * W + col),
     )
     order = (want == frm).astype(F32).astype(BF16)
-    roll = (iota((C, C), 0) == lax.rem(64 * z + 32 + iota((C, C), 1), C)).astype(F32).astype(BF16)
+    roll = (iota((C, C), 0) == channel_at(z, x, iota((C, C), 1))).astype(F32).astype(BF16)
     sorted_rows = bdot(order, source).astype(BF16)
     rolled = bdot(sorted_rows, roll).astype(BF16)
+    sums = jnp.concatenate([join_space(sums_ref[...]), jnp.zeros((8, 128), F32)], axis=0)
+    high, middle, low = in_three(sums)
+    thirds = jnp.concatenate([high[:, :GROUPS], middle[:, :GROUPS], low[:, :GROUPS]], axis=1)
+    thirds = jnp.concatenate([thirds, jnp.zeros((16, HALF - 3 * GROUPS), BF16)], axis=1)
     for y in range(NY):
         for core in range(NC):
             lanes = slice(HALF, C) if core == 0 else slice(0, HALF)
             lo, hi = max(4 * y - 1, 0), min(4 * y + 5, W)
             first = lo - (4 * y - 1)
             out_ref[2 * y + core, 16 * first : 16 * (first + hi - lo), :] = rolled[16 * lo : 16 * hi, lanes]
+            out_ref[2 * y + core, 96:112, :] = thirds
             if y == 0:
                 out_ref[2 * y + core, 0:16, :] = jnp.zeros((16, HALF), BF16)
             if y == NY - 1:
@@ -103,30 +126,12 @@
     return start
 
 
-def convolve(
-    at_ref, lengths_ref, sums_ref, gamma_ref, beta_ref, smooth_ref, x_ref, own, r1, r2, r3, r4,
-    keep_ref, send_ref, w_ref, act_ref, acc_ref, sem,
-):
-    y, core, z, s = at_ref[0], at_ref[1], at_ref[2], at_ref[3]
-    copies = []
-
-    def bring(source, count, first, row):
-        for i in range(count):
-            at = pl.multiple_of(row + 16 * i, 16)
-            copy = pltpu.make_async_copy(
-                source.at[first + i], w_ref.at[:, pl.ds(at, 16), :], sem.at[len(copies)]
-            )
-            copy.start()
-            copies.append(copy)
-
-    bring(own, 2, 2 * core, jnp.where(core == 0, 224, 0))
-    bring(r1, 4, 0, jnp.where(core == 0, 160, 32))
-    bring(r2, 4, 0, 96)
-    bring(r3, 4, 0, jnp.where(core == 0, 32, 160))
-    bring(r4, 2, 0, jnp.where(core == 0, 0, 224))
-
+def activate(at_ref, lengths_ref, gamma_ref, beta_ref, smooth_ref, x_ref, act_ref):
+    y, core, z, s, x = at_ref[0], at_ref[1], at_ref[2], at_ref[3], at_ref[4]
     n = 2 * T
-    sums = sums_ref[...].reshape(n, 128)
+    thirds = x_ref[:, 96:112, :].astype(F32)[:, :8, :128].reshape(n, 128)
+    add = ((iota((128, 128), 0) % GROUPS == iota((128, 128), 1)) & (iota((128, 128), 0) < 3 * GROUPS)).astype(F32)
+    sums = fdot(thirds, add)
     frame_a = (iota((n, n), 0) // 8) * FR + iota((n, n), 0) % FR
     frame_b = (iota((n, n), 1) // 8) * FR + iota((n, n), 1) % FR
     squares_b = (iota((n, n), 1) // 4) % 2
@@ -141,9 +146,9 @@
     pick = (
         (iota((T, n), 1) // 8 * FR + iota((T, n), 1) % FR == iota((T, n), 0)) & ((iota((T, n), 1) // 4) % 2 == 0)
     ).astype(F32)
-    base = 64 * z + jnp.where(core == 0, 32 + HALF, 32)
-    mine = (iota((C, HALF), 0) == lax.rem(base + iota((C, HALF), 1), C)).astype(F32)
-    to_group = (iota((128, HALF), 0) == lax.rem(base + iota((128, HALF), 1), C) // GW).astype(F32)
+    first = jnp.where(core == 0, HALF, 0)
+    mine = (iota((C, HALF), 0) == channel_at(z, x, first + iota((C, HALF), 1))).astype(F32)
+    to_group = (iota((128, HALF), 0) == channel_at(z, x, first + iota((128, HALF), 1)) // GW).astype(F32)
     gamma, beta, smooth = fdot(gamma_ref[...], mine), fdot(beta_ref[...], mine), fdot(smooth_ref[...], mine)
     mean = fdot(fdot(pick, mean), to_group)
     scale = fdot(fdot(pick, inverse), to_group) * gamma
@@ -181,15 +186,52 @@
             act_ref[0, r, c] = e[:T]
             act_ref[1, r, c] = e[T:]
 
+
+def convolve(at_ref, act_hbm, a0, b0, a1, b1, a2, b2, a3, b3, r4, keep_ref, send_ref, w_ref, act_ref, acc_ref, sem, act_sem):
+    core = at_ref[1]
+    copies = []
+
+    def bring(source, count, first, row):
+        for i in range(count):
+            at = pl.multiple_of(row + 16 * i, 16)
+            copy = pltpu.make_async_copy(source.at[first + i], w_ref.at[:, pl.ds(at, 16), :], sem.at[len(copies)])
+            copy.start()
+            copies.append(copy)
+
+    moves = [pltpu.make_async_copy(act_hbm.at[j], act_ref.at[j], act_sem.at[j]) for j in range(3)]
+    for move in moves:
+        move.start()
+    own_sems = [sem.at[0], sem.at[1]]
+
+    @pl.when(core == 0)
+    def _():
+        for i in range(2):
+            pltpu.make_async_copy(a0.at[i], w_ref.at[:, pl.ds(224 + 16 * i, 16), :], own_sems[i]).start()
+
+    @pl.when(core == 1)
+    def _():
+        for i in range(2):
+            pltpu.make_async_copy(b0.at[i], w_ref.at[:, pl.ds(16 * i, 16), :], own_sems[i]).start()
+
+    copies += [pltpu.make_async_copy(a0.at[i], w_ref.at[:, pl.ds(16 * i, 16), :], own_sems[i]) for i in range(2)]
+    bring(a1, 2, 0, jnp.where(core == 0, 160, 32))
+    bring(b1, 2, 0, jnp.where(core == 0, 192, 64))
+    bring(a2, 2, 0, 96)
+    bring(b2, 2, 0, 128)
+    bring(a3, 2, 0, jnp.where(core == 0, 32, 160))
+    bring(b3, 2, 0, jnp.where(core == 0, 64, 192))
+    bring(r4, 2, 0, jnp.where(core == 0, 0, 224))
+
     for copy in copies:
         copy.wait()
     total = None
-    for j in range(3):
-        for a in range(3):
-            for b in range(3):
-                lhs = act_ref[j, a : a + 2, b : b + 4].reshape(8 * T, HALF)
-                term = bdot(lhs, w_ref[9 * j + 3 * a + b])
-                total = term if total is None else total + term
+    for tap in range(27):
+        j, a, b = tap // 9, tap // 3 % 3, tap % 3
+        if tap % 9 == 0:
+            moves[j].wait()
+        lhs = act_ref[j, a : a + 2, b : b + 4].reshape(8 * T, HALF)
+        term = bdot(lhs, w_ref[tap])
+        total = term if total is None else total + term
     acc_ref[...] = total.reshape(2, 4, T, CO)
     keep_ref[...] = acc_ref[:, pl.ds(2 * core, 2)]
     send_ref[...] = acc_ref[:, pl.ds(2 - 2 * core, 2)]
@@ -234,49 +276,54 @@
 
 def local(latent, gamma, beta, smooth, weights, w_scale, bias, lengths, order):
     y, core, z, x = (lax.axis_index(a) for a in AXES)
-    at = jnp.stack([y, core, z, z * NX + x]).astype(jnp.int32)
+    at = jnp.stack([y, core, z, z * NX + x, x]).astype(jnp.int32)
     latent = latent[0]
     weights = weights.reshape(27, GW, CO)
 
-    own = lax.all_to_all(jnp.broadcast_to(weights[None], (NX, 27, GW, CO)), "x", 0, 0, tiled=True)
-
-    sums = pl.pallas_call(
-        local_sums, out_shape=struct((8, 128), F32), in_specs=[VMEM], out_specs=VMEM, compiler_params=params(),
-        cost_estimate=cost(2**20, 2**18),
+    spread = pl.pallas_call(
+        local_sums, out_shape=struct((NZ * NX, 8, 128), F32), in_specs=[ANY], out_specs=VMEM,
+        scratch_shapes=[pltpu.VMEM((FR, 2, W, C), BF16), pltpu.SemaphoreType.DMA((FR,))],
+        compiler_params=params(60), cost_estimate=cost(2**16, 2**16),
     )(latent)
+
+    def ring(v):
+        return shift(v, lambda y, core, z, x: (y, core, z + 1 - 2 * core, x))
+
+    def beside(d):
+        return shift(weights, lambda y, core, z, x: (y, core, z, (x - d) % NX))
+
+    x1, x2, x3 = beside(1), beside(2), beside(3)
     up = shift(latent[:, 1], lambda y, core, z, x: by_space(y, core, z * NX + x + 1))
     down = shift(latent[:, 0], lambda y, core, z, x: by_space(y, core, z * NX + x - 1))
-    gathered = lax.all_to_all(jnp.broadcast_to(sums[None], (NZ * NX, 8, 128)), ("z", "x"), 0, 0, tiled=True)
-
-    def ring(v):
-        return shift(v, lambda y, core, z, x: (y, core, z + 1 - 2 * core, x))
-
-    r1 = ring(own)
+    gathered = lax.all_to_all(spread, ("z", "x"), 0, 0, tiled=True)
+    a0, b0 = jnp.stack([weights, x1]), jnp.stack([x2, x3])
+    gathered, a0, b0, up, down = lax.optimization_barrier((gathered, a0, b0, up, down))
+    a1, b1 = ring(a0), ring(b0)
     windows = pl.pallas_call(
-        pack, out_shape=struct((SLABS, 96, HALF), BF16), in_specs=[SMEM, VMEM, VMEM, VMEM], out_specs=VMEM,
-        compiler_params=params(), cost_estimate=cost(2**29, 2**21),
-    )(at, latent, up, down)
+        pack, out_shape=struct((SLABS, 112, HALF), BF16), in_specs=[SMEM] + [VMEM] * 4, out_specs=VMEM,
+        compiler_params=params(), cost_estimate=cost(2**16, 2**16),
+    )(at, latent, up, down, gathered)
     columns = lax.all_to_all(windows, ("y", "core"), 0, 0, tiled=True)
-    sums = pl.pallas_call(
-        join_space, out_shape=struct((8, 128), F32), in_specs=[VMEM], out_specs=VMEM, compiler_params=params(),
-        cost_estimate=cost(2**18, 2**17),
-    )(gathered)
-    sums = lax.all_to_all(jnp.broadcast_to(sums[None], (SLABS, 8, 128)), ("y", "core"), 0, 0, tiled=True)
-    r2 = ring(r1)
-    r3 = ring(r2)
-    r4 = ring(jnp.where(core == 0, r3[2:], r3[:2]))
+    a2, b2 = ring(a1), ring(b1)
+    a3, b3 = ring(a2), ring(b2)
+    act = pl.pallas_call(
+        activate, out_shape=struct((3, 4, 6, T, HALF), BF16), in_specs=[SMEM, SMEM] + [VMEM] * 4, out_specs=VMEM,
+        compiler_params=params(), cost_estimate=cost(2**16, 2**16),
+    )(at, lengths, gamma[None], beta[None], smooth[None], columns)
+    r4 = ring(jnp.where(core == 0, b3, a3))
 
     part = struct((2, 2, T, CO), F32)
     keep, send = pl.pallas_call(
-        convolve, out_shape=(part, part), in_specs=[SMEM, SMEM] + [VMEM] * 5 + [ANY] * 5, out_specs=(VMEM, VMEM),
+        convolve, out_shape=(part, part), in_specs=[SMEM] + [ANY] * 10, out_specs=(VMEM, VMEM),
         scratch_shapes=[
             pltpu.VMEM((27, HALF, CO), BF16),
             pltpu.VMEM((3, 4, 6, T, HALF), BF16),
             pltpu.VMEM((2, 4, T, CO), F32),
             pltpu.SemaphoreType.DMA((16,)),
+            pltpu.SemaphoreType.DMA((3,)),
         ],
-        compiler_params=params(), cost_estimate=cost(2**31, 2**22),
-    )(at, lengths, sums, gamma[None], beta[None], smooth[None], columns, own, r1, r2, r3, r4)
+        compiler_params=params(60), cost_estimate=cost(2**16, 2**16),
+    )(at, act, a0, b0, a1, b1, a2, b2, a3, b3, r4)
     other = shift(send, lambda y, core, z, x: (y, 1 - core, z, x))
     out = pl.pallas_call(
         finish, out_shape=struct((T, 4 * CO), BF16), in_specs=[VMEM] * 5, out_specs=VMEM, compiler_params=params(),

time: 119 us -> 112 us (0.941)
  the two profiles are of different devices: /device:TPU:1 before, /device:TPU:15 now
where the time goes in v2:
time: 112 us; the launch traced here: 111 us
  starting transfers between devices  65 us (58%)
  waiting for transfers between devices  24.1 us (22%)
  Pallas kernels  16.5 us (15%)
  local copies, waits for them, and re-layouts  4.23 us (4%)
    ppermute x13, starting transfers between devices, shift(): return lax.ppermute(value, AXES, pairs)  41.2 us
    ppermute x13, waiting for transfers between devices, shift(): return lax.ppermute(value, AXES, pairs)  24.1 us
    all_to_all x1, starting transfers between devices, local(): gathered = lax.all_to_all(spread, ('z', 'x'), 0, 0, tiled=True)  12.9 us
    all_to_all x1, starting transfers between devices, local(): columns = lax.all_to_all(windows, ('y', 'core'), 0, 0, tiled=True)  11 us
    pallas_call x1, Pallas kernels, local(): pl.pallas_call(convolve, out_shape=(part, part), in_specs=[SMEM] + [ANY]...  7.8 us
    pallas_call x1, Pallas kernels, local(): pl.pallas_call(activate, out_shape=struct((3, 4, 6, T, HALF), BF16), in_s...  3.83 us
    unnamed x37, local copies, waits for them, and re-layouts  3.39 us
    pallas_call x1, Pallas kernels, local(): pl.pallas_call(local_sums, out_shape=struct((NZ * NX, 8, 128), F32), in_s...  2.42 us
  transfers between devices with their start and end apart: 15, of which 8 were waited for; matrix products, arithmetic and copies ran while one was open for 2% of the time, Pallas kernels for 8%

profile of v2, /device:TPU:15, one launch (start us, length us, event | category | flops | bytes accessed | tf_op | source)
XLA Modules:
  0.0 111.2 jit_solution(17868187740614332507)
XLA Ops:
  0.0 3.2 %collective-permute-start.1 = (bf16[27,16,256]{2,1,0:T(8,128)(2,1)}, bf16[27,16,256]{2,1,0:T(8,128)(2,1)S(1)}, u32[]{:S(2)}, u32[]{:S(2)}) collective-permute-start(bf16[27,16,256]{2,1,0:T(8,128)(2,1)} %bitcast.33), channel_id=1, source_target_pairs={{0,2},{1,3},{2,0},{3,1},{4,6},{5,7},{6,4},{7,5},{8,10},{9,11},{10,... | collective-permute-start | bytes 663560 | tf_op jit(solution)/shard_map/ppermute | solution.py:258
  3.2 3.7 %collective-permute-start.2 = (bf16[27,16,256]{2,1,0:T(8,128)(2,1)}, bf16[27,16,256]{2,1,0:T(8,128)(2,1)S(1)}, u32[]{:S(2)}, u32[]{:S(2)}) collective-permute-start(bf16[27,16,256]{2,1,0:T(8,128)(2,1)} %bitcast.34), channel_id=1, source_target_pairs={{0,1},{1,2},{2,3},{3,0},{4,5},{5,6},{6,7},{7,4},{8,9},{9,10},{10,1... | collective-permute-start | bytes 663560 | tf_op jit(solution)/shard_map/ppermute | solution.py:258
  6.9 1.9 %collective-permute-start = (bf16[27,16,256]{2,1,0:T(8,128)(2,1)}, bf16[27,16,256]{2,1,0:T(8,128)(2,1)S(1)}, u32[]{:S(2)}, u32[]{:S(2)}) collective-permute-start(bf16[27,16,256]{2,1,0:T(8,128)(2,1)} %bitcast.35), channel_id=1, source_target_pairs={{0,3},{1,0},{2,1},{3,2},{4,7},{5,4},{6,5},{7,6},{8,11},{9,8},{10,9... | collective-permute-start | bytes 663560 | tf_op jit(solution)/shard_map/ppermute | solution.py:258
  8.8 2.4 %shard_map.91 = f32[32,8,128]{2,1,0:T(8,128)} custom-call(bf16[4,2,32,512]{3,2,1,0:T(8,128)(2,1)} %bitcast.24), custom_call_target="tpu_custom_call" | custom-call | flops 65536 | bytes 65536 | tf_op jit(solution)/shard_map/pallas_call | solution.py:283
  11.3 12.9 %all-to-all-start = ((f32[32,8,128]{2,1,0:T(8,128)}), f32[32,8,128]{2,1,0:T(8,128)S(1)}, u32[]{:S(2)}, u32[]{:S(2)}) async-start(f32[32,8,128]{2,1,0:T(8,128)} %shard_map.91), calls=%async_computation | async-start | bytes 262144 | tf_op jit(solution)/shard_map/all_to_all | solution.py:298
  24.1 1.0 copy.15
  25.1 3.1 %collective-permute-start.3 = (bf16[4,32,512]{2,1,0:T(8,128)(2,1)S(1)}, bf16[4,32,512]{2,1,0:T(8,128)(2,1)S(1)}, u32[]{:S(2)}, u32[]{:S(2)}) collective-permute-start(bf16[4,32,512]{2,1,0:T(8,128)(2,1)S(1)} %get-tuple-element.20), channel_id=1, source_target_pairs={{0,1},{1,2},{2,3},{3,4},{4,5},{5,6},{6,7},{7,8},{8,9},{9,10},{10,1... | collective-permute-start | bytes 393224 | tf_op jit(solution)/shard_map/ppermute | solution.py:258
  28.2 2.2 %collective-permute-start.4 = (bf16[4,32,512]{2,1,0:T(8,128)(2,1)S(1)}, bf16[4,32,512]{2,1,0:T(8,128)(2,1)S(1)}, u32[]{:S(2)}, u32[]{:S(2)}) collective-permute-start(bf16[4,32,512]{2,1,0:T(8,128)(2,1)S(1)} %get-tuple-element.19), channel_id=1, source_target_pairs={{1,0},{2,1},{3,2},{4,3},{5,4},{6,5},{7,6},{8,7},{9,8},{10,9},{11,1... | collective-permute-start | bytes 393224 | tf_op jit(solution)/shard_map/ppermute | solution.py:258
  30.6 1.0 collective-permute-done.3.up_ref
  31.6 4.4 %collective-permute-done.4.down_ref = bf16[4,32,512]{2,1,0:T(8,128)(2,1)S(1)} collective-permute-done((bf16[4,32,512]{2,1,0:T(8,128)(2,1)S(1)}, bf16[4,32,512]{2,1,0:T(8,128)(2,1)S(1)}, u32[]{:S(2)}, u32[]{:S(2)}) %collective-permute-start.4) | collective-permute-done | bytes 131104 | tf_op jit(solution)/shard_map/ppermute | solution.py:258
  36.0 1.9 %collective-permute-start.6 = (bf16[2,27,16,256]{3,2,1,0:T(8,128)(2,1)S(1)}, bf16[2,27,16,256]{3,2,1,0:T(8,128)(2,1)S(1)}, u32[]{:S(2)}, u32[]{:S(2)}) collective-permute-start(bf16[2,27,16,256]{3,2,1,0:T(8,128)(2,1)S(1)} %pad_maximum_fusion.1.b0), channel_id=1, source_target_pairs={{0,4},{1,5},{2,6},{3,7},{4,8},{5,9},{6,10},{7,11},{8,12},{9,13},{1... | collective-permute-start | bytes 1327112 | tf_op jit(solution)/shard_map/ppermute | solution.py:258
  38.0 4.6 %collective-permute-start.5 = (bf16[2,27,16,256]{3,2,1,0:T(8,128)(2,1)S(1)}, bf16[2,27,16,256]{3,2,1,0:T(8,128)(2,1)S(1)}, u32[]{:S(2)}, u32[]{:S(2)}) collective-permute-start(bf16[2,27,16,256]{3,2,1,0:T(8,128)(2,1)S(1)} %pad_maximum_fusion.a0), channel_id=1, source_target_pairs={{0,4},{1,5},{2,6},{3,7},{4,8},{5,9},{6,10},{7,11},{8,12},{9,13},{1... | collective-permute-start | bytes 1327112 | tf_op jit(solution)/shard_map/ppermute | solution.py:258
  42.8 2.2 %shard_map.92 = bf16[16,112,256]{2,1,0:T(8,128)(2,1)} custom-call(s32[5]{0:T(128)S(1)} %stack.38.at_ref, bf16[4,2,32,512]{3,2,1,0:T(8,128)(2,1)S(1)} %bitcast.25, bf16[4,32,512]{2,1,0:T(8,128)(2,1)S(1)} %collective-permute-done.3.up_ref, bf16[4,32,512]{2,1,0:T(8,128)(2,1)S(1)} %collective-permute-done.4.down_ref, f32[32,8,128]{2,1,0:T(8,128)S(1)} %all-to-all-done.sums_ref), custom_call_target="tpu_custom_call" | custom-call | flops 65536 | bytes 65536 | tf_op jit(solution)/shard_map/pallas_call | solution.py:302
  45.0 11.0 %all-to-all-start.1 = ((bf16[16,112,256]{2,1,0:T(8,128)(2,1)}), bf16[16,112,256]{2,1,0:T(8,128)(2,1)S(1)}, u32[]{:S(2)}, u32[]{:S(2)}) async-start(bf16[16,112,256]{2,1,0:T(8,128)(2,1)} %shard_map.92), calls=%async_computation.1 | async-start | bytes 1835008 | tf_op jit(solution)/shard_map/all_to_all | solution.py:306
  56.0 3.4 %collective-permute-start.8 = (bf16[2,27,16,256]{3,2,1,0:T(8,128)(2,1)S(1)}, bf16[2,27,16,256]{3,2,1,0:T(8,128)(2,1)}, u32[]{:S(2)}, u32[]{:S(2)}) collective-permute-start(bf16[2,27,16,256]{3,2,1,0:T(8,128)(2,1)S(1)} %collective-permute-done.6.b1), channel_id=1, source_target_pairs={{0,4},{1,5},{2,6},{3,7},{4,8},{5,9},{6,10},{7,11},{8,12},{9,13},{1... | collective-permute-start | bytes 1327112 | tf_op jit(solution)/shard_map/ppermute | solution.py:258
  59.4 2.3 %collective-permute-start.7 = (bf16[2,27,16,256]{3,2,1,0:T(8,128)(2,1)S(1)}, bf16[2,27,16,256]{3,2,1,0:T(8,128)(2,1)}, u32[]{:S(2)}, u32[]{:S(2)}) collective-permute-start(bf16[2,27,16,256]{3,2,1,0:T(8,128)(2,1)S(1)} %collective-permute-done.5.a1), channel_id=1, source_target_pairs={{0,4},{1,5},{2,6},{3,7},{4,8},{5,9},{6,10},{7,11},{8,12},{9,13},{1... | collective-permute-start | bytes 1327112 | tf_op jit(solution)/shard_map/ppermute | solution.py:258
  61.7 6.0 %collective-permute-done.8.b2 = bf16[2,27,16,256]{3,2,1,0:T(8,128)(2,1)} collective-permute-done((bf16[2,27,16,256]{3,2,1,0:T(8,128)(2,1)S(1)}, bf16[2,27,16,256]{3,2,1,0:T(8,128)(2,1)}, u32[]{:S(2)}, u32[]{:S(2)}) %collective-permute-start.8) | collective-permute-done | bytes 442400 | tf_op jit(solution)/shard_map/ppermute | solution.py:258
  67.7 2.1 %collective-permute-start.10 = (bf16[2,27,16,256]{3,2,1,0:T(8,128)(2,1)}, bf16[2,27,16,256]{3,2,1,0:T(8,128)(2,1)S(1)}, u32[]{:S(2)}, u32[]{:S(2)}) collective-permute-start(bf16[2,27,16,256]{3,2,1,0:T(8,128)(2,1)} %collective-permute-done.8.b2), channel_id=1, source_target_pairs={{0,4},{1,5},{2,6},{3,7},{4,8},{5,9},{6,10},{7,11},{8,12},{9,13},{1... | collective-permute-start | bytes 1327112 | tf_op jit(solution)/shard_map/ppermute | solution.py:258
  69.9 2.7 %collective-permute-done.7.a2 = bf16[2,27,16,256]{3,2,1,0:T(8,128)(2,1)} collective-permute-done((bf16[2,27,16,256]{3,2,1,0:T(8,128)(2,1)S(1)}, bf16[2,27,16,256]{3,2,1,0:T(8,128)(2,1)}, u32[]{:S(2)}, u32[]{:S(2)}) %collective-permute-start.7) | collective-permute-done | bytes 442400 | tf_op jit(solution)/shard_map/ppermute | solution.py:258
  72.6 2.0 %collective-permute-start.9 = (bf16[2,27,16,256]{3,2,1,0:T(8,128)(2,1)}, bf16[2,27,16,256]{3,2,1,0:T(8,128)(2,1)S(1)}, u32[]{:S(2)}, u32[]{:S(2)}) collective-permute-start(bf16[2,27,16,256]{3,2,1,0:T(8,128)(2,1)} %collective-permute-done.7.a2), channel_id=1, source_target_pairs={{0,4},{1,5},{2,6},{3,7},{4,8},{5,9},{6,10},{7,11},{8,12},{9,13},{1... | collective-permute-start | bytes 1327112 | tf_op jit(solution)/shard_map/ppermute | solution.py:258
  74.6 2.7 %collective-permute-done.10.b3 = bf16[2,27,16,256]{3,2,1,0:T(8,128)(2,1)S(1)} collective-permute-done((bf16[2,27,16,256]{3,2,1,0:T(8,128)(2,1)}, bf16[2,27,16,256]{3,2,1,0:T(8,128)(2,1)S(1)}, u32[]{:S(2)}, u32[]{:S(2)}) %collective-permute-start.10) | collective-permute-done | bytes 442400 | tf_op jit(solution)/shard_map/ppermute | solution.py:258
  77.4 4.7 %collective-permute-done.9.a3 = bf16[2,27,16,256]{3,2,1,0:T(8,128)(2,1)S(1)} collective-permute-done((bf16[2,27,16,256]{3,2,1,0:T(8,128)(2,1)}, bf16[2,27,16,256]{3,2,1,0:T(8,128)(2,1)S(1)}, u32[]{:S(2)}, u32[]{:S(2)}) %collective-permute-start.9) | collective-permute-done | bytes 442400 | tf_op jit(solution)/shard_map/ppermute | solution.py:258
  82.1 0.9 broadcast_select_fusion
  83.0 3.0 %collective-permute-start.11 = (bf16[2,27,16,256]{3,2,1,0:T(8,128)(2,1)}, bf16[2,27,16,256]{3,2,1,0:T(8,128)(2,1)}, u32[]{:S(2)}, u32[]{:S(2)}) collective-permute-start(bf16[2,27,16,256]{3,2,1,0:T(8,128)(2,1)} %broadcast_select_fusion), channel_id=1, source_target_pairs={{0,4},{1,5},{2,6},{3,7},{4,8},{5,9},{6,10},{7,11},{8,12},{9,13},{1... | collective-permute-start | bytes 1327112 | tf_op jit(solution)/shard_map/ppermute | solution.py:258
  86.1 3.8 %shard_map.93.act_hbm = bf16[3,4,6,64,256]{4,3,2,1,0:T(8,128)(2,1)S(1)} custom-call(s32[5]{0:T(128)S(1)} %stack.38.at_ref, s32[10]{0:T(128)S(1)} %copy-done.10, f32[1,512]{1,0:T(1,128)S(1)} %bitcast.26, f32[1,512]{1,0:T(1,128)S(1)} %bitcast.27, f32[1,512]{1,0:T(1,128)S(1)} %bitcast.28, bf16[16,112,256]{2,1,0:T(8,128)(2,1)S(1)} %all-to-all-done.1.x_ref), custom_call_target="tpu_custom_call" | custom-call | flops 65536 | bytes 65536 | tf_op jit(solution)/shard_map/pallas_call | solution.py:309
  89.9 1.4 %copy-done = bf16[3,4,6,64,256]{4,3,2,1,0:T(8,128)(2,1)} copy-done((bf16[3,4,6,64,256]{4,3,2,1,0:T(8,128)(2,1)}, bf16[3,4,6,64,256]{4,3,2,1,0:T(8,128)(2,1)S(1)}, u32[]{:S(2)}) %copy-start) | copy-done | bytes 2359320
  91.3 1.1 collective-permute-done.11.r4
  92.4 7.8 %shard_map.94 = (f32[2,2,64,256]{3,2,1,0:T(8,128)}, f32[2,2,64,256]{3,2,1,0:T(8,128)}) custom-call(s32[5]{0:T(128)} %copy-done.3, bf16[3,4,6,64,256]{4,3,2,1,0:T(8,128)(2,1)} %copy-done, bf16[2,27,16,256]{3,2,1,0:T(8,128)(2,1)} %copy-done.12, bf16[2,27,16,256]{3,2,1,0:T(8,128)(2,1)} %copy-done.11, bf16[2,27,16,256]{3,2,1,0:T(8,128)(2,1)} %copy-done.16, ...), custom_call_target="tpu_custom_call" | custom-call | flops 65536 | bytes 65536 | tf_op jit(solution)/shard_map/pallas_call | solution.py:316
  100.2 7.7 %collective-permute-start.12 = (f32[2,2,64,256]{3,2,1,0:T(8,128)}, f32[2,2,64,256]{3,2,1,0:T(8,128)S(1)}, u32[]{:S(2)}, u32[]{:S(2)}) collective-permute-start(f32[2,2,64,256]{3,2,1,0:T(8,128)} %get-tuple-element.18), channel_id=1, source_target_pairs={{0,32},{1,33},{2,34},{3,35},{4,36},{5,37},{6,38},{7,39},{8,40},{9,... | collective-permute-start | bytes 786440 | tf_op jit(solution)/shard_map/ppermute | solution.py:258
  107.9 1.4 %collective-permute-done.12.b_ref = f32[2,2,64,256]{3,2,1,0:T(8,128)S(1)} collective-permute-done((f32[2,2,64,256]{3,2,1,0:T(8,128)}, f32[2,2,64,256]{3,2,1,0:T(8,128)S(1)}, u32[]{:S(2)}, u32[]{:S(2)}) %collective-permute-start.12) | collective-permute-done | bytes 262176 | tf_op jit(solution)/shard_map/ppermute | solution.py:258
  109.3 0.9 copy-done.2
  110.4 0.7 reshape.7
  (46 shorter events, 0.5 us)
Async XLA Ops:
  0.0 30.5 %copy-start.17 = (bf16[3,3,3,16,256]{4,3,2,1,0:T(8,128)(2,1)S(1)}, bf16[3,3,3,16,256]{4,3,2,1,0:T(8,128)(2,1)}, u32[]{:S(2)}) copy-start(bf16[3,3,3,16,256]{4,3,2,1,0:T(8,128)(2,1)} %param.13) | copy-start | bytes 663556
  0.0 42.7 %copy-start.1 = (bf16[1,4,2,32,512]{4,3,2,1,0:T(8,128)(2,1)S(1)}, bf16[1,4,2,32,512]{4,3,2,1,0:T(8,128)(2,1)}, u32[]{:S(2)}) copy-start(bf16[1,4,2,32,512]{4,3,2,1,0:T(8,128)(2,1)} %param.9) | copy-start | bytes 786436
  0.0 30.4 %collective-permute-start.1 = (bf16[27,16,256]{2,1,0:T(8,128)(2,1)}, bf16[27,16,256]{2,1,0:T(8,128)(2,1)S(1)}, u32[]{:S(2)}, u32[]{:S(2)}) collective-permute-start(bf16[27,16,256]{2,1,0:T(8,128)(2,1)} %bitcast.33), channel_id=1, source_target_pairs={{0,2},{1,3},{2,0},{3,1},{4,6},{5,7},{6,4},{7,5},{8,10},{9,11},{10,... | collective-permute-start | bytes 663560 | tf_op jit(solution)/shard_map/ppermute | solution.py:258
  3.2 27.3 %collective-permute-start.2 = (bf16[27,16,256]{2,1,0:T(8,128)(2,1)}, bf16[27,16,256]{2,1,0:T(8,128)(2,1)S(1)}, u32[]{:S(2)}, u32[]{:S(2)}) collective-permute-start(bf16[27,16,256]{2,1,0:T(8,128)(2,1)} %bitcast.34), channel_id=1, source_target_pairs={{0,1},{1,2},{2,3},{3,0},{4,5},{5,6},{6,7},{7,4},{8,9},{9,10},{10,1... | collective-permute-start | bytes 663560 | tf_op jit(solution)/shard_map/ppermute | solution.py:258
  6.9 23.6 %collective-permute-start = (bf16[27,16,256]{2,1,0:T(8,128)(2,1)}, bf16[27,16,256]{2,1,0:T(8,128)(2,1)S(1)}, u32[]{:S(2)}, u32[]{:S(2)}) collective-permute-start(bf16[27,16,256]{2,1,0:T(8,128)(2,1)} %bitcast.35), channel_id=1, source_target_pairs={{0,3},{1,0},{2,1},{3,2},{4,7},{5,4},{6,5},{7,6},{8,11},{9,8},{10,9... | collective-permute-start | bytes 663560 | tf_op jit(solution)/shard_map/ppermute | solution.py:258
  11.3 24.8 %all-to-all-start = ((f32[32,8,128]{2,1,0:T(8,128)}), f32[32,8,128]{2,1,0:T(8,128)S(1)}, u32[]{:S(2)}, u32[]{:S(2)}) async-start(f32[32,8,128]{2,1,0:T(8,128)} %shard_map.91), calls=%async_computation | async-start | bytes 262144 | tf_op jit(solution)/shard_map/all_to_all | solution.py:298
  25.1 6.5 %collective-permute-start.3 = (bf16[4,32,512]{2,1,0:T(8,128)(2,1)S(1)}, bf16[4,32,512]{2,1,0:T(8,128)(2,1)S(1)}, u32[]{:S(2)}, u32[]{:S(2)}) collective-permute-start(bf16[4,32,512]{2,1,0:T(8,128)(2,1)S(1)} %get-tuple-element.20), channel_id=1, source_target_pairs={{0,1},{1,2},{2,3},{3,4},{4,5},{5,6},{6,7},{7,8},{8,9},{9,10},{10,1... | collective-permute-start | bytes 393224 | tf_op jit(solution)/shard_map/ppermute | solution.py:258
  28.2 7.8 %collective-permute-start.4 = (bf16[4,32,512]{2,1,0:T(8,128)(2,1)S(1)}, bf16[4,32,512]{2,1,0:T(8,128)(2,1)S(1)}, u32[]{:S(2)}, u32[]{:S(2)}) collective-permute-start(bf16[4,32,512]{2,1,0:T(8,128)(2,1)S(1)} %get-tuple-element.19), channel_id=1, source_target_pairs={{1,0},{2,1},{3,2},{4,3},{5,4},{6,5},{7,6},{8,7},{9,8},{10,9},{11,1... | collective-permute-start | bytes 393224 | tf_op jit(solution)/shard_map/ppermute | solution.py:258
  30.5 52.5 %copy-start.11 = (bf16[2,27,16,256]{3,2,1,0:T(8,128)(2,1)}, bf16[2,27,16,256]{3,2,1,0:T(8,128)(2,1)S(1)}, u32[]{:S(2)}) copy-start(bf16[2,27,16,256]{3,2,1,0:T(8,128)(2,1)S(1)} %pad_maximum_fusion.1.b0) | copy-start | bytes 1327108
  30.6 52.4 %copy-start.12 = (bf16[2,27,16,256]{3,2,1,0:T(8,128)(2,1)}, bf16[2,27,16,256]{3,2,1,0:T(8,128)(2,1)S(1)}, u32[]{:S(2)}) copy-start(bf16[2,27,16,256]{3,2,1,0:T(8,128)(2,1)S(1)} %pad_maximum_fusion.a0) | copy-start | bytes 1327108
  36.0 19.9 %collective-permute-start.6 = (bf16[2,27,16,256]{3,2,1,0:T(8,128)(2,1)S(1)}, bf16[2,27,16,256]{3,2,1,0:T(8,128)(2,1)S(1)}, u32[]{:S(2)}, u32[]{:S(2)}) collective-permute-start(bf16[2,27,16,256]{3,2,1,0:T(8,128)(2,1)S(1)} %pad_maximum_fusion.1.b0), channel_id=1, source_target_pairs={{0,4},{1,5},{2,6},{3,7},{4,8},{5,9},{6,10},{7,11},{8,12},{9,13},{1... | collective-permute-start | bytes 1327112 | tf_op jit(solution)/shard_map/ppermute | solution.py:258
  38.0 21.4 %collective-permute-start.5 = (bf16[2,27,16,256]{3,2,1,0:T(8,128)(2,1)S(1)}, bf16[2,27,16,256]{3,2,1,0:T(8,128)(2,1)S(1)}, u32[]{:S(2)}, u32[]{:S(2)}) collective-permute-start(bf16[2,27,16,256]{3,2,1,0:T(8,128)(2,1)S(1)} %pad_maximum_fusion.a0), channel_id=1, source_target_pairs={{0,4},{1,5},{2,6},{3,7},{4,8},{5,9},{6,10},{7,11},{8,12},{9,13},{1... | collective-permute-start | bytes 1327112 | tf_op jit(solution)/shard_map/ppermute | solution.py:258
  42.7 43.3 %copy-start.3 = (s32[5]{0:T(128)}, s32[5]{0:T(128)S(1)}, u32[]{:S(2)}) copy-start(s32[5]{0:T(128)S(1)} %stack.38.at_ref) | copy-start | bytes 64
  42.7 43.3 %copy-start.4 = (f32[512]{0:T(512)S(1)}, f32[512]{0:T(512)}, u32[]{:S(2)}) copy-start(f32[512]{0:T(512)} %param.10) | copy-start | bytes 6148
  42.7 43.3 %copy-start.5 = (f32[512]{0:T(512)S(1)}, f32[512]{0:T(512)}, u32[]{:S(2)}) copy-start(f32[512]{0:T(512)} %param.11) | copy-start | bytes 6148
  42.7 43.3 %copy-start.6 = (f32[512]{0:T(512)S(1)}, f32[512]{0:T(512)}, u32[]{:S(2)}) copy-start(f32[512]{0:T(512)} %param.12) | copy-start | bytes 6148
  42.7 43.3 %copy-start.10 = (s32[10]{0:T(128)S(1)}, s32[10]{0:T(128)}, u32[]{:S(2)}) copy-start(s32[10]{0:T(128)} %lengths_ref.1) | copy-start | bytes 124
  45.0 41.0 %all-to-all-start.1 = ((bf16[16,112,256]{2,1,0:T(8,128)(2,1)}), bf16[16,112,256]{2,1,0:T(8,128)(2,1)S(1)}, u32[]{:S(2)}, u32[]{:S(2)}) async-start(bf16[16,112,256]{2,1,0:T(8,128)(2,1)} %shard_map.92), calls=%async_computation.1 | async-start | bytes 1835008 | tf_op jit(solution)/shard_map/all_to_all | solution.py:306
  55.9 5.8 %copy-start.15 = (bf16[2,27,16,256]{3,2,1,0:T(8,128)(2,1)}, bf16[2,27,16,256]{3,2,1,0:T(8,128)(2,1)S(1)}, u32[]{:S(2)}) copy-start(bf16[2,27,16,256]{3,2,1,0:T(8,128)(2,1)S(1)} %collective-permute-done.6.b1) | copy-start | bytes 1327108
  56.0 11.8 %collective-permute-start.8 = (bf16[2,27,16,256]{3,2,1,0:T(8,128)(2,1)S(1)}, bf16[2,27,16,256]{3,2,1,0:T(8,128)(2,1)}, u32[]{:S(2)}, u32[]{:S(2)}) collective-permute-start(bf16[2,27,16,256]{3,2,1,0:T(8,128)(2,1)S(1)} %collective-permute-done.6.b1), channel_id=1, source_target_pairs={{0,4},{1,5},{2,6},{3,7},{4,8},{5,9},{6,10},{7,11},{8,12},{9,13},{1... | collective-permute-start | bytes 1327112 | tf_op jit(solution)/shard_map/ppermute | solution.py:258
  59.4 10.5 %copy-start.16 = (bf16[2,27,16,256]{3,2,1,0:T(8,128)(2,1)}, bf16[2,27,16,256]{3,2,1,0:T(8,128)(2,1)S(1)}, u32[]{:S(2)}) copy-start(bf16[2,27,16,256]{3,2,1,0:T(8,128)(2,1)S(1)} %collective-permute-done.5.a1) | copy-start | bytes 1327108
  59.4 13.2 %collective-permute-start.7 = (bf16[2,27,16,256]{3,2,1,0:T(8,128)(2,1)S(1)}, bf16[2,27,16,256]{3,2,1,0:T(8,128)(2,1)}, u32[]{:S(2)}, u32[]{:S(2)}) collective-permute-start(bf16[2,27,16,256]{3,2,1,0:T(8,128)(2,1)S(1)} %collective-permute-done.5.a1), channel_id=1, source_target_pairs={{0,4},{1,5},{2,6},{3,7},{4,8},{5,9},{6,10},{7,11},{8,12},{9,13},{1... | collective-permute-start | bytes 1327112 | tf_op jit(solution)/shard_map/ppermute | solution.py:258
  67.7 9.6 %collective-permute-start.10 = (bf16[2,27,16,256]{3,2,1,0:T(8,128)(2,1)}, bf16[2,27,16,256]{3,2,1,0:T(8,128)(2,1)S(1)}, u32[]{:S(2)}, u32[]{:S(2)}) collective-permute-start(bf16[2,27,16,256]{3,2,1,0:T(8,128)(2,1)} %collective-permute-done.8.b2), channel_id=1, source_target_pairs={{0,4},{1,5},{2,6},{3,7},{4,8},{5,9},{6,10},{7,11},{8,12},{9,13},{1... | collective-permute-start | bytes 1327112 | tf_op jit(solution)/shard_map/ppermute | solution.py:258
  72.6 9.5 %collective-permute-start.9 = (bf16[2,27,16,256]{3,2,1,0:T(8,128)(2,1)}, bf16[2,27,16,256]{3,2,1,0:T(8,128)(2,1)S(1)}, u32[]{:S(2)}, u32[]{:S(2)}) collective-permute-start(bf16[2,27,16,256]{3,2,1,0:T(8,128)(2,1)} %collective-permute-done.7.a2), channel_id=1, source_target_pairs={{0,4},{1,5},{2,6},{3,7},{4,8},{5,9},{6,10},{7,11},{8,12},{9,13},{1... | collective-permute-start | bytes 1327112 | tf_op jit(solution)/shard_map/ppermute | solution.py:258
  77.4 15.0 %copy-start.13 = (bf16[2,27,16,256]{3,2,1,0:T(8,128)(2,1)}, bf16[2,27,16,256]{3,2,1,0:T(8,128)(2,1)S(1)}, u32[]{:S(2)}) copy-start(bf16[2,27,16,256]{3,2,1,0:T(8,128)(2,1)S(1)} %collective-permute-done.10.b3) | copy-start | bytes 1327108
  82.1 10.2 %copy-start.14 = (bf16[2,27,16,256]{3,2,1,0:T(8,128)(2,1)}, bf16[2,27,16,256]{3,2,1,0:T(8,128)(2,1)S(1)}, u32[]{:S(2)}) copy-start(bf16[2,27,16,256]{3,2,1,0:T(8,128)(2,1)S(1)} %collective-permute-done.9.a3) | copy-start | bytes 1327108
  83.0 9.4 %collective-permute-start.11 = (bf16[2,27,16,256]{3,2,1,0:T(8,128)(2,1)}, bf16[2,27,16,256]{3,2,1,0:T(8,128)(2,1)}, u32[]{:S(2)}, u32[]{:S(2)}) collective-permute-start(bf16[2,27,16,256]{3,2,1,0:T(8,128)(2,1)} %broadcast_select_fusion), channel_id=1, source_target_pairs={{0,4},{1,5},{2,6},{3,7},{4,8},{5,9},{6,10},{7,11},{8,12},{9,13},{1... | collective-permute-start | bytes 1327112 | tf_op jit(solution)/shard_map/ppermute | solution.py:258
  89.9 1.4 %copy-start = (bf16[3,4,6,64,256]{4,3,2,1,0:T(8,128)(2,1)}, bf16[3,4,6,64,256]{4,3,2,1,0:T(8,128)(2,1)S(1)}, u32[]{:S(2)}) copy-start(bf16[3,4,6,64,256]{4,3,2,1,0:T(8,128)(2,1)S(1)} %shard_map.93.act_hbm) | copy-start | bytes 7077892
  91.3 17.9 %copy-start.7 = (f32[256]{0:T(256)S(1)}, f32[256]{0:T(256)}, u32[]{:S(2)}) copy-start(f32[256]{0:T(256)} %param.14) | copy-start | bytes 3076
  91.3 17.9 %copy-start.8 = (f32[256]{0:T(256)S(1)}, f32[256]{0:T(256)}, u32[]{:S(2)}) copy-start(f32[256]{0:T(256)} %param.15) | copy-start | bytes 3076
  91.3 18.0 %copy-start.9 = (s32[64]{0:T(128)S(1)}, s32[64]{0:T(128)}, u32[]{:S(2)}) copy-start(s32[64]{0:T(128)} %param.17) | copy-start | bytes 772
  100.2 9.0 %collective-permute-start.12 = (f32[2,2,64,256]{3,2,1,0:T(8,128)}, f32[2,2,64,256]{3,2,1,0:T(8,128)S(1)}, u32[]{:S(2)}, u32[]{:S(2)}) collective-permute-start(f32[2,2,64,256]{3,2,1,0:T(8,128)} %get-tuple-element.18), channel_id=1, source_target_pairs={{0,32},{1,33},{2,34},{3,35},{4,36},{5,37},{6,38},{7,39},{8,40},{9,... | collective-permute-start | bytes 786440 | tf_op jit(solution)/shard_map/ppermute | solution.py:258
  (1 other events, 1.0 us)

commit v3 on v2

v3 whole, which is shorter than its diff:
```python
import functools
import jax
import jax.numpy as jnp
from jax import lax
from jax.experimental import pallas as pl
from jax.experimental.pallas import tpu as pltpu
from jax.sharding import Mesh, PartitionSpec as P

C = 512
CO = 256
GROUPS = 32
GW = C // GROUPS
FR = 4
W = 32
SLABS = 16
T = FR * SLABS
HALF = C // 2
SHARD = 27 * GW
EDGE = FR * W
NY, NC, NZ, NX = 8, 2, 8, 4
AXES = ("y", "core", "z", "x")
HIGH = lax.Precision.HIGHEST
F32 = jnp.float32
BF16 = jnp.bfloat16
CELLS = 64 * GW
FRAME_CELLS = CELLS * NZ * NX
VMEM = pl.BlockSpec(memory_space=pltpu.VMEM)
SMEM = pl.BlockSpec(memory_space=pltpu.SMEM)
ANY = pl.BlockSpec(memory_space=pl.ANY)


def iota(shape, dim):
    return lax.broadcasted_iota(jnp.int32, shape, dim)


def group_of(shape, channel_dim, group_dim):
    return flag((iota(shape, channel_dim) >> 4) == iota(shape, group_dim))


def flag(condition):
    return condition.astype(F32).astype(BF16)


def bdot(a, b):
    return jnp.dot(a, b, preferred_element_type=F32)


def in_three(v):
    high = v.astype(BF16)
    rest = v - high.astype(F32)
    middle = rest.astype(BF16)
    return high, middle, (rest - middle.astype(F32)).astype(BF16)


def take(v, picks):
    n = v.shape[0]
    pad = -n % 8
    parts = [jnp.concatenate([p.astype(F32), jnp.zeros((pad, v.shape[1]), F32)], axis=0) for p in in_three(v)]
    out = bdot(jnp.concatenate(parts, axis=0).astype(BF16), picks)
    return out[:n] + out[n + pad : 2 * n + pad] + out[2 * (n + pad) : 3 * n + 2 * pad]


def prepare(x_hbm, w_ref, sums_ref, next_ref, prev_ref, x_ref, sem):
    loads = [pltpu.make_async_copy(x_hbm.at[f], x_ref.at[f], sem.at[f]) for f in range(FR)]
    for copy in loads:
        copy.start()
    for out_ref in (next_ref, prev_ref):
        out_ref[:SHARD] = w_ref[...].reshape(SHARD, CO)
    to_groups, to_channels = group_of((C, 128), 0, 1), group_of((128, C), 1, 0)
    rows = []
    for f in range(FR):
        loads[f].wait()
        rows.append(x_ref[f].reshape(2 * W, C).astype(F32))
    totals = jnp.concatenate([jnp.sum(v, axis=0, keepdims=True) for v in rows], axis=0)
    mean = take(totals, to_groups) * (1.0 / CELLS)
    spread = take(mean, to_channels)
    squares = []
    for f in range(FR):
        d = rows[f] - spread[f : f + 1]
        squares.append(jnp.sum(d * d, axis=0, keepdims=True))
    squares = take(jnp.concatenate(squares, axis=0), to_groups)
    for out_ref, row in ((next_ref, 1), (prev_ref, 0)):
        edge = x_ref[:, row].reshape(EDGE, C)
        out_ref[SHARD : SHARD + EDGE] = edge[:, :HALF]
        out_ref[SHARD + EDGE :] = edge[:, HALF:]
    sums_ref[...] = jnp.broadcast_to(jnp.concatenate([mean, squares], axis=0)[None], sums_ref.shape)


def join_space(v):
    n = NZ * NX
    mean = jnp.sum(v[:, :FR], axis=0) * (1.0 / n)
    d = v[:, :FR] - mean[None]
    squares = jnp.sum(v[:, FR:], axis=0) + CELLS * jnp.sum(d * d, axis=0)
    return jnp.concatenate([mean, squares], axis=0)


def channel_at(s, core, place):
    step = (place + 2 * GW) >> 6
    nth = jnp.where(step == 0, place >> 4, ((place >> 4) + 2) & 3)
    away = jnp.where(core == 0, jnp.where(nth == 2, -1, jnp.where(nth == 3, 2, nth)), jnp.where(nth == 0, 2, nth - 2))
    away = away + NX * jnp.where(core == 0, -step, step)
    return (((s + away) & (NZ * NX - 1)) << 4) + (place & 15)


def pack(at_ref, own_ref, up_ref, down0_ref, down1_ref, sums_ref, out_ref):
    s = at_ref[2]

    def edge(ref):
        return jnp.concatenate([ref[SHARD : SHARD + EDGE], ref[SHARD + EDGE :]], axis=1)

    down = jnp.where(at_ref[1] == 0, edge(down0_ref), edge(down1_ref))
    source = jnp.concatenate([edge(up_ref), own_ref[...].reshape(2 * EDGE, C), down], axis=0)
    n = 4 * FR * W
    to = iota((n, 1), 0)
    col, row, frame = to >> 4, (to >> 2) & 3, to & 3
    want = jnp.where(
        row == 0,
        frame * W + col,
        jnp.where(row == 3, 3 * EDGE + frame * W + col, EDGE + (frame * 2 + row - 1) * W + col),
    )
    order = flag(want == iota((n, n), 1))
    place = iota((1, C), 1)
    roll = flag(iota((C, C), 0) == channel_at(s, place >> 8, place & (HALF - 1)))
    sorted_rows = bdot(order, source).astype(BF16)
    rolled = bdot(sorted_rows, roll).astype(BF16)
    sums = jnp.concatenate([join_space(sums_ref[...]), jnp.zeros((8, 128), F32)], axis=0)
    thirds = [p[:, :GROUPS] for p in in_three(sums)]
    thirds = jnp.concatenate(thirds + [jnp.zeros((16, HALF - 3 * GROUPS), BF16)], axis=1)
    for y in range(NY):
        for core in range(NC):
            lanes = slice(HALF * core, HALF * (core + 1))
            lo, hi = max(4 * y - 1, 0), min(4 * y + 5, W)
            first = lo - (4 * y - 1)
            out_ref[2 * y + core, 16 * first : 16 * (first + hi - lo), :] = rolled[16 * lo : 16 * hi, lanes]
            out_ref[2 * y + core, 96:112, :] = thirds
            if y == 0:
                out_ref[2 * y + core, 0:16, :] = jnp.zeros((16, HALF), BF16)
            if y == NY - 1:
                out_ref[2 * y + core, 80:96, :] = jnp.zeros((16, HALF), BF16)


def starts(lengths_ref, frame):
    end = lengths_ref[0]
    start = jnp.zeros_like(frame)
    for k in range(1, lengths_ref.shape[0]):
        start = jnp.where(frame >= end, end, start)
        end = end + lengths_ref[k]
    return start


def activate(at_ref, lengths_ref, gamma_ref, beta_ref, smooth_ref, x_ref, act_ref):
    y, core, s = at_ref[0], at_ref[1], at_ref[2]
    n = 2 * T
    thirds = x_ref[:, 96:112, :].astype(F32)[:, :8, :128].reshape(n, 128)
    rows, columns = iota((n, 1), 0), iota((1, n), 1)
    frame_a, frame_b = (rows >> 3) * FR + (rows & 3), (columns >> 3) * FR + (columns & 3)
    same = starts(lengths_ref, frame_a) == starts(lengths_ref, frame_b)
    means_b = (columns & 4) == 0
    on_means, on_squares = same & means_b, flag(same & jnp.logical_not(means_b))
    count = jnp.sum(on_means.astype(F32), axis=1, keepdims=True)
    on_means = flag(on_means)

    def whole(v):
        return v[:, :GROUPS] + v[:, GROUPS : 2 * GROUPS] + v[:, 2 * GROUPS : 3 * GROUPS]

    def parts(v):
        return jnp.concatenate(list(in_three(v)) + [jnp.zeros((n, 128 - 3 * GROUPS), BF16)], axis=1)

    mean = whole(bdot(on_means, thirds.astype(BF16))) / count
    off = whole(thirds) - mean
    squares = whole(bdot(on_squares, thirds.astype(BF16))) + FRAME_CELLS * whole(bdot(on_means, parts(off * off)))
    inverse = lax.rsqrt(squares / (count * FRAME_CELLS) + 1e-6)
    pick = flag((frame_b == iota((T, 1), 0)) & means_b)
    channels = channel_at(s, core, iota((1, HALF), 1))
    mine = flag(iota((C, HALF), 0) == channels)
    third = iota((128, 1), 0)
    to_group = flag(((third & (GROUPS - 1)) == (channels >> 4)) & (third < 3 * GROUPS))
    affine = take(jnp.concatenate([gamma_ref[...], beta_ref[...], smooth_ref[...]], axis=0), mine)
    gamma, beta, unsmooth = affine[0:1], affine[1:2], 1.0 / affine[2:3]
    mean = bdot(bdot(pick, parts(mean)).astype(BF16), to_group)
    scale = bdot(bdot(pick, parts(inverse)).astype(BF16), to_group) * gamma

    m = 16 * 16
    to = iota((m, 1), 0)
    row, t = to >> 6, to & (T - 1)
    by_row = flag(iota((m, m), 1) == (t >> 2) * 16 + row * FR + (t & 3))
    frame, other = iota((T, 1), 0), iota((T, T), 1)
    start = starts(lengths_ref, frame)
    earlier = [flag(other == jnp.maximum(frame - back, start)) for back in (2, 1)]
    earlier = jnp.concatenate(earlier, axis=0)
    for c in range(6):
        rows = x_ref[:, 16 * c : 16 * (c + 1), :].reshape(m, HALF)
        values = bdot(by_row, rows)
        for r in range(4):
            v = (values[T * r : T * (r + 1)] - mean) * scale + beta
            v = v / (1.0 + jnp.exp(-v)) * unsmooth
            inside = None
            if r == 0:
                inside = s > 0
            if r == 3:
                inside = s < NZ * NX - 1
            if c == 0:
                inside = (y > 0) if inside is None else inside & (y > 0)
            if c == 5:
                inside = (y < NY - 1) if inside is None else inside & (y < NY - 1)
            if inside is not None:
                v = v * inside.astype(F32)
            v = v.astype(BF16)
            act_ref[2, r, c] = v
            e = bdot(earlier, v).astype(BF16)
            act_ref[0, r, c] = e[:T]
            act_ref[1, r, c] = e[T:]


def convolve(own_columns, at_ref, act_ref, *refs):
    weights, out_ref = refs[:-1], refs[-1]
    core = at_ref[1]
    column = 2 * core if own_columns else 2 - 2 * core
    total = None
    for tap in range(27):
        j, a, b = tap // 9, tap // 3 % 3, tap % 3
        lhs = act_ref[j, a : a + 2, pl.ds(column + b, 2)].reshape(4 * T, HALF)
        rows = jnp.concatenate([v[i, tap] for v in weights for i in range(2)], axis=0)
        term = bdot(lhs, rows)
        total = term if total is None else total + term
    out_ref[...] = total.reshape(2, 2, T, CO)


def finish(order_ref, scale_ref, bias_ref, a_ref, b_ref, out_ref):
    picked = (iota((T, T), 0) == order_ref[...]).astype(F32).astype(BF16)
    for r in range(2):
        for c in range(2):
            v = ((a_ref[r, c] + b_ref[r, c]) * scale_ref[...] + bias_ref[...]).astype(BF16)
            v = lax.dot_general(picked, v, (((0,), (0,)), ((), ())), preferred_element_type=F32)
            at = (2 * r + c) * CO
            out_ref[:, at : at + CO] = v.astype(BF16)


def shift(value, step):
    pairs = []
    for i in range(NY * NC * NZ * NX):
        y, core, z, x = i // 64, i // 32 % 2, i // 4 % 8, i % 4
        to = step(y, core, z, x)
        if to is not None:
            ty, tc, tz, tx = to
            pairs.append((i, ((ty * NC + tc) * NZ + tz % NZ) * NX + tx))
    return lax.ppermute(value, AXES, pairs)


def by_space(y, core, s):
    return (y, core, s // NX, s % NX) if 0 <= s < NZ * NX else None


def struct(shape, dtype):
    return jax.ShapeDtypeStruct(shape, dtype)


def params(mib=48):
    return pltpu.CompilerParams(vmem_limit_bytes=mib * 2**20)


def cost(flops, size):
    return pl.CostEstimate(flops=flops, bytes_accessed=size, transcendentals=0)


def call_prepare(latent, weights):
    beside = struct((SHARD + 2 * EDGE, CO), BF16)
    return pl.pallas_call(
        prepare, out_shape=(struct((NZ * NX, 8, 128), F32), beside, beside), in_specs=[ANY, VMEM],
        out_specs=(VMEM, VMEM, VMEM),
        scratch_shapes=[pltpu.VMEM((FR, 2, W, C), BF16), pltpu.SemaphoreType.DMA((FR,))],
        compiler_params=params(60), cost_estimate=cost(2**16, 2**16),
    )(latent, weights)


def call_pack(*args):
    return pl.pallas_call(
        pack, out_shape=struct((SLABS, 112, HALF), BF16), in_specs=[SMEM] + [VMEM] * 5, out_specs=VMEM,
        compiler_params=params(), cost_estimate=cost(2**16, 2**16),
    )(*args)


def call_activate(*args):
    return pl.pallas_call(
        activate, out_shape=struct((3, 4, 6, T, HALF), BF16), in_specs=[SMEM, SMEM] + [VMEM] * 4, out_specs=VMEM,
        compiler_params=params(), cost_estimate=cost(2**16, 2**16),
    )(*args)


def call_finish(*args):
    return pl.pallas_call(
        finish, out_shape=struct((T, 4 * CO), BF16), in_specs=[VMEM] * 5, out_specs=VMEM, compiler_params=params(),
        cost_estimate=cost(2**22, 2**20),
    )(*args)


def local(latent, gamma, beta, smooth, weights, w_scale, bias, lengths, order):
    y, core, z, x = (lax.axis_index(a) for a in AXES)
    at = jnp.stack([y, core, z * NX + x]).astype(jnp.int32)
    latent = latent[0]
    weights = weights.reshape(27, GW, CO)

    spread, to_next, to_prev = call_prepare(latent, weights)

    def ring(v):
        return shift(v, lambda y, core, z, x: (y, core, z + 1 - 2 * core, x))

    def along(v, *d):
        return shift(v, lambda y, core, z, x: by_space(y, core, (z * NX + x - d[core]) % (NZ * NX)))

    def shard(v):
        return v[:SHARD].reshape(27, GW, CO)

    n1, n2, n3 = along(to_prev, 1, 2), along(to_next, -1, -1), along(to_prev, 2, 1)
    gathered = lax.all_to_all(spread, ("z", "x"), 0, 0, tiled=True)
    a0 = jnp.where(core == 0, jnp.stack([weights, shard(n1)]), jnp.stack([shard(n1), shard(n2)]))
    b0 = jnp.where(core == 0, jnp.stack([shard(n2), shard(n3)]), jnp.stack([weights, shard(n3)]))
    a1, b1 = ring(a0), ring(b0)
    windows = call_pack(at, latent, n2, n1, n3, gathered)
    columns = lax.all_to_all(windows, ("y", "core"), 0, 0, tiled=True)
    a2, b2 = ring(lax.optimization_barrier((a1, b1))[0]), ring(b1)
    a3, b3 = ring(a2), ring(b2)
    act = call_activate(at, lengths, gamma[None], beta[None], smooth[None], columns)
    a4 = ring(a3)


    def part(own_columns):
        return pl.pallas_call(
            functools.partial(convolve, own_columns), out_shape=struct((2, 2, T, CO), F32),
            in_specs=[SMEM] + [VMEM] * 9, out_specs=VMEM, compiler_params=params(32), cost_estimate=cost(2**30, 2**16),
        )(at, act, a0, a1, b1, a2, b2, a3, b3, a4)

    other = shift(part(False), lambda y, core, z, x: (y, 1 - core, z, x))
    keep = part(True)
    out = call_finish(order[None], w_scale[None], bias[None], keep, other)
    return out.reshape(SLABS, FR, 2, 2, CO)


def solution(mesh):
    inner = Mesh(mesh.devices.reshape(NY, NC, NZ, NX), AXES)
    slab, space = ("y", "core"), ("z", "x")
    in_specs = (
        P(slab, None, space, None, None), P(), P(), P(), P(None, None, None, space, None), P(), P(), P(), P(),
    )
    out_specs = P(None, None, space, slab, None)
    return jax.shard_map(local, mesh=inner, in_specs=in_specs, out_specs=out_specs, check_vma=False)
```

time: 112 us -> 98.9 us (0.88)
  the two profiles are of different devices: /device:TPU:15 before, /device:TPU:1 now
where the time goes in v3:
time: 98.9 us; the launch traced here: 98.2 us
  starting transfers between devices  70.5 us (71%)
  Pallas kernels  13.5 us (14%)
  waiting for transfers between devices  11.1 us (11%)
  other arithmetic  1.92 us (2%)
    ppermute x11, starting transfers between devices, shift(): return lax.ppermute(value, AXES, pairs)  57.1 us
    ppermute x11, waiting for transfers between devices, shift(): return lax.ppermute(value, AXES, pairs)  11.1 us
    all_to_all x1, starting transfers between devices, local(): columns = lax.all_to_all(windows, ('y', 'core'), 0, 0, tiled=True)  8.06 us
    all_to_all x1, starting transfers between devices, local(): gathered = lax.all_to_all(spread, ('z', 'x'), 0, 0, tiled=True)  5.31 us
    pallas_call x2, Pallas kernels, part(): pl.pallas_call(functools.partial(convolve, own_columns), out_shape=struct...  4.76 us
    pallas_call x1, Pallas kernels, call_prepare(): pl.pallas_call(prepare, out_shape=(struct((NZ * NX, 8, 128), F32), beside...  3.22 us
    pallas_call x1, Pallas kernels, call_activate(): pl.pallas_call(activate, out_shape=struct((3, 4, 6, T, HALF), BF16), in_s...  3.04 us
    pallas_call x1, Pallas kernels, call_pack(): pl.pallas_call(pack, out_shape=struct((SLABS, 112, HALF), BF16), in_specs...  2.24 us
  transfers between devices with their start and end apart: 13, of which 4 were waited for; matrix products, arithmetic and copies ran while one was open for 2% of the time, Pallas kernels for 8%

profile of v3, /device:TPU:1, one launch (start us, length us, event | category | flops | bytes accessed | tf_op | source)
XLA Modules:
  0.0 98.2 jit_solution(4815709453108292020)
XLA Ops:
  0.0 3.2 %shard_map.91 = (f32[32,8,128]{2,1,0:T(8,128)}, bf16[688,256]{1,0:T(8,128)(2,1)}, bf16[688,256]{1,0:T(8,128)(2,1)}) custom-call(bf16[4,2,32,512]{3,2,1,0:T(8,128)(2,1)} %bitcast.15, bf16[27,16,256]{2,1,0:T(8,128)(2,1)} %bitcast.26), custom_call_target="tpu_custom_call" | custom-call | flops 65536 | bytes 65536 | tf_op jit(solution)/shard_map/pallas_call | solution.py:268
  3.2 13.7 %collective-permute-start.2 = (bf16[688,256]{1,0:T(8,128)(2,1)}, bf16[688,256]{1,0:T(8,128)(2,1)S(1)}, u32[]{:S(2)}, u32[]{:S(2)}) collective-permute-start(bf16[688,256]{1,0:T(8,128)(2,1)} %get-tuple-element.10), channel_id=1, source_target_pairs={{0,30},{1,31},{2,0},{3,1},{4,2},{5,3},{6,4},{7,5},{8,6},{9,7},{10,... | collective-permute-start | bytes 1056776 | tf_op jit(solution)/shard_map/ppermute | solution.py:247
  16.9 1.9 %collective-permute-start = (bf16[688,256]{1,0:T(8,128)(2,1)}, bf16[688,256]{1,0:T(8,128)(2,1)S(1)}, u32[]{:S(2)}, u32[]{:S(2)}) collective-permute-start(bf16[688,256]{1,0:T(8,128)(2,1)} %get-tuple-element.9), channel_id=1, source_target_pairs={{0,1},{1,2},{2,3},{3,4},{4,5},{5,6},{6,7},{7,8},{8,9},{9,10},{10,1... | collective-permute-start | bytes 1056776 | tf_op jit(solution)/shard_map/ppermute | solution.py:247
  18.9 3.6 %collective-permute-start.1 = (bf16[688,256]{1,0:T(8,128)(2,1)}, bf16[688,256]{1,0:T(8,128)(2,1)S(1)}, u32[]{:S(2)}, u32[]{:S(2)}) collective-permute-start(bf16[688,256]{1,0:T(8,128)(2,1)} %get-tuple-element.10), channel_id=1, source_target_pairs={{0,31},{1,0},{2,1},{3,2},{4,3},{5,4},{6,5},{7,6},{8,7},{9,8},{10,9... | collective-permute-start | bytes 1056776 | tf_op jit(solution)/shard_map/ppermute | solution.py:247
  22.5 5.3 %all-to-all-start = ((f32[32,8,128]{2,1,0:T(8,128)}), f32[32,8,128]{2,1,0:T(8,128)S(1)}, u32[]{:S(2)}, u32[]{:S(2)}) async-start(f32[32,8,128]{2,1,0:T(8,128)} %get-tuple-element.11), calls=%async_computation | async-start | bytes 262144 | tf_op jit(solution)/shard_map/all_to_all | solution.py:315
  27.8 0.0 collective-permute-done.2.down1_ref
  27.9 6.6 %collective-permute-done.up_ref = bf16[688,256]{1,0:T(8,128)(2,1)S(1)} collective-permute-done((bf16[688,256]{1,0:T(8,128)(2,1)}, bf16[688,256]{1,0:T(8,128)(2,1)S(1)}, u32[]{:S(2)}, u32[]{:S(2)}) %collective-permute-start) | collective-permute-done | bytes 352288 | tf_op jit(solution)/shard_map/ppermute | solution.py:247
  34.5 1.8 %fusion = (bf16[2,27,16,256]{3,2,1,0:T(8,128)(2,1)}, bf16[2,27,16,256]{3,2,1,0:T(8,128)(2,1)S(1)}) fusion(bf16[1,27,16,256]{3,2,1,0:T(8,128)(2,1)S(1)} %bitcast.23, bf16[1,27,16,256]{3,2,1,0:T(8,128)(2,1)} %bitcast.27, bf16[1,27,16,256]{3,2,1,0:T(8,128)(2,1)S(1)} %bitcast.24, pred[]{:T(512)S(6)} %eq.4, bf16[1,27,16,256]{3,2,1,0:T(8,128)(2,1)S(1)} %bitcast.25), kind=kLoop, calls=%fused_computation.3 | loop fusion | flops 1327104 | bytes 1769473 | tf_op jit(solution)/shard_map/jit(_where)/select_n | solution.py:317
  36.4 4.2 %collective-permute-start.3 = (bf16[2,27,16,256]{3,2,1,0:T(8,128)(2,1)S(1)}, bf16[2,27,16,256]{3,2,1,0:T(8,128)(2,1)S(1)}, u32[]{:S(2)}, u32[]{:S(2)}) collective-permute-start(bf16[2,27,16,256]{3,2,1,0:T(8,128)(2,1)S(1)} %get-tuple-element.14.refs_0_), channel_id=1, source_target_pairs={{0,4},{1,5},{2,6},{3,7},{4,8},{5,9},{6,10},{7,11},{8,12},{9,13},{1... | collective-permute-start | bytes 1327112 | tf_op jit(solution)/shard_map/ppermute | solution.py:247
  40.5 1.9 %collective-permute-start.4 = (bf16[2,27,16,256]{3,2,1,0:T(8,128)(2,1)}, bf16[2,27,16,256]{3,2,1,0:T(8,128)(2,1)S(1)}, u32[]{:S(2)}, u32[]{:S(2)}) collective-permute-start(bf16[2,27,16,256]{3,2,1,0:T(8,128)(2,1)} %get-tuple-element.13), channel_id=1, source_target_pairs={{0,4},{1,5},{2,6},{3,7},{4,8},{5,9},{6,10},{7,11},{8,12},{9,13},{1... | collective-permute-start | bytes 1327112 | tf_op jit(solution)/shard_map/ppermute | solution.py:247
  42.5 0.1 pad_add_fusion.at_ref
  42.6 0.0 all-to-all-done.sums_ref
  42.6 2.2 %shard_map.92 = bf16[16,112,256]{2,1,0:T(8,128)(2,1)} custom-call(s32[3]{0:T(128)S(1)} %pad_add_fusion.at_ref, bf16[4,2,32,512]{3,2,1,0:T(8,128)(2,1)S(1)} %bitcast.16, bf16[688,256]{1,0:T(8,128)(2,1)S(1)} %collective-permute-done.up_ref, bf16[688,256]{1,0:T(8,128)(2,1)S(1)} %collective-permute-done.1.down0_ref, ...), custom_call_target="tpu_custom_call" | custom-call | flops 65536 | bytes 65536 | tf_op jit(solution)/shard_map/pallas_call | solution.py:277
  44.8 8.1 %all-to-all-start.1 = ((bf16[16,112,256]{2,1,0:T(8,128)(2,1)}), bf16[16,112,256]{2,1,0:T(8,128)(2,1)S(1)}, u32[]{:S(2)}, u32[]{:S(2)}) async-start(bf16[16,112,256]{2,1,0:T(8,128)(2,1)} %shard_map.92), calls=%async_computation.1 | async-start | bytes 1835008 | tf_op jit(solution)/shard_map/all_to_all | solution.py:320
  52.9 0.0 collective-permute-done.4.refs_2_
  52.9 4.9 %collective-permute-start.5 = (bf16[2,27,16,256]{3,2,1,0:T(8,128)(2,1)S(1)}, bf16[2,27,16,256]{3,2,1,0:T(8,128)(2,1)S(1)}, u32[]{:S(2)}, u32[]{:S(2)}) collective-permute-start(bf16[2,27,16,256]{3,2,1,0:T(8,128)(2,1)S(1)} %collective-permute-done.3.refs_1_), channel_id=1, source_target_pairs={{0,4},{1,5},{2,6},{3,7},{4,8},{5,9},{6,10},{7,11},{8,12},{9,13},{1... | collective-permute-start | bytes 1327112 | tf_op jit(solution)/shard_map/ppermute | solution.py:247
  57.7 3.6 %collective-permute-start.6 = (bf16[2,27,16,256]{3,2,1,0:T(8,128)(2,1)S(1)}, bf16[2,27,16,256]{3,2,1,0:T(8,128)(2,1)S(1)}, u32[]{:S(2)}, u32[]{:S(2)}) collective-permute-start(bf16[2,27,16,256]{3,2,1,0:T(8,128)(2,1)S(1)} %collective-permute-done.4.refs_2_), channel_id=1, source_target_pairs={{0,4},{1,5},{2,6},{3,7},{4,8},{5,9},{6,10},{7,11},{8,12},{9,13},{1... | collective-permute-start | bytes 1327112 | tf_op jit(solution)/shard_map/ppermute | solution.py:247
  61.4 1.6 %collective-permute-done.5.refs_3_ = bf16[2,27,16,256]{3,2,1,0:T(8,128)(2,1)S(1)} collective-permute-done((bf16[2,27,16,256]{3,2,1,0:T(8,128)(2,1)S(1)}, bf16[2,27,16,256]{3,2,1,0:T(8,128)(2,1)S(1)}, u32[]{:S(2)}, u32[]{:S(2)}) %collective-permute-start.5) | collective-permute-done | bytes 442400 | tf_op jit(solution)/shard_map/ppermute | solution.py:247
  63.0 5.3 %collective-permute-start.7 = (bf16[2,27,16,256]{3,2,1,0:T(8,128)(2,1)S(1)}, bf16[2,27,16,256]{3,2,1,0:T(8,128)(2,1)}, u32[]{:S(2)}, u32[]{:S(2)}) collective-permute-start(bf16[2,27,16,256]{3,2,1,0:T(8,128)(2,1)S(1)} %collective-permute-done.5.refs_3_), channel_id=1, source_target_pairs={{0,4},{1,5},{2,6},{3,7},{4,8},{5,9},{6,10},{7,11},{8,12},{9,13},{1... | collective-permute-start | bytes 1327112 | tf_op jit(solution)/shard_map/ppermute | solution.py:247
  68.3 4.7 %collective-permute-start.8 = (bf16[2,27,16,256]{3,2,1,0:T(8,128)(2,1)S(1)}, bf16[2,27,16,256]{3,2,1,0:T(8,128)(2,1)}, u32[]{:S(2)}, u32[]{:S(2)}) collective-permute-start(bf16[2,27,16,256]{3,2,1,0:T(8,128)(2,1)S(1)} %collective-permute-done.6.refs_4_), channel_id=1, source_target_pairs={{0,4},{1,5},{2,6},{3,7},{4,8},{5,9},{6,10},{7,11},{8,12},{9,13},{1... | collective-permute-start | bytes 1327112 | tf_op jit(solution)/shard_map/ppermute | solution.py:247
  73.0 0.5 collective-permute-done.7.refs_5_
  73.5 5.2 %collective-permute-start.9 = (bf16[2,27,16,256]{3,2,1,0:T(8,128)(2,1)}, bf16[2,27,16,256]{3,2,1,0:T(8,128)(2,1)}, u32[]{:S(2)}, u32[]{:S(2)}) collective-permute-start(bf16[2,27,16,256]{3,2,1,0:T(8,128)(2,1)} %collective-permute-done.7.refs_5_), channel_id=1, source_target_pairs={{0,4},{1,5},{2,6},{3,7},{4,8},{5,9},{6,10},{7,11},{8,12},{9,13},{1... | collective-permute-start | bytes 1327112 | tf_op jit(solution)/shard_map/ppermute | solution.py:247
  78.7 3.0 %shard_map.93.act_ref = bf16[3,4,6,64,256]{4,3,2,1,0:T(8,128)(2,1)S(1)} custom-call(s32[3]{0:T(128)S(1)} %pad_add_fusion.at_ref, s32[10]{0:T(128)S(1)} %copy-done.7, f32[1,512]{1,0:T(1,128)S(1)} %bitcast.17, f32[1,512]{1,0:T(1,128)S(1)} %bitcast.18, f32[1,512]{1,0:T(1,128)S(1)} %bitcast.19, bf16[16,112,256]{2,1,0:T(8,128)(2,1)S(1)} %all-to-all-done.1.x_ref), custom_call_target="tpu_custom_call" | custom-call | flops 65536 | bytes 65536 | tf_op jit(solution)/shard_map/pallas_call | solution.py:284
  81.8 2.4 %collective-permute-done.9.refs_7_ = bf16[2,27,16,256]{3,2,1,0:T(8,128)(2,1)} collective-permute-done((bf16[2,27,16,256]{3,2,1,0:T(8,128)(2,1)}, bf16[2,27,16,256]{3,2,1,0:T(8,128)(2,1)}, u32[]{:S(2)}, u32[]{:S(2)}) %collective-permute-start.9) | collective-permute-done | bytes 442400 | tf_op jit(solution)/shard_map/ppermute | solution.py:247
  84.2 2.4 %shard_map.95 = f32[2,2,64,256]{3,2,1,0:T(8,128)S(1)} custom-call(s32[3]{0:T(128)S(1)} %pad_add_fusion.at_ref, bf16[3,4,6,64,256]{4,3,2,1,0:T(8,128)(2,1)S(1)} %shard_map.93.act_ref, bf16[2,27,16,256]{3,2,1,0:T(8,128)(2,1)S(1)} %get-tuple-element.14.refs_0_, bf16[2,27,16,256]{3,2,1,0:T(8,128)(2,1)S(1)} %collective-permute-done.3.refs_1_, ...), custom_call_target="tpu_custom_call" | custom-call | flops 1073741824 | bytes 65536 | tf_op jit(solution)/shard_map/pallas_call | solution.py:328
  86.6 0.0 copy-start.4
  86.6 0.0 copy-start.5
  86.6 0.0 copy-start.6
  86.6 8.1 %collective-permute-start.10 = (f32[2,2,64,256]{3,2,1,0:T(8,128)S(1)}, f32[2,2,64,256]{3,2,1,0:T(8,128)S(1)}, u32[]{:S(2)}, u32[]{:S(2)}) collective-permute-start(f32[2,2,64,256]{3,2,1,0:T(8,128)S(1)} %shard_map.95), channel_id=1, source_target_pairs={{0,32},{1,33},{2,34},{3,35},{4,36},{5,37},{6,38},{7,39},{8,40},{9,... | collective-permute-start | bytes 786440 | tf_op jit(solution)/shard_map/ppermute | solution.py:247
  94.8 2.4 %shard_map.94.a_ref = f32[2,2,64,256]{3,2,1,0:T(8,128)S(1)} custom-call(s32[3]{0:T(128)S(1)} %pad_add_fusion.at_ref, bf16[3,4,6,64,256]{4,3,2,1,0:T(8,128)(2,1)S(1)} %shard_map.93.act_ref, bf16[2,27,16,256]{3,2,1,0:T(8,128)(2,1)S(1)} %get-tuple-element.14.refs_0_, bf16[2,27,16,256]{3,2,1,0:T(8,128)(2,1)S(1)} %collective-permute-done.3.refs_1_, ...), custom_call_target="tpu_custom_call" | custom-call | flops 1073741824 | bytes 65536 | tf_op jit(solution)/shard_map/pallas_call | solution.py:328
  97.2 0.2 shard_map.96
  97.4 0.7 reshape.7
  (22 shorter events, 0.1 us)
Async XLA Ops:
  0.0 42.6 %copy-start = (bf16[1,4,2,32,512]{4,3,2,1,0:T(8,128)(2,1)S(1)}, bf16[1,4,2,32,512]{4,3,2,1,0:T(8,128)(2,1)}, u32[]{:S(2)}) copy-start(bf16[1,4,2,32,512]{4,3,2,1,0:T(8,128)(2,1)} %param.9) | copy-start | bytes 786436
  3.2 24.6 %collective-permute-start.2 = (bf16[688,256]{1,0:T(8,128)(2,1)}, bf16[688,256]{1,0:T(8,128)(2,1)S(1)}, u32[]{:S(2)}, u32[]{:S(2)}) collective-permute-start(bf16[688,256]{1,0:T(8,128)(2,1)} %get-tuple-element.10), channel_id=1, source_target_pairs={{0,30},{1,31},{2,0},{3,1},{4,2},{5,3},{6,4},{7,5},{8,6},{9,7},{10,... | collective-permute-start | bytes 1056776 | tf_op jit(solution)/shard_map/ppermute | solution.py:247
  16.9 17.5 %collective-permute-start = (bf16[688,256]{1,0:T(8,128)(2,1)}, bf16[688,256]{1,0:T(8,128)(2,1)S(1)}, u32[]{:S(2)}, u32[]{:S(2)}) collective-permute-start(bf16[688,256]{1,0:T(8,128)(2,1)} %get-tuple-element.9), channel_id=1, source_target_pairs={{0,1},{1,2},{2,3},{3,4},{4,5},{5,6},{6,7},{7,8},{8,9},{9,10},{10,1... | collective-permute-start | bytes 1056776 | tf_op jit(solution)/shard_map/ppermute | solution.py:247
  18.9 15.6 %collective-permute-start.1 = (bf16[688,256]{1,0:T(8,128)(2,1)}, bf16[688,256]{1,0:T(8,128)(2,1)S(1)}, u32[]{:S(2)}, u32[]{:S(2)}) collective-permute-start(bf16[688,256]{1,0:T(8,128)(2,1)} %get-tuple-element.10), channel_id=1, source_target_pairs={{0,31},{1,0},{2,1},{3,2},{4,3},{5,4},{6,5},{7,6},{8,7},{9,8},{10,9... | collective-permute-start | bytes 1056776 | tf_op jit(solution)/shard_map/ppermute | solution.py:247
  22.5 20.1 %all-to-all-start = ((f32[32,8,128]{2,1,0:T(8,128)}), f32[32,8,128]{2,1,0:T(8,128)S(1)}, u32[]{:S(2)}, u32[]{:S(2)}) async-start(f32[32,8,128]{2,1,0:T(8,128)} %get-tuple-element.11), calls=%async_computation | async-start | bytes 262144 | tf_op jit(solution)/shard_map/all_to_all | solution.py:315
  36.4 42.3 %copy-start.1 = (f32[512]{0:T(512)S(1)}, f32[512]{0:T(512)}, u32[]{:S(2)}) copy-start(f32[512]{0:T(512)} %param.10) | copy-start | bytes 6148
  36.4 42.3 %copy-start.2 = (f32[512]{0:T(512)S(1)}, f32[512]{0:T(512)}, u32[]{:S(2)}) copy-start(f32[512]{0:T(512)} %param.11) | copy-start | bytes 6148
  36.4 42.3 %copy-start.3 = (f32[512]{0:T(512)S(1)}, f32[512]{0:T(512)}, u32[]{:S(2)}) copy-start(f32[512]{0:T(512)} %param.12) | copy-start | bytes 6148
  36.4 42.3 %copy-start.7 = (s32[10]{0:T(128)S(1)}, s32[10]{0:T(128)}, u32[]{:S(2)}) copy-start(s32[10]{0:T(128)} %lengths_ref.1) | copy-start | bytes 124
  36.4 16.5 %collective-permute-start.3 = (bf16[2,27,16,256]{3,2,1,0:T(8,128)(2,1)S(1)}, bf16[2,27,16,256]{3,2,1,0:T(8,128)(2,1)S(1)}, u32[]{:S(2)}, u32[]{:S(2)}) collective-permute-start(bf16[2,27,16,256]{3,2,1,0:T(8,128)(2,1)S(1)} %get-tuple-element.14.refs_0_), channel_id=1, source_target_pairs={{0,4},{1,5},{2,6},{3,7},{4,8},{5,9},{6,10},{7,11},{8,12},{9,13},{1... | collective-permute-start | bytes 1327112 | tf_op jit(solution)/shard_map/ppermute | solution.py:247
  40.5 12.3 %collective-permute-start.4 = (bf16[2,27,16,256]{3,2,1,0:T(8,128)(2,1)}, bf16[2,27,16,256]{3,2,1,0:T(8,128)(2,1)S(1)}, u32[]{:S(2)}, u32[]{:S(2)}) collective-permute-start(bf16[2,27,16,256]{3,2,1,0:T(8,128)(2,1)} %get-tuple-element.13), channel_id=1, source_target_pairs={{0,4},{1,5},{2,6},{3,7},{4,8},{5,9},{6,10},{7,11},{8,12},{9,13},{1... | collective-permute-start | bytes 1327112 | tf_op jit(solution)/shard_map/ppermute | solution.py:247
  44.8 33.9 %all-to-all-start.1 = ((bf16[16,112,256]{2,1,0:T(8,128)(2,1)}), bf16[16,112,256]{2,1,0:T(8,128)(2,1)S(1)}, u32[]{:S(2)}, u32[]{:S(2)}) async-start(bf16[16,112,256]{2,1,0:T(8,128)(2,1)} %shard_map.92), calls=%async_computation.1 | async-start | bytes 1835008 | tf_op jit(solution)/shard_map/all_to_all | solution.py:320
  52.9 10.1 %collective-permute-start.5 = (bf16[2,27,16,256]{3,2,1,0:T(8,128)(2,1)S(1)}, bf16[2,27,16,256]{3,2,1,0:T(8,128)(2,1)S(1)}, u32[]{:S(2)}, u32[]{:S(2)}) collective-permute-start(bf16[2,27,16,256]{3,2,1,0:T(8,128)(2,1)S(1)} %collective-permute-done.3.refs_1_), channel_id=1, source_target_pairs={{0,4},{1,5},{2,6},{3,7},{4,8},{5,9},{6,10},{7,11},{8,12},{9,13},{1... | collective-permute-start | bytes 1327112 | tf_op jit(solution)/shard_map/ppermute | solution.py:247
  57.7 10.5 %collective-permute-start.6 = (bf16[2,27,16,256]{3,2,1,0:T(8,128)(2,1)S(1)}, bf16[2,27,16,256]{3,2,1,0:T(8,128)(2,1)S(1)}, u32[]{:S(2)}, u32[]{:S(2)}) collective-permute-start(bf16[2,27,16,256]{3,2,1,0:T(8,128)(2,1)S(1)} %collective-permute-done.4.refs_2_), channel_id=1, source_target_pairs={{0,4},{1,5},{2,6},{3,7},{4,8},{5,9},{6,10},{7,11},{8,12},{9,13},{1... | collective-permute-start | bytes 1327112 | tf_op jit(solution)/shard_map/ppermute | solution.py:247
  63.0 10.5 %collective-permute-start.7 = (bf16[2,27,16,256]{3,2,1,0:T(8,128)(2,1)S(1)}, bf16[2,27,16,256]{3,2,1,0:T(8,128)(2,1)}, u32[]{:S(2)}, u32[]{:S(2)}) collective-permute-start(bf16[2,27,16,256]{3,2,1,0:T(8,128)(2,1)S(1)} %collective-permute-done.5.refs_3_), channel_id=1, source_target_pairs={{0,4},{1,5},{2,6},{3,7},{4,8},{5,9},{6,10},{7,11},{8,12},{9,13},{1... | collective-permute-start | bytes 1327112 | tf_op jit(solution)/shard_map/ppermute | solution.py:247
  68.3 13.5 %collective-permute-start.8 = (bf16[2,27,16,256]{3,2,1,0:T(8,128)(2,1)S(1)}, bf16[2,27,16,256]{3,2,1,0:T(8,128)(2,1)}, u32[]{:S(2)}, u32[]{:S(2)}) collective-permute-start(bf16[2,27,16,256]{3,2,1,0:T(8,128)(2,1)S(1)} %collective-permute-done.6.refs_4_), channel_id=1, source_target_pairs={{0,4},{1,5},{2,6},{3,7},{4,8},{5,9},{6,10},{7,11},{8,12},{9,13},{1... | collective-permute-start | bytes 1327112 | tf_op jit(solution)/shard_map/ppermute | solution.py:247
  73.5 10.7 %collective-permute-start.9 = (bf16[2,27,16,256]{3,2,1,0:T(8,128)(2,1)}, bf16[2,27,16,256]{3,2,1,0:T(8,128)(2,1)}, u32[]{:S(2)}, u32[]{:S(2)}) collective-permute-start(bf16[2,27,16,256]{3,2,1,0:T(8,128)(2,1)} %collective-permute-done.7.refs_5_), channel_id=1, source_target_pairs={{0,4},{1,5},{2,6},{3,7},{4,8},{5,9},{6,10},{7,11},{8,12},{9,13},{1... | collective-permute-start | bytes 1327112 | tf_op jit(solution)/shard_map/ppermute | solution.py:247
  86.6 10.6 %copy-start.4 = (f32[256]{0:T(256)S(1)}, f32[256]{0:T(256)}, u32[]{:S(2)}) copy-start(f32[256]{0:T(256)} %param.14) | copy-start | bytes 3076
  86.6 10.6 %copy-start.5 = (f32[256]{0:T(256)S(1)}, f32[256]{0:T(256)}, u32[]{:S(2)}) copy-start(f32[256]{0:T(256)} %param.15) | copy-start | bytes 3076
  86.6 10.6 %copy-start.6 = (s32[64]{0:T(128)S(1)}, s32[64]{0:T(128)}, u32[]{:S(2)}) copy-start(s32[64]{0:T(128)} %param.17) | copy-start | bytes 772
  86.6 10.6 %collective-permute-start.10 = (f32[2,2,64,256]{3,2,1,0:T(8,128)S(1)}, f32[2,2,64,256]{3,2,1,0:T(8,128)S(1)}, u32[]{:S(2)}, u32[]{:S(2)}) collective-permute-start(f32[2,2,64,256]{3,2,1,0:T(8,128)S(1)} %shard_map.95), channel_id=1, source_target_pairs={{0,32},{1,33},{2,34},{3,35},{4,36},{5,37},{6,38},{7,39},{8,40},{9,... | collective-permute-start | bytes 786440 | tf_op jit(solution)/shard_map/ppermute | solution.py:247

commit v4 on v3

--- a/solution.py
+++ b/solution.py
@@ -60,12 +60,11 @@
     return out[:n] + out[n + pad : 2 * n + pad] + out[2 * (n + pad) : 3 * n + 2 * pad]
 
 
-def prepare(x_hbm, w_ref, sums_ref, next_ref, prev_ref, x_ref, sem):
+def prepare(x_hbm, w_ref, sums_ref, beside_ref, edge_ref, x_ref, sem):
     loads = [pltpu.make_async_copy(x_hbm.at[f], x_ref.at[f], sem.at[f]) for f in range(FR)]
     for copy in loads:
         copy.start()
-    for out_ref in (next_ref, prev_ref):
-        out_ref[:SHARD] = w_ref[...].reshape(SHARD, CO)
+    beside_ref[:SHARD] = w_ref[...].reshape(SHARD, CO)
     to_groups, to_channels = group_of((C, 128), 0, 1), group_of((128, C), 1, 0)
     rows = []
     for f in range(FR):
@@ -79,10 +78,11 @@
         d = rows[f] - spread[f : f + 1]
         squares.append(jnp.sum(d * d, axis=0, keepdims=True))
     squares = take(jnp.concatenate(squares, axis=0), to_groups)
-    for out_ref, row in ((next_ref, 1), (prev_ref, 0)):
-        edge = x_ref[:, row].reshape(EDGE, C)
-        out_ref[SHARD : SHARD + EDGE] = edge[:, :HALF]
-        out_ref[SHARD + EDGE :] = edge[:, HALF:]
+    core = lax.axis_index("core")
+    edge = x_ref[:, core].reshape(EDGE, C)
+    beside_ref[SHARD : SHARD + EDGE] = edge[:, :HALF]
+    beside_ref[SHARD + EDGE :] = edge[:, HALF:]
+    edge_ref[...] = x_ref[:, 1 - core].reshape(EDGE, C)
     sums_ref[...] = jnp.broadcast_to(jnp.concatenate([mean, squares], axis=0)[None], sums_ref.shape)
 
 
@@ -97,19 +97,18 @@
 def channel_at(s, core, place):
     step = (place + 2 * GW) >> 6
     nth = jnp.where(step == 0, place >> 4, ((place >> 4) + 2) & 3)
-    away = jnp.where(core == 0, jnp.where(nth == 2, -1, jnp.where(nth == 3, 2, nth)), jnp.where(nth == 0, 2, nth - 2))
+    nth = (nth + 2 * core) & 3
+    away = jnp.where(nth == 3, -1, nth)
     away = away + NX * jnp.where(core == 0, -step, step)
     return (((s + away) & (NZ * NX - 1)) << 4) + (place & 15)
 
 
-def pack(at_ref, own_ref, up_ref, down0_ref, down1_ref, sums_ref, out_ref):
-    s = at_ref[2]
-
-    def edge(ref):
-        return jnp.concatenate([ref[SHARD : SHARD + EDGE], ref[SHARD + EDGE :]], axis=1)
-
-    down = jnp.where(at_ref[1] == 0, edge(down0_ref), edge(down1_ref))
-    source = jnp.concatenate([edge(up_ref), own_ref[...].reshape(2 * EDGE, C), down], axis=0)
+def pack(own_ref, beside_ref, edge_ref, sums_ref, out_ref):
+    core, s = lax.axis_index("core"), lax.axis_index("z") * NX + lax.axis_index("x")
+    beside = jnp.concatenate([beside_ref[SHARD : SHARD + EDGE], beside_ref[SHARD + EDGE :]], axis=1)
+    edge, first = edge_ref[...], core == 0
+    up, down = jnp.where(first, edge, beside), jnp.where(first, beside, edge)
+    source = jnp.concatenate([up, own_ref[...].reshape(2 * EDGE, C), down], axis=0)
     n = 4 * FR * W
     to = iota((n, 1), 0)
     col, row, frame = to >> 4, (to >> 2) & 3, to & 3
@@ -148,8 +147,8 @@
     return start
 
 
-def activate(at_ref, lengths_ref, gamma_ref, beta_ref, smooth_ref, x_ref, act_ref):
-    y, core, s = at_ref[0], at_ref[1], at_ref[2]
+def activate(lengths_ref, gamma_ref, beta_ref, smooth_ref, x_ref, act_ref):
+    y, core, s = lax.axis_index("y"), lax.axis_index("core"), lax.axis_index("z") * NX + lax.axis_index("x")
     n = 2 * T
     thirds = x_ref[:, 96:112, :].astype(F32)[:, :8, :128].reshape(n, 128)
     rows, columns = iota((n, 1), 0), iota((1, n), 1)
@@ -212,9 +211,9 @@
             act_ref[1, r, c] = e[T:]
 
 
-def convolve(own_columns, at_ref, act_ref, *refs):
+def convolve(own_columns, act_ref, *refs):
     weights, out_ref = refs[:-1], refs[-1]
-    core = at_ref[1]
+    core = lax.axis_index("core")
     column = 2 * core if own_columns else 2 - 2 * core
     total = None
     for tap in range(27):
@@ -263,26 +262,28 @@
     return pl.CostEstimate(flops=flops, bytes_accessed=size, transcendentals=0)
 
 
-def call_prepare(latent, weights):
-    beside = struct((SHARD + 2 * EDGE, CO), BF16)
+def call_prepare(*args):
     return pl.pallas_call(
-        prepare, out_shape=(struct((NZ * NX, 8, 128), F32), beside, beside), in_specs=[ANY, VMEM],
-        out_specs=(VMEM, VMEM, VMEM),
+        prepare,
+        out_shape=(
+            struct((NZ * NX, 8, 128), F32), struct((SHARD + 2 * EDGE, CO), BF16), struct((EDGE, C), BF16)
+        ),
+        in_specs=[ANY, VMEM], out_specs=(VMEM, VMEM, VMEM),
         scratch_shapes=[pltpu.VMEM((FR, 2, W, C), BF16), pltpu.SemaphoreType.DMA((FR,))],
         compiler_params=params(60), cost_estimate=cost(2**16, 2**16),
-    )(latent, weights)
+    )(*args)
 
 
 def call_pack(*args):
     return pl.pallas_call(
-        pack, out_shape=struct((SLABS, 112, HALF), BF16), in_specs=[SMEM] + [VMEM] * 5, out_specs=VMEM,
+        pack, out_shape=struct((SLABS, 112, HALF), BF16), in_specs=[VMEM] * 4, out_specs=VMEM,
         compiler_params=params(), cost_estimate=cost(2**16, 2**16),
     )(*args)
 
 
 def call_activate(*args):
     return pl.pallas_call(
-        activate, out_shape=struct((3, 4, 6, T, HALF), BF16), in_specs=[SMEM, SMEM] + [VMEM] * 4, out_specs=VMEM,
+        activate, out_shape=struct((3, 4, 6, T, HALF), BF16), in_specs=[SMEM] + [VMEM] * 4, out_specs=VMEM,
         compiler_params=params(), cost_estimate=cost(2**16, 2**16),
     )(*args)
 
@@ -295,42 +296,46 @@
 
 
 def local(latent, gamma, beta, smooth, weights, w_scale, bias, lengths, order):
-    y, core, z, x = (lax.axis_index(a) for a in AXES)
-    at = jnp.stack([y, core, z * NX + x]).astype(jnp.int32)
+    core = lax.axis_index("core")
     latent = latent[0]
     weights = weights.reshape(27, GW, CO)
 
-    spread, to_next, to_prev = call_prepare(latent, weights)
+    spread, to_beside, edge = call_prepare(latent, weights)
 
     def ring(v):
         return shift(v, lambda y, core, z, x: (y, core, z + 1 - 2 * core, x))
 
     def along(v, *d):
-        return shift(v, lambda y, core, z, x: by_space(y, core, (z * NX + x - d[core]) % (NZ * NX)))
-
-    def shard(v):
-        return v[:SHARD].reshape(27, GW, CO)
-
-    n1, n2, n3 = along(to_prev, 1, 2), along(to_next, -1, -1), along(to_prev, 2, 1)
+        def step(y, core, z, x):
+            return None if d[core] is None else by_space(y, core, (z * NX + x - d[core]) % (NZ * NX))
+
+        return shift(v, step)
+
+    def other_core(v):
+        return shift(v, lambda y, core, z, x: (y, 1 - core, z, x))
+
+    beside, second = along(to_beside, 1, -1), along(weights, None, 2)
     gathered = lax.all_to_all(spread, ("z", "x"), 0, 0, tiled=True)
-    a0 = jnp.where(core == 0, jnp.stack([weights, shard(n1)]), jnp.stack([shard(n1), shard(n2)]))
-    b0 = jnp.where(core == 0, jnp.stack([shard(n2), shard(n3)]), jnp.stack([weights, shard(n3)]))
+    edge = along(edge, -1, 1)
+    near = beside[:SHARD].reshape(27, GW, CO)
+    a0 = jnp.where(core == 0, jnp.stack([weights, near]), jnp.stack([second, near]))
+    b0 = other_core(a0)
     a1, b1 = ring(a0), ring(b0)
-    windows = call_pack(at, latent, n2, n1, n3, gathered)
+    windows = call_pack(latent, beside, edge, gathered)
     columns = lax.all_to_all(windows, ("y", "core"), 0, 0, tiled=True)
-    a2, b2 = ring(lax.optimization_barrier((a1, b1))[0]), ring(b1)
+    a2, b2 = ring(a1), ring(b1)
     a3, b3 = ring(a2), ring(b2)
-    act = call_activate(at, lengths, gamma[None], beta[None], smooth[None], columns)
+    act = call_activate(lengths, gamma[None], beta[None], smooth[None], columns)
     a4 = ring(a3)
 
 
     def part(own_columns):
         return pl.pallas_call(
             functools.partial(convolve, own_columns), out_shape=struct((2, 2, T, CO), F32),
-            in_specs=[SMEM] + [VMEM] * 9, out_specs=VMEM, compiler_params=params(32), cost_estimate=cost(2**30, 2**16),
-        )(at, act, a0, a1, b1, a2, b2, a3, b3, a4)
-
-    other = shift(part(False), lambda y, core, z, x: (y, 1 - core, z, x))
+            in_specs=[VMEM] * 9, out_specs=VMEM, compiler_params=params(32), cost_estimate=cost(2**30, 2**16),
+        )(act, a0, a1, b1, a2, b2, a3, b3, a4)
+
+    other = other_core(part(False))
     keep = part(True)
     out = call_finish(order[None], w_scale[None], bias[None], keep, other)
     return out.reshape(SLABS, FR, 2, 2, CO)

time: 98.9 us -> 93.5 us (0.945)
  waiting for transfers between devices: 11.1 us -> 6.15 us
  starting transfers between devices: 70.5 us -> 71.6 us
    ppermute x11 -> x12, waiting for transfers between devices: 11.1 us -> 6.15 us  [shift(): return lax.ppermute(value, AXES, pairs)]
    ppermute x11 -> x12, starting transfers between devices: 57.1 us -> 60.5 us  [shift(): return lax.ppermute(value, AXES, pairs)]
    all_to_all x1, starting transfers between devices: 5.31 us -> 3.87 us  [local(): gathered = lax.all_to_all(spread, ('z', 'x'), 0, 0, tiled=True)]
  transfers between devices with their start and end apart: 13 -> 14, of which waited for: 4 -> 3; matrix products, arithmetic and copies ran while one was open for 2% -> 1% of each run, Pallas kernels for 8% -> 8%
where the time goes in v4:
time: 93.5 us; the launch traced here: 92.8 us
  starting transfers between devices  71.6 us (77%)
  Pallas kernels  12.8 us (14%)
  waiting for transfers between devices  6.15 us (7%)
  other arithmetic  1.01 us (1%)
    ppermute x12, starting transfers between devices, shift(): return lax.ppermute(value, AXES, pairs)  60.5 us
    all_to_all x1, starting transfers between devices, local(): columns = lax.all_to_all(windows, ('y', 'core'), 0, 0, tiled=True)  7.23 us
    ppermute x12, waiting for transfers between devices, shift(): return lax.ppermute(value, AXES, pairs)  6.15 us
    pallas_call x2, Pallas kernels, part(): pl.pallas_call(functools.partial(convolve, own_columns), out_shape=struct...  4.73 us
    all_to_all x1, starting transfers between devices, local(): gathered = lax.all_to_all(spread, ('z', 'x'), 0, 0, tiled=True)  3.87 us
    pallas_call x1, Pallas kernels, call_prepare(): pl.pallas_call(prepare, out_shape=(struct((NZ * NX, 8, 128), F32), struct...  3.14 us
    pallas_call x1, Pallas kernels, call_activate(): pl.pallas_call(activate, out_shape=struct((3, 4, 6, T, HALF), BF16), in_s...  3.03 us
  transfers between devices with their start and end apart: 14, of which 3 were waited for; matrix products, arithmetic and copies ran while one was open for 1% of the time, Pallas kernels for 8%

profile of v4, /device:TPU:1, one launch (start us, length us, event | category | flops | bytes accessed | tf_op | source)
XLA Modules:
  0.0 92.8 jit_solution(14007077308722880501)
XLA Ops:
  0.0 3.1 %shard_map.91 = (f32[32,8,128]{2,1,0:T(8,128)}, bf16[688,256]{1,0:T(8,128)(2,1)}, bf16[128,512]{1,0:T(8,128)(2,1)}) custom-call(bf16[4,2,32,512]{3,2,1,0:T(8,128)(2,1)} %bitcast.11, bf16[27,16,256]{2,1,0:T(8,128)(2,1)} %bitcast.20), custom_call_target="tpu_custom_call" | custom-call | flops 65536 | bytes 65536 | tf_op jit(solution)/shard_map/pallas_call | solution.py:266
  3.2 3.9 %collective-permute-start = (bf16[688,256]{1,0:T(8,128)(2,1)}, bf16[688,256]{1,0:T(8,128)(2,1)S(1)}, u32[]{:S(2)}, u32[]{:S(2)}) collective-permute-start(bf16[688,256]{1,0:T(8,128)(2,1)} %get-tuple-element.8), channel_id=1, source_target_pairs={{0,31},{1,0},{2,1},{3,2},{4,3},{5,4},{6,5},{7,6},{8,7},{9,8},{10,9... | collective-permute-start | bytes 1056776 | tf_op jit(solution)/shard_map/ppermute | solution.py:246
  7.1 12.8 %collective-permute-start.2 = (bf16[27,16,256]{2,1,0:T(8,128)(2,1)}, bf16[27,16,256]{2,1,0:T(8,128)(2,1)S(1)}, u32[]{:S(2)}, u32[]{:S(2)}) collective-permute-start(bf16[27,16,256]{2,1,0:T(8,128)(2,1)} %bitcast.21), channel_id=1, source_target_pairs={{32,62},{33,63},{34,32},{35,33},{36,34},{37,35},{38,36},{39,37},{4... | collective-permute-start | bytes 663560 | tf_op jit(solution)/shard_map/ppermute | solution.py:246
  20.0 3.9 %all-to-all-start = ((f32[32,8,128]{2,1,0:T(8,128)}), f32[32,8,128]{2,1,0:T(8,128)S(1)}, u32[]{:S(2)}, u32[]{:S(2)}) async-start(f32[32,8,128]{2,1,0:T(8,128)} %get-tuple-element.10), calls=%async_computation | async-start | bytes 262144 | tf_op jit(solution)/shard_map/all_to_all | solution.py:318
  23.8 6.6 %collective-permute-start.1 = (bf16[128,512]{1,0:T(8,128)(2,1)}, bf16[128,512]{1,0:T(8,128)(2,1)S(1)}, u32[]{:S(2)}, u32[]{:S(2)}) collective-permute-start(bf16[128,512]{1,0:T(8,128)(2,1)} %get-tuple-element.9), channel_id=1, source_target_pairs={{0,1},{1,2},{2,3},{3,4},{4,5},{5,6},{6,7},{7,8},{8,9},{9,10},{10,1... | collective-permute-start | bytes 393224 | tf_op jit(solution)/shard_map/ppermute | solution.py:246
  30.4 0.0 copy-start.1
  30.5 0.0 copy-start.2
  30.5 0.0 copy-start.3
  30.5 0.0 copy-start.6
  30.5 1.0 %fusion.refs_0_ = bf16[2,27,16,256]{3,2,1,0:T(8,128)(2,1)S(1)} fusion(bf16[1,27,16,256]{3,2,1,0:T(8,128)(2,1)S(1)} %bitcast.19, bf16[1,27,16,256]{3,2,1,0:T(8,128)(2,1)} %bitcast.22, bf16[1,27,16,256]{3,2,1,0:T(8,128)(2,1)S(1)} %bitcast.23, pred[]{:T(512)S(6)} %eq.3), kind=kLoop, calls=%fused_computation.2 | loop fusion | flops 663552 | bytes 1105921 | tf_op jit(solution)/shard_map/jit(_where)/select_n | solution.py:321
  31.5 1.9 %collective-permute-start.4 = (bf16[2,27,16,256]{3,2,1,0:T(8,128)(2,1)S(1)}, bf16[2,27,16,256]{3,2,1,0:T(8,128)(2,1)S(1)}, u32[]{:S(2)}, u32[]{:S(2)}) collective-permute-start(bf16[2,27,16,256]{3,2,1,0:T(8,128)(2,1)S(1)} %fusion.refs_0_), channel_id=1, source_target_pairs={{0,32},{1,33},{2,34},{3,35},{4,36},{5,37},{6,38},{7,39},{8,40},{9,... | collective-permute-start | bytes 1327112 | tf_op jit(solution)/shard_map/ppermute | solution.py:246
  33.4 3.1 %collective-permute-start.3 = (bf16[2,27,16,256]{3,2,1,0:T(8,128)(2,1)S(1)}, bf16[2,27,16,256]{3,2,1,0:T(8,128)(2,1)S(1)}, u32[]{:S(2)}, u32[]{:S(2)}) collective-permute-start(bf16[2,27,16,256]{3,2,1,0:T(8,128)(2,1)S(1)} %fusion.refs_0_), channel_id=1, source_target_pairs={{0,4},{1,5},{2,6},{3,7},{4,8},{5,9},{6,10},{7,11},{8,12},{9,13},{1... | collective-permute-start | bytes 1327112 | tf_op jit(solution)/shard_map/ppermute | solution.py:246
  36.5 1.7 %shard_map.92 = bf16[16,112,256]{2,1,0:T(8,128)(2,1)} custom-call(bf16[4,2,32,512]{3,2,1,0:T(8,128)(2,1)S(1)} %bitcast.12, bf16[688,256]{1,0:T(8,128)(2,1)S(1)} %collective-permute-done.beside_ref, bf16[128,512]{1,0:T(8,128)(2,1)S(1)} %collective-permute-done.1.edge_ref, f32[32,8,128]{2,1,0:T(8,128)S(1)} %all-to-all-done.sums_ref), custom_call_target="tpu_custom_call" | custom-call | flops 65536 | bytes 65536 | tf_op jit(solution)/shard_map/pallas_call | solution.py:278
  38.3 7.2 %all-to-all-start.1 = ((bf16[16,112,256]{2,1,0:T(8,128)(2,1)}), bf16[16,112,256]{2,1,0:T(8,128)(2,1)S(1)}, u32[]{:S(2)}, u32[]{:S(2)}) async-start(bf16[16,112,256]{2,1,0:T(8,128)(2,1)} %shard_map.92), calls=%async_computation.1 | async-start | bytes 1835008 | tf_op jit(solution)/shard_map/all_to_all | solution.py:325
  45.5 4.1 %collective-permute-start.5 = (bf16[2,27,16,256]{3,2,1,0:T(8,128)(2,1)S(1)}, bf16[2,27,16,256]{3,2,1,0:T(8,128)(2,1)S(1)}, u32[]{:S(2)}, u32[]{:S(2)}) collective-permute-start(bf16[2,27,16,256]{3,2,1,0:T(8,128)(2,1)S(1)} %collective-permute-done.4), channel_id=1, source_target_pairs={{0,4},{1,5},{2,6},{3,7},{4,8},{5,9},{6,10},{7,11},{8,12},{9,13},{1... | collective-permute-start | bytes 1327112 | tf_op jit(solution)/shard_map/ppermute | solution.py:246
  49.6 2.0 %collective-permute-start.6 = (bf16[2,27,16,256]{3,2,1,0:T(8,128)(2,1)S(1)}, bf16[2,27,16,256]{3,2,1,0:T(8,128)(2,1)S(1)}, u32[]{:S(2)}, u32[]{:S(2)}) collective-permute-start(bf16[2,27,16,256]{3,2,1,0:T(8,128)(2,1)S(1)} %collective-permute-done.3.refs_1_), channel_id=1, source_target_pairs={{0,4},{1,5},{2,6},{3,7},{4,8},{5,9},{6,10},{7,11},{8,12},{9,13},{1... | collective-permute-start | bytes 1327112 | tf_op jit(solution)/shard_map/ppermute | solution.py:246
  51.6 3.2 %collective-permute-done.5.refs_2_ = bf16[2,27,16,256]{3,2,1,0:T(8,128)(2,1)S(1)} collective-permute-done((bf16[2,27,16,256]{3,2,1,0:T(8,128)(2,1)S(1)}, bf16[2,27,16,256]{3,2,1,0:T(8,128)(2,1)S(1)}, u32[]{:S(2)}, u32[]{:S(2)}) %collective-permute-start.5) | collective-permute-done | bytes 442400 | tf_op jit(solution)/shard_map/ppermute | solution.py:246
  54.8 5.3 %collective-permute-start.7 = (bf16[2,27,16,256]{3,2,1,0:T(8,128)(2,1)S(1)}, bf16[2,27,16,256]{3,2,1,0:T(8,128)(2,1)S(1)}, u32[]{:S(2)}, u32[]{:S(2)}) collective-permute-start(bf16[2,27,16,256]{3,2,1,0:T(8,128)(2,1)S(1)} %collective-permute-done.5.refs_2_), channel_id=1, source_target_pairs={{0,4},{1,5},{2,6},{3,7},{4,8},{5,9},{6,10},{7,11},{8,12},{9,13},{1... | collective-permute-start | bytes 1327112 | tf_op jit(solution)/shard_map/ppermute | solution.py:246
  60.1 4.7 %collective-permute-start.8 = (bf16[2,27,16,256]{3,2,1,0:T(8,128)(2,1)S(1)}, bf16[2,27,16,256]{3,2,1,0:T(8,128)(2,1)}, u32[]{:S(2)}, u32[]{:S(2)}) collective-permute-start(bf16[2,27,16,256]{3,2,1,0:T(8,128)(2,1)S(1)} %collective-permute-done.6.refs_3_), channel_id=1, source_target_pairs={{0,4},{1,5},{2,6},{3,7},{4,8},{5,9},{6,10},{7,11},{8,12},{9,13},{1... | collective-permute-start | bytes 1327112 | tf_op jit(solution)/shard_map/ppermute | solution.py:246
  64.9 0.5 collective-permute-done.7.refs_4_
  65.4 5.2 %collective-permute-start.9 = (bf16[2,27,16,256]{3,2,1,0:T(8,128)(2,1)S(1)}, bf16[2,27,16,256]{3,2,1,0:T(8,128)(2,1)}, u32[]{:S(2)}, u32[]{:S(2)}) collective-permute-start(bf16[2,27,16,256]{3,2,1,0:T(8,128)(2,1)S(1)} %collective-permute-done.7.refs_4_), channel_id=1, source_target_pairs={{0,4},{1,5},{2,6},{3,7},{4,8},{5,9},{6,10},{7,11},{8,12},{9,13},{1... | collective-permute-start | bytes 1327112 | tf_op jit(solution)/shard_map/ppermute | solution.py:246
  70.5 4.7 %collective-permute-start.10 = (bf16[2,27,16,256]{3,2,1,0:T(8,128)(2,1)}, bf16[2,27,16,256]{3,2,1,0:T(8,128)(2,1)}, u32[]{:S(2)}, u32[]{:S(2)}) collective-permute-start(bf16[2,27,16,256]{3,2,1,0:T(8,128)(2,1)} %collective-permute-done.8.refs_5_), channel_id=1, source_target_pairs={{0,4},{1,5},{2,6},{3,7},{4,8},{5,9},{6,10},{7,11},{8,12},{9,13},{1... | collective-permute-start | bytes 1327112 | tf_op jit(solution)/shard_map/ppermute | solution.py:246
  75.3 3.0 %shard_map.93.act_ref = bf16[3,4,6,64,256]{4,3,2,1,0:T(8,128)(2,1)S(1)} custom-call(s32[10]{0:T(128)S(1)} %copy-done.6, f32[1,512]{1,0:T(1,128)S(1)} %bitcast.13, f32[1,512]{1,0:T(1,128)S(1)} %bitcast.14, f32[1,512]{1,0:T(1,128)S(1)} %bitcast.15, bf16[16,112,256]{2,1,0:T(8,128)(2,1)S(1)} %all-to-all-done.1.x_ref), custom_call_target="tpu_custom_call" | custom-call | flops 65536 | bytes 65536 | tf_op jit(solution)/shard_map/pallas_call | solution.py:285
  78.3 2.4 %collective-permute-done.10.refs_7_ = bf16[2,27,16,256]{3,2,1,0:T(8,128)(2,1)} collective-permute-done((bf16[2,27,16,256]{3,2,1,0:T(8,128)(2,1)}, bf16[2,27,16,256]{3,2,1,0:T(8,128)(2,1)}, u32[]{:S(2)}, u32[]{:S(2)}) %collective-permute-start.10) | collective-permute-done | bytes 442400 | tf_op jit(solution)/shard_map/ppermute | solution.py:246
  80.8 2.4 %shard_map.95 = f32[2,2,64,256]{3,2,1,0:T(8,128)S(1)} custom-call(bf16[3,4,6,64,256]{4,3,2,1,0:T(8,128)(2,1)S(1)} %shard_map.93.act_ref, bf16[2,27,16,256]{3,2,1,0:T(8,128)(2,1)S(1)} %fusion.refs_0_, bf16[2,27,16,256]{3,2,1,0:T(8,128)(2,1)S(1)} %collective-permute-done.3.refs_1_, bf16[2,27,16,256]{3,2,1,0:T(8,128)(2,1)S(1)} %collective-permute-done.5.refs_2_, ...), custom_call_target="tpu_custom_call" | custom-call | flops 1073741824 | bytes 65536 | tf_op jit(solution)/shard_map/pallas_call | solution.py:333
  83.1 0.0 copy-start.4
  83.2 0.0 copy-start.5
  83.2 0.0 copy-start.7
  83.2 6.2 %collective-permute-start.11 = (f32[2,2,64,256]{3,2,1,0:T(8,128)S(1)}, f32[2,2,64,256]{3,2,1,0:T(8,128)S(1)}, u32[]{:S(2)}, u32[]{:S(2)}) collective-permute-start(f32[2,2,64,256]{3,2,1,0:T(8,128)S(1)} %shard_map.95), channel_id=1, source_target_pairs={{0,32},{1,33},{2,34},{3,35},{4,36},{5,37},{6,38},{7,39},{8,40},{9,... | collective-permute-start | bytes 786440 | tf_op jit(solution)/shard_map/ppermute | solution.py:246
  89.4 2.4 %shard_map.94.a_ref = f32[2,2,64,256]{3,2,1,0:T(8,128)S(1)} custom-call(bf16[3,4,6,64,256]{4,3,2,1,0:T(8,128)(2,1)S(1)} %shard_map.93.act_ref, bf16[2,27,16,256]{3,2,1,0:T(8,128)(2,1)S(1)} %fusion.refs_0_, bf16[2,27,16,256]{3,2,1,0:T(8,128)(2,1)S(1)} %collective-permute-done.3.refs_1_, bf16[2,27,16,256]{3,2,1,0:T(8,128)(2,1)S(1)} %collective-permute-done.5.refs_2_, ...), custom_call_target="tpu_custom_call" | custom-call | flops 1073741824 | bytes 65536 | tf_op jit(solution)/shard_map/pallas_call | solution.py:333
  91.8 0.2 shard_map.96
  92.0 0.7 reshape.7
  (21 shorter events, 0.1 us)
Async XLA Ops:
  0.0 36.5 %copy-start = (bf16[1,4,2,32,512]{4,3,2,1,0:T(8,128)(2,1)S(1)}, bf16[1,4,2,32,512]{4,3,2,1,0:T(8,128)(2,1)}, u32[]{:S(2)}) copy-start(bf16[1,4,2,32,512]{4,3,2,1,0:T(8,128)(2,1)} %param.9) | copy-start | bytes 786436
  3.2 27.2 %collective-permute-start = (bf16[688,256]{1,0:T(8,128)(2,1)}, bf16[688,256]{1,0:T(8,128)(2,1)S(1)}, u32[]{:S(2)}, u32[]{:S(2)}) collective-permute-start(bf16[688,256]{1,0:T(8,128)(2,1)} %get-tuple-element.8), channel_id=1, source_target_pairs={{0,31},{1,0},{2,1},{3,2},{4,3},{5,4},{6,5},{7,6},{8,7},{9,8},{10,9... | collective-permute-start | bytes 1056776 | tf_op jit(solution)/shard_map/ppermute | solution.py:246
  7.1 23.3 %collective-permute-start.2 = (bf16[27,16,256]{2,1,0:T(8,128)(2,1)}, bf16[27,16,256]{2,1,0:T(8,128)(2,1)S(1)}, u32[]{:S(2)}, u32[]{:S(2)}) collective-permute-start(bf16[27,16,256]{2,1,0:T(8,128)(2,1)} %bitcast.21), channel_id=1, source_target_pairs={{32,62},{33,63},{34,32},{35,33},{36,34},{37,35},{38,36},{39,37},{4... | collective-permute-start | bytes 663560 | tf_op jit(solution)/shard_map/ppermute | solution.py:246
  20.0 16.6 %all-to-all-start = ((f32[32,8,128]{2,1,0:T(8,128)}), f32[32,8,128]{2,1,0:T(8,128)S(1)}, u32[]{:S(2)}, u32[]{:S(2)}) async-start(f32[32,8,128]{2,1,0:T(8,128)} %get-tuple-element.10), calls=%async_computation | async-start | bytes 262144 | tf_op jit(solution)/shard_map/all_to_all | solution.py:318
  23.8 12.7 %collective-permute-start.1 = (bf16[128,512]{1,0:T(8,128)(2,1)}, bf16[128,512]{1,0:T(8,128)(2,1)S(1)}, u32[]{:S(2)}, u32[]{:S(2)}) collective-permute-start(bf16[128,512]{1,0:T(8,128)(2,1)} %get-tuple-element.9), channel_id=1, source_target_pairs={{0,1},{1,2},{2,3},{3,4},{4,5},{5,6},{6,7},{7,8},{8,9},{9,10},{10,1... | collective-permute-start | bytes 393224 | tf_op jit(solution)/shard_map/ppermute | solution.py:246
  30.4 44.8 %copy-start.1 = (f32[512]{0:T(512)S(1)}, f32[512]{0:T(512)}, u32[]{:S(2)}) copy-start(f32[512]{0:T(512)} %param.10) | copy-start | bytes 6148
  30.5 44.8 %copy-start.2 = (f32[512]{0:T(512)S(1)}, f32[512]{0:T(512)}, u32[]{:S(2)}) copy-start(f32[512]{0:T(512)} %param.11) | copy-start | bytes 6148
  30.5 44.8 %copy-start.3 = (f32[512]{0:T(512)S(1)}, f32[512]{0:T(512)}, u32[]{:S(2)}) copy-start(f32[512]{0:T(512)} %param.12) | copy-start | bytes 6148
  30.5 44.8 %copy-start.6 = (s32[10]{0:T(128)S(1)}, s32[10]{0:T(128)}, u32[]{:S(2)}) copy-start(s32[10]{0:T(128)} %lengths_ref.1) | copy-start | bytes 124
  31.5 14.0 %collective-permute-start.4 = (bf16[2,27,16,256]{3,2,1,0:T(8,128)(2,1)S(1)}, bf16[2,27,16,256]{3,2,1,0:T(8,128)(2,1)S(1)}, u32[]{:S(2)}, u32[]{:S(2)}) collective-permute-start(bf16[2,27,16,256]{3,2,1,0:T(8,128)(2,1)S(1)} %fusion.refs_0_), channel_id=1, source_target_pairs={{0,32},{1,33},{2,34},{3,35},{4,36},{5,37},{6,38},{7,39},{8,40},{9,... | collective-permute-start | bytes 1327112 | tf_op jit(solution)/shard_map/ppermute | solution.py:246
  33.4 16.2 %collective-permute-start.3 = (bf16[2,27,16,256]{3,2,1,0:T(8,128)(2,1)S(1)}, bf16[2,27,16,256]{3,2,1,0:T(8,128)(2,1)S(1)}, u32[]{:S(2)}, u32[]{:S(2)}) collective-permute-start(bf16[2,27,16,256]{3,2,1,0:T(8,128)(2,1)S(1)} %fusion.refs_0_), channel_id=1, source_target_pairs={{0,4},{1,5},{2,6},{3,7},{4,8},{5,9},{6,10},{7,11},{8,12},{9,13},{1... | collective-permute-start | bytes 1327112 | tf_op jit(solution)/shard_map/ppermute | solution.py:246
  38.3 37.0 %all-to-all-start.1 = ((bf16[16,112,256]{2,1,0:T(8,128)(2,1)}), bf16[16,112,256]{2,1,0:T(8,128)(2,1)S(1)}, u32[]{:S(2)}, u32[]{:S(2)}) async-start(bf16[16,112,256]{2,1,0:T(8,128)(2,1)} %shard_map.92), calls=%async_computation.1 | async-start | bytes 1835008 | tf_op jit(solution)/shard_map/all_to_all | solution.py:325
  45.5 9.3 %collective-permute-start.5 = (bf16[2,27,16,256]{3,2,1,0:T(8,128)(2,1)S(1)}, bf16[2,27,16,256]{3,2,1,0:T(8,128)(2,1)S(1)}, u32[]{:S(2)}, u32[]{:S(2)}) collective-permute-start(bf16[2,27,16,256]{3,2,1,0:T(8,128)(2,1)S(1)} %collective-permute-done.4), channel_id=1, source_target_pairs={{0,4},{1,5},{2,6},{3,7},{4,8},{5,9},{6,10},{7,11},{8,12},{9,13},{1... | collective-permute-start | bytes 1327112 | tf_op jit(solution)/shard_map/ppermute | solution.py:246
  49.6 10.5 %collective-permute-start.6 = (bf16[2,27,16,256]{3,2,1,0:T(8,128)(2,1)S(1)}, bf16[2,27,16,256]{3,2,1,0:T(8,128)(2,1)S(1)}, u32[]{:S(2)}, u32[]{:S(2)}) collective-permute-start(bf16[2,27,16,256]{3,2,1,0:T(8,128)(2,1)S(1)} %collective-permute-done.3.refs_1_), channel_id=1, source_target_pairs={{0,4},{1,5},{2,6},{3,7},{4,8},{5,9},{6,10},{7,11},{8,12},{9,13},{1... | collective-permute-start | bytes 1327112 | tf_op jit(solution)/shard_map/ppermute | solution.py:246
  54.8 10.5 %collective-permute-start.7 = (bf16[2,27,16,256]{3,2,1,0:T(8,128)(2,1)S(1)}, bf16[2,27,16,256]{3,2,1,0:T(8,128)(2,1)S(1)}, u32[]{:S(2)}, u32[]{:S(2)}) collective-permute-start(bf16[2,27,16,256]{3,2,1,0:T(8,128)(2,1)S(1)} %collective-permute-done.5.refs_2_), channel_id=1, source_target_pairs={{0,4},{1,5},{2,6},{3,7},{4,8},{5,9},{6,10},{7,11},{8,12},{9,13},{1... | collective-permute-start | bytes 1327112 | tf_op jit(solution)/shard_map/ppermute | solution.py:246
  60.1 10.4 %collective-permute-start.8 = (bf16[2,27,16,256]{3,2,1,0:T(8,128)(2,1)S(1)}, bf16[2,27,16,256]{3,2,1,0:T(8,128)(2,1)}, u32[]{:S(2)}, u32[]{:S(2)}) collective-permute-start(bf16[2,27,16,256]{3,2,1,0:T(8,128)(2,1)S(1)} %collective-permute-done.6.refs_3_), channel_id=1, source_target_pairs={{0,4},{1,5},{2,6},{3,7},{4,8},{5,9},{6,10},{7,11},{8,12},{9,13},{1... | collective-permute-start | bytes 1327112 | tf_op jit(solution)/shard_map/ppermute | solution.py:246
  65.4 13.0 %collective-permute-start.9 = (bf16[2,27,16,256]{3,2,1,0:T(8,128)(2,1)S(1)}, bf16[2,27,16,256]{3,2,1,0:T(8,128)(2,1)}, u32[]{:S(2)}, u32[]{:S(2)}) collective-permute-start(bf16[2,27,16,256]{3,2,1,0:T(8,128)(2,1)S(1)} %collective-permute-done.7.refs_4_), channel_id=1, source_target_pairs={{0,4},{1,5},{2,6},{3,7},{4,8},{5,9},{6,10},{7,11},{8,12},{9,13},{1... | collective-permute-start | bytes 1327112 | tf_op jit(solution)/shard_map/ppermute | solution.py:246
  70.5 10.2 %collective-permute-start.10 = (bf16[2,27,16,256]{3,2,1,0:T(8,128)(2,1)}, bf16[2,27,16,256]{3,2,1,0:T(8,128)(2,1)}, u32[]{:S(2)}, u32[]{:S(2)}) collective-permute-start(bf16[2,27,16,256]{3,2,1,0:T(8,128)(2,1)} %collective-permute-done.8.refs_5_), channel_id=1, source_target_pairs={{0,4},{1,5},{2,6},{3,7},{4,8},{5,9},{6,10},{7,11},{8,12},{9,13},{1... | collective-permute-start | bytes 1327112 | tf_op jit(solution)/shard_map/ppermute | solution.py:246
  83.1 8.7 %copy-start.4 = (f32[256]{0:T(256)S(1)}, f32[256]{0:T(256)}, u32[]{:S(2)}) copy-start(f32[256]{0:T(256)} %param.14) | copy-start | bytes 3076
  83.2 8.7 %copy-start.5 = (f32[256]{0:T(256)S(1)}, f32[256]{0:T(256)}, u32[]{:S(2)}) copy-start(f32[256]{0:T(256)} %param.15) | copy-start | bytes 3076
  83.2 8.7 %copy-start.7 = (s32[64]{0:T(128)S(1)}, s32[64]{0:T(128)}, u32[]{:S(2)}) copy-start(s32[64]{0:T(128)} %param.17) | copy-start | bytes 772
  83.2 8.6 %collective-permute-start.11 = (f32[2,2,64,256]{3,2,1,0:T(8,128)S(1)}, f32[2,2,64,256]{3,2,1,0:T(8,128)S(1)}, u32[]{:S(2)}, u32[]{:S(2)}) collective-permute-start(f32[2,2,64,256]{3,2,1,0:T(8,128)S(1)} %shard_map.95), channel_id=1, source_target_pairs={{0,32},{1,33},{2,34},{3,35},{4,36},{5,37},{6,38},{7,39},{8,40},{9,... | collective-permute-start | bytes 786440 | tf_op jit(solution)/shard_map/ppermute | solution.py:246

commit v5 on v4

--- a/solution.py
+++ b/solution.py
@@ -319,11 +319,11 @@
     edge = along(edge, -1, 1)
     near = beside[:SHARD].reshape(27, GW, CO)
     a0 = jnp.where(core == 0, jnp.stack([weights, near]), jnp.stack([second, near]))
-    b0 = other_core(a0)
-    a1, b1 = ring(a0), ring(b0)
+    a1 = ring(a0)
+    b1 = shift(a0, lambda y, core, z, x: (y, 1 - core, z - 1 + 2 * core, x))
     windows = call_pack(latent, beside, edge, gathered)
     columns = lax.all_to_all(windows, ("y", "core"), 0, 0, tiled=True)
-    a2, b2 = ring(a1), ring(b1)
+    a2, b2 = ring(lax.optimization_barrier((a1, b1))[0]), ring(b1)
     a3, b3 = ring(a2), ring(b2)
     act = call_activate(lengths, gamma[None], beta[None], smooth[None], columns)
     a4 = ring(a3)

time: 93.5 us -> 90.2 us (0.965)
  starting transfers between devices: 71.6 us -> 66.9 us
  waiting for transfers between devices: 6.15 us -> 7.64 us
    ppermute x12 -> x11, starting transfers between devices: 60.5 us -> 54.4 us  [shift(): return lax.ppermute(value, AXES, pairs)]
    all_to_all x1, starting transfers between devices: 7.23 us -> 8.65 us  [local(): columns = lax.all_to_all(windows, ('y', 'core'), 0, 0, tiled=True)]
    all_to_all x1, waiting for transfers between devices: 0.01 us -> 1.28 us  [local(): columns = lax.all_to_all(windows, ('y', 'core'), 0, 0, tiled=True)]
    ppermute x12 -> x11, waiting for transfers between devices: 6.15 us -> 6.36 us  [shift(): return lax.ppermute(value, AXES, pairs)]
  transfers between devices with their start and end apart: 14 -> 13, of which waited for: 3 -> 5; matrix products, arithmetic and copies ran while one was open for 1% -> 1% of each run, Pallas kernels for 8% -> 8%
where the time goes in v5:
time: 90.2 us; the launch traced here: 89.5 us
  starting transfers between devices  66.9 us (74%)
  Pallas kernels  12.8 us (14%)
  waiting for transfers between devices  7.64 us (8%)
  other arithmetic  1.01 us (1%)
    ppermute x11, starting transfers between devices, shift(): return lax.ppermute(value, AXES, pairs)  54.4 us
    all_to_all x1, starting transfers between devices, local(): columns = lax.all_to_all(windows, ('y', 'core'), 0, 0, tiled=True)  8.65 us
    ppermute x11, waiting for transfers between devices, shift(): return lax.ppermute(value, AXES, pairs)  6.36 us
    pallas_call x2, Pallas kernels, part(): pl.pallas_call(functools.partial(convolve, own_columns), out_shape=struct...  4.72 us
    all_to_all x1, starting transfers between devices, local(): gathered = lax.all_to_all(spread, ('z', 'x'), 0, 0, tiled=True)  3.87 us
    pallas_call x1, Pallas kernels, call_prepare(): pl.pallas_call(prepare, out_shape=(struct((NZ * NX, 8, 128), F32), struct...  3.14 us
    pallas_call x1, Pallas kernels, call_activate(): pl.pallas_call(activate, out_shape=struct((3, 4, 6, T, HALF), BF16), in_s...  3.03 us
  transfers between devices with their start and end apart: 13, of which 5 were waited for; matrix products, arithmetic and copies ran while one was open for 1% of the time, Pallas kernels for 8%

profile of v5, /device:TPU:1, one launch (start us, length us, event | category | flops | bytes accessed | tf_op | source)
XLA Modules:
  0.0 89.5 jit_solution(13192692276790680846)
XLA Ops:
  0.0 3.1 %shard_map.91 = (f32[32,8,128]{2,1,0:T(8,128)}, bf16[688,256]{1,0:T(8,128)(2,1)}, bf16[128,512]{1,0:T(8,128)(2,1)}) custom-call(bf16[4,2,32,512]{3,2,1,0:T(8,128)(2,1)} %bitcast.11, bf16[27,16,256]{2,1,0:T(8,128)(2,1)} %bitcast.20), custom_call_target="tpu_custom_call" | custom-call | flops 65536 | bytes 65536 | tf_op jit(solution)/shard_map/pallas_call | solution.py:266
  3.2 3.9 %collective-permute-start = (bf16[688,256]{1,0:T(8,128)(2,1)}, bf16[688,256]{1,0:T(8,128)(2,1)S(1)}, u32[]{:S(2)}, u32[]{:S(2)}) collective-permute-start(bf16[688,256]{1,0:T(8,128)(2,1)} %get-tuple-element.9), channel_id=1, source_target_pairs={{0,31},{1,0},{2,1},{3,2},{4,3},{5,4},{6,5},{7,6},{8,7},{9,8},{10,9... | collective-permute-start | bytes 1056776 | tf_op jit(solution)/shard_map/ppermute | solution.py:246
  7.1 12.8 %collective-permute-start.2 = (bf16[27,16,256]{2,1,0:T(8,128)(2,1)}, bf16[27,16,256]{2,1,0:T(8,128)(2,1)S(1)}, u32[]{:S(2)}, u32[]{:S(2)}) collective-permute-start(bf16[27,16,256]{2,1,0:T(8,128)(2,1)} %bitcast.21), channel_id=1, source_target_pairs={{32,62},{33,63},{34,32},{35,33},{36,34},{37,35},{38,36},{39,37},{4... | collective-permute-start | bytes 663560 | tf_op jit(solution)/shard_map/ppermute | solution.py:246
  20.0 3.9 %all-to-all-start = ((f32[32,8,128]{2,1,0:T(8,128)}), f32[32,8,128]{2,1,0:T(8,128)S(1)}, u32[]{:S(2)}, u32[]{:S(2)}) async-start(f32[32,8,128]{2,1,0:T(8,128)} %get-tuple-element.11), calls=%async_computation | async-start | bytes 262144 | tf_op jit(solution)/shard_map/all_to_all | solution.py:318
  23.8 6.6 %collective-permute-start.1 = (bf16[128,512]{1,0:T(8,128)(2,1)}, bf16[128,512]{1,0:T(8,128)(2,1)S(1)}, u32[]{:S(2)}, u32[]{:S(2)}) collective-permute-start(bf16[128,512]{1,0:T(8,128)(2,1)} %get-tuple-element.10), channel_id=1, source_target_pairs={{0,1},{1,2},{2,3},{3,4},{4,5},{5,6},{6,7},{7,8},{8,9},{9,10},{10,1... | collective-permute-start | bytes 393224 | tf_op jit(solution)/shard_map/ppermute | solution.py:246
  30.4 0.0 copy-start.1
  30.5 0.0 copy-start.2
  30.5 0.0 copy-start.3
  30.5 0.0 copy-start.6
  30.5 1.0 %fusion.refs_0_ = bf16[2,27,16,256]{3,2,1,0:T(8,128)(2,1)S(1)} fusion(bf16[1,27,16,256]{3,2,1,0:T(8,128)(2,1)S(1)} %bitcast.19, bf16[1,27,16,256]{3,2,1,0:T(8,128)(2,1)} %bitcast.22, bf16[1,27,16,256]{3,2,1,0:T(8,128)(2,1)S(1)} %bitcast.23, pred[]{:T(512)S(6)} %eq.3), kind=kLoop, calls=%fused_computation.2 | loop fusion | flops 663552 | bytes 1105921 | tf_op jit(solution)/shard_map/jit(_where)/select_n | solution.py:321
  31.5 3.1 %collective-permute-start.3 = (bf16[2,27,16,256]{3,2,1,0:T(8,128)(2,1)S(1)}, bf16[2,27,16,256]{3,2,1,0:T(8,128)(2,1)S(1)}, u32[]{:S(2)}, u32[]{:S(2)}) collective-permute-start(bf16[2,27,16,256]{3,2,1,0:T(8,128)(2,1)S(1)} %fusion.refs_0_), channel_id=1, source_target_pairs={{0,4},{1,5},{2,6},{3,7},{4,8},{5,9},{6,10},{7,11},{8,12},{9,13},{1... | collective-permute-start | bytes 1327112 | tf_op jit(solution)/shard_map/ppermute | solution.py:246
  34.6 1.9 %collective-permute-start.4 = (bf16[2,27,16,256]{3,2,1,0:T(8,128)(2,1)S(1)}, bf16[2,27,16,256]{3,2,1,0:T(8,128)(2,1)S(1)}, u32[]{:S(2)}, u32[]{:S(2)}) collective-permute-start(bf16[2,27,16,256]{3,2,1,0:T(8,128)(2,1)S(1)} %fusion.refs_0_), channel_id=1, source_target_pairs={{0,60},{1,61},{2,62},{3,63},{4,32},{5,33},{6,34},{7,35},{8,36},{9,... | collective-permute-start | bytes 1327112 | tf_op jit(solution)/shard_map/ppermute | solution.py:246
  36.5 1.7 %shard_map.92 = bf16[16,112,256]{2,1,0:T(8,128)(2,1)} custom-call(bf16[4,2,32,512]{3,2,1,0:T(8,128)(2,1)S(1)} %bitcast.12, bf16[688,256]{1,0:T(8,128)(2,1)S(1)} %collective-permute-done.beside_ref, bf16[128,512]{1,0:T(8,128)(2,1)S(1)} %collective-permute-done.1.edge_ref, f32[32,8,128]{2,1,0:T(8,128)S(1)} %all-to-all-done.sums_ref), custom_call_target="tpu_custom_call" | custom-call | flops 65536 | bytes 65536 | tf_op jit(solution)/shard_map/pallas_call | solution.py:278
  38.3 8.7 %all-to-all-start.1 = ((bf16[16,112,256]{2,1,0:T(8,128)(2,1)}), bf16[16,112,256]{2,1,0:T(8,128)(2,1)S(1)}, u32[]{:S(2)}, u32[]{:S(2)}) async-start(bf16[16,112,256]{2,1,0:T(8,128)(2,1)} %shard_map.92), calls=%async_computation.1 | async-start | bytes 1835008 | tf_op jit(solution)/shard_map/all_to_all | solution.py:325
  46.9 3.1 %collective-permute-start.5 = (bf16[2,27,16,256]{3,2,1,0:T(8,128)(2,1)S(1)}, bf16[2,27,16,256]{3,2,1,0:T(8,128)(2,1)S(1)}, u32[]{:S(2)}, u32[]{:S(2)}) collective-permute-start(bf16[2,27,16,256]{3,2,1,0:T(8,128)(2,1)S(1)} %collective-permute-done.3.refs_1_), channel_id=1, source_target_pairs={{0,4},{1,5},{2,6},{3,7},{4,8},{5,9},{6,10},{7,11},{8,12},{9,13},{1... | collective-permute-start | bytes 1327112 | tf_op jit(solution)/shard_map/ppermute | solution.py:246
  50.0 2.2 %collective-permute-start.6 = (bf16[2,27,16,256]{3,2,1,0:T(8,128)(2,1)S(1)}, bf16[2,27,16,256]{3,2,1,0:T(8,128)(2,1)S(1)}, u32[]{:S(2)}, u32[]{:S(2)}) collective-permute-start(bf16[2,27,16,256]{3,2,1,0:T(8,128)(2,1)S(1)} %collective-permute-done.4.refs_2_), channel_id=1, source_target_pairs={{0,4},{1,5},{2,6},{3,7},{4,8},{5,9},{6,10},{7,11},{8,12},{9,13},{1... | collective-permute-start | bytes 1327112 | tf_op jit(solution)/shard_map/ppermute | solution.py:246
  52.2 4.1 %collective-permute-done.5.refs_3_ = bf16[2,27,16,256]{3,2,1,0:T(8,128)(2,1)S(1)} collective-permute-done((bf16[2,27,16,256]{3,2,1,0:T(8,128)(2,1)S(1)}, bf16[2,27,16,256]{3,2,1,0:T(8,128)(2,1)S(1)}, u32[]{:S(2)}, u32[]{:S(2)}) %collective-permute-start.5) | collective-permute-done | bytes 442400 | tf_op jit(solution)/shard_map/ppermute | solution.py:246
  56.3 4.3 %collective-permute-start.7 = (bf16[2,27,16,256]{3,2,1,0:T(8,128)(2,1)S(1)}, bf16[2,27,16,256]{3,2,1,0:T(8,128)(2,1)}, u32[]{:S(2)}, u32[]{:S(2)}) collective-permute-start(bf16[2,27,16,256]{3,2,1,0:T(8,128)(2,1)S(1)} %collective-permute-done.5.refs_3_), channel_id=1, source_target_pairs={{0,4},{1,5},{2,6},{3,7},{4,8},{5,9},{6,10},{7,11},{8,12},{9,13},{1... | collective-permute-start | bytes 1327112 | tf_op jit(solution)/shard_map/ppermute | solution.py:246
  60.5 0.5 collective-permute-done.6.refs_4_
  61.0 4.3 %collective-permute-start.8 = (bf16[2,27,16,256]{3,2,1,0:T(8,128)(2,1)S(1)}, bf16[2,27,16,256]{3,2,1,0:T(8,128)(2,1)}, u32[]{:S(2)}, u32[]{:S(2)}) collective-permute-start(bf16[2,27,16,256]{3,2,1,0:T(8,128)(2,1)S(1)} %collective-permute-done.6.refs_4_), channel_id=1, source_target_pairs={{0,4},{1,5},{2,6},{3,7},{4,8},{5,9},{6,10},{7,11},{8,12},{9,13},{1... | collective-permute-start | bytes 1327112 | tf_op jit(solution)/shard_map/ppermute | solution.py:246
  65.3 0.6 collective-permute-done.7.refs_5_
  65.9 5.1 %collective-permute-start.9 = (bf16[2,27,16,256]{3,2,1,0:T(8,128)(2,1)}, bf16[2,27,16,256]{3,2,1,0:T(8,128)(2,1)}, u32[]{:S(2)}, u32[]{:S(2)}) collective-permute-start(bf16[2,27,16,256]{3,2,1,0:T(8,128)(2,1)} %collective-permute-done.7.refs_5_), channel_id=1, source_target_pairs={{0,4},{1,5},{2,6},{3,7},{4,8},{5,9},{6,10},{7,11},{8,12},{9,13},{1... | collective-permute-start | bytes 1327112 | tf_op jit(solution)/shard_map/ppermute | solution.py:246
  70.9 1.3 %all-to-all-done.1.x_ref = bf16[16,112,256]{2,1,0:T(8,128)(2,1)S(1)} async-done(((bf16[16,112,256]{2,1,0:T(8,128)(2,1)}), bf16[16,112,256]{2,1,0:T(8,128)(2,1)S(1)}, u32[]{:S(2)}, u32[]{:S(2)}) %all-to-all-start.1) | async-done | bytes 917536 | tf_op jit(solution)/shard_map/all_to_all | solution.py:325
  72.2 3.0 %shard_map.93.act_ref = bf16[3,4,6,64,256]{4,3,2,1,0:T(8,128)(2,1)S(1)} custom-call(s32[10]{0:T(128)S(1)} %copy-done.6, f32[1,512]{1,0:T(1,128)S(1)} %bitcast.13, f32[1,512]{1,0:T(1,128)S(1)} %bitcast.14, f32[1,512]{1,0:T(1,128)S(1)} %bitcast.15, bf16[16,112,256]{2,1,0:T(8,128)(2,1)S(1)} %all-to-all-done.1.x_ref), custom_call_target="tpu_custom_call" | custom-call | flops 65536 | bytes 65536 | tf_op jit(solution)/shard_map/pallas_call | solution.py:285
  75.3 1.2 %collective-permute-done.9.refs_7_ = bf16[2,27,16,256]{3,2,1,0:T(8,128)(2,1)} collective-permute-done((bf16[2,27,16,256]{3,2,1,0:T(8,128)(2,1)}, bf16[2,27,16,256]{3,2,1,0:T(8,128)(2,1)}, u32[]{:S(2)}, u32[]{:S(2)}) %collective-permute-start.9) | collective-permute-done | bytes 442400 | tf_op jit(solution)/shard_map/ppermute | solution.py:246
  76.5 2.4 %shard_map.95 = f32[2,2,64,256]{3,2,1,0:T(8,128)S(1)} custom-call(bf16[3,4,6,64,256]{4,3,2,1,0:T(8,128)(2,1)S(1)} %shard_map.93.act_ref, bf16[2,27,16,256]{3,2,1,0:T(8,128)(2,1)S(1)} %fusion.refs_0_, bf16[2,27,16,256]{3,2,1,0:T(8,128)(2,1)S(1)} %collective-permute-done.3.refs_1_, bf16[2,27,16,256]{3,2,1,0:T(8,128)(2,1)S(1)} %collective-permute-done.4.refs_2_, ...), custom_call_target="tpu_custom_call" | custom-call | flops 1073741824 | bytes 65536 | tf_op jit(solution)/shard_map/pallas_call | solution.py:333
  78.8 0.0 copy-start.4
  78.9 0.0 copy-start.5
  78.9 7.2 %collective-permute-start.10 = (f32[2,2,64,256]{3,2,1,0:T(8,128)S(1)}, f32[2,2,64,256]{3,2,1,0:T(8,128)S(1)}, u32[]{:S(2)}, u32[]{:S(2)}) collective-permute-start(f32[2,2,64,256]{3,2,1,0:T(8,128)S(1)} %shard_map.95), channel_id=1, source_target_pairs={{0,32},{1,33},{2,34},{3,35},{4,36},{5,37},{6,38},{7,39},{8,40},{9,... | collective-permute-start | bytes 786440 | tf_op jit(solution)/shard_map/ppermute | solution.py:246
  86.1 2.4 %shard_map.94.a_ref = f32[2,2,64,256]{3,2,1,0:T(8,128)S(1)} custom-call(bf16[3,4,6,64,256]{4,3,2,1,0:T(8,128)(2,1)S(1)} %shard_map.93.act_ref, bf16[2,27,16,256]{3,2,1,0:T(8,128)(2,1)S(1)} %fusion.refs_0_, bf16[2,27,16,256]{3,2,1,0:T(8,128)(2,1)S(1)} %collective-permute-done.3.refs_1_, bf16[2,27,16,256]{3,2,1,0:T(8,128)(2,1)S(1)} %collective-permute-done.4.refs_2_, ...), custom_call_target="tpu_custom_call" | custom-call | flops 1073741824 | bytes 65536 | tf_op jit(solution)/shard_map/pallas_call | solution.py:333
  88.5 0.2 shard_map.96
  88.7 0.7 reshape.7
  (19 shorter events, 0.1 us)
Async XLA Ops:
  0.0 36.5 %copy-start = (bf16[1,4,2,32,512]{4,3,2,1,0:T(8,128)(2,1)S(1)}, bf16[1,4,2,32,512]{4,3,2,1,0:T(8,128)(2,1)}, u32[]{:S(2)}) copy-start(bf16[1,4,2,32,512]{4,3,2,1,0:T(8,128)(2,1)} %param.9) | copy-start | bytes 786436
  3.2 27.2 %collective-permute-start = (bf16[688,256]{1,0:T(8,128)(2,1)}, bf16[688,256]{1,0:T(8,128)(2,1)S(1)}, u32[]{:S(2)}, u32[]{:S(2)}) collective-permute-start(bf16[688,256]{1,0:T(8,128)(2,1)} %get-tuple-element.9), channel_id=1, source_target_pairs={{0,31},{1,0},{2,1},{3,2},{4,3},{5,4},{6,5},{7,6},{8,7},{9,8},{10,9... | collective-permute-start | bytes 1056776 | tf_op jit(solution)/shard_map/ppermute | solution.py:246
  7.1 23.3 %collective-permute-start.2 = (bf16[27,16,256]{2,1,0:T(8,128)(2,1)}, bf16[27,16,256]{2,1,0:T(8,128)(2,1)S(1)}, u32[]{:S(2)}, u32[]{:S(2)}) collective-permute-start(bf16[27,16,256]{2,1,0:T(8,128)(2,1)} %bitcast.21), channel_id=1, source_target_pairs={{32,62},{33,63},{34,32},{35,33},{36,34},{37,35},{38,36},{39,37},{4... | collective-permute-start | bytes 663560 | tf_op jit(solution)/shard_map/ppermute | solution.py:246
  20.0 16.6 %all-to-all-start = ((f32[32,8,128]{2,1,0:T(8,128)}), f32[32,8,128]{2,1,0:T(8,128)S(1)}, u32[]{:S(2)}, u32[]{:S(2)}) async-start(f32[32,8,128]{2,1,0:T(8,128)} %get-tuple-element.11), calls=%async_computation | async-start | bytes 262144 | tf_op jit(solution)/shard_map/all_to_all | solution.py:318
  23.8 12.7 %collective-permute-start.1 = (bf16[128,512]{1,0:T(8,128)(2,1)}, bf16[128,512]{1,0:T(8,128)(2,1)S(1)}, u32[]{:S(2)}, u32[]{:S(2)}) collective-permute-start(bf16[128,512]{1,0:T(8,128)(2,1)} %get-tuple-element.10), channel_id=1, source_target_pairs={{0,1},{1,2},{2,3},{3,4},{4,5},{5,6},{6,7},{7,8},{8,9},{9,10},{10,1... | collective-permute-start | bytes 393224 | tf_op jit(solution)/shard_map/ppermute | solution.py:246
  30.4 41.8 %copy-start.1 = (f32[512]{0:T(512)S(1)}, f32[512]{0:T(512)}, u32[]{:S(2)}) copy-start(f32[512]{0:T(512)} %param.10) | copy-start | bytes 6148
  30.5 41.8 %copy-start.2 = (f32[512]{0:T(512)S(1)}, f32[512]{0:T(512)}, u32[]{:S(2)}) copy-start(f32[512]{0:T(512)} %param.11) | copy-start | bytes 6148
  30.5 41.8 %copy-start.3 = (f32[512]{0:T(512)S(1)}, f32[512]{0:T(512)}, u32[]{:S(2)}) copy-start(f32[512]{0:T(512)} %param.12) | copy-start | bytes 6148
  30.5 41.7 %copy-start.6 = (s32[10]{0:T(128)S(1)}, s32[10]{0:T(128)}, u32[]{:S(2)}) copy-start(s32[10]{0:T(128)} %lengths_ref.1) | copy-start | bytes 124
  31.5 15.4 %collective-permute-start.3 = (bf16[2,27,16,256]{3,2,1,0:T(8,128)(2,1)S(1)}, bf16[2,27,16,256]{3,2,1,0:T(8,128)(2,1)S(1)}, u32[]{:S(2)}, u32[]{:S(2)}) collective-permute-start(bf16[2,27,16,256]{3,2,1,0:T(8,128)(2,1)S(1)} %fusion.refs_0_), channel_id=1, source_target_pairs={{0,4},{1,5},{2,6},{3,7},{4,8},{5,9},{6,10},{7,11},{8,12},{9,13},{1... | collective-permute-start | bytes 1327112 | tf_op jit(solution)/shard_map/ppermute | solution.py:246
  34.6 12.4 %collective-permute-start.4 = (bf16[2,27,16,256]{3,2,1,0:T(8,128)(2,1)S(1)}, bf16[2,27,16,256]{3,2,1,0:T(8,128)(2,1)S(1)}, u32[]{:S(2)}, u32[]{:S(2)}) collective-permute-start(bf16[2,27,16,256]{3,2,1,0:T(8,128)(2,1)S(1)} %fusion.refs_0_), channel_id=1, source_target_pairs={{0,60},{1,61},{2,62},{3,63},{4,32},{5,33},{6,34},{7,35},{8,36},{9,... | collective-permute-start | bytes 1327112 | tf_op jit(solution)/shard_map/ppermute | solution.py:246
  38.3 33.9 %all-to-all-start.1 = ((bf16[16,112,256]{2,1,0:T(8,128)(2,1)}), bf16[16,112,256]{2,1,0:T(8,128)(2,1)S(1)}, u32[]{:S(2)}, u32[]{:S(2)}) async-start(bf16[16,112,256]{2,1,0:T(8,128)(2,1)} %shard_map.92), calls=%async_computation.1 | async-start | bytes 1835008 | tf_op jit(solution)/shard_map/all_to_all | solution.py:325
  46.9 9.3 %collective-permute-start.5 = (bf16[2,27,16,256]{3,2,1,0:T(8,128)(2,1)S(1)}, bf16[2,27,16,256]{3,2,1,0:T(8,128)(2,1)S(1)}, u32[]{:S(2)}, u32[]{:S(2)}) collective-permute-start(bf16[2,27,16,256]{3,2,1,0:T(8,128)(2,1)S(1)} %collective-permute-done.3.refs_1_), channel_id=1, source_target_pairs={{0,4},{1,5},{2,6},{3,7},{4,8},{5,9},{6,10},{7,11},{8,12},{9,13},{1... | collective-permute-start | bytes 1327112 | tf_op jit(solution)/shard_map/ppermute | solution.py:246
  50.0 11.0 %collective-permute-start.6 = (bf16[2,27,16,256]{3,2,1,0:T(8,128)(2,1)S(1)}, bf16[2,27,16,256]{3,2,1,0:T(8,128)(2,1)S(1)}, u32[]{:S(2)}, u32[]{:S(2)}) collective-permute-start(bf16[2,27,16,256]{3,2,1,0:T(8,128)(2,1)S(1)} %collective-permute-done.4.refs_2_), channel_id=1, source_target_pairs={{0,4},{1,5},{2,6},{3,7},{4,8},{5,9},{6,10},{7,11},{8,12},{9,13},{1... | collective-permute-start | bytes 1327112 | tf_op jit(solution)/shard_map/ppermute | solution.py:246
  56.3 9.6 %collective-permute-start.7 = (bf16[2,27,16,256]{3,2,1,0:T(8,128)(2,1)S(1)}, bf16[2,27,16,256]{3,2,1,0:T(8,128)(2,1)}, u32[]{:S(2)}, u32[]{:S(2)}) collective-permute-start(bf16[2,27,16,256]{3,2,1,0:T(8,128)(2,1)S(1)} %collective-permute-done.5.refs_3_), channel_id=1, source_target_pairs={{0,4},{1,5},{2,6},{3,7},{4,8},{5,9},{6,10},{7,11},{8,12},{9,13},{1... | collective-permute-start | bytes 1327112 | tf_op jit(solution)/shard_map/ppermute | solution.py:246
  61.0 14.3 %collective-permute-start.8 = (bf16[2,27,16,256]{3,2,1,0:T(8,128)(2,1)S(1)}, bf16[2,27,16,256]{3,2,1,0:T(8,128)(2,1)}, u32[]{:S(2)}, u32[]{:S(2)}) collective-permute-start(bf16[2,27,16,256]{3,2,1,0:T(8,128)(2,1)S(1)} %collective-permute-done.6.refs_4_), channel_id=1, source_target_pairs={{0,4},{1,5},{2,6},{3,7},{4,8},{5,9},{6,10},{7,11},{8,12},{9,13},{1... | collective-permute-start | bytes 1327112 | tf_op jit(solution)/shard_map/ppermute | solution.py:246
  65.9 10.6 %collective-permute-start.9 = (bf16[2,27,16,256]{3,2,1,0:T(8,128)(2,1)}, bf16[2,27,16,256]{3,2,1,0:T(8,128)(2,1)}, u32[]{:S(2)}, u32[]{:S(2)}) collective-permute-start(bf16[2,27,16,256]{3,2,1,0:T(8,128)(2,1)} %collective-permute-done.7.refs_5_), channel_id=1, source_target_pairs={{0,4},{1,5},{2,6},{3,7},{4,8},{5,9},{6,10},{7,11},{8,12},{9,13},{1... | collective-permute-start | bytes 1327112 | tf_op jit(solution)/shard_map/ppermute | solution.py:246
  78.8 9.7 %copy-start.4 = (f32[256]{0:T(256)S(1)}, f32[256]{0:T(256)}, u32[]{:S(2)}) copy-start(f32[256]{0:T(256)} %param.14) | copy-start | bytes 3076
  78.9 9.7 %copy-start.5 = (f32[256]{0:T(256)S(1)}, f32[256]{0:T(256)}, u32[]{:S(2)}) copy-start(f32[256]{0:T(256)} %param.15) | copy-start | bytes 3076
  78.9 9.7 %copy-start.7 = (s32[64]{0:T(128)S(1)}, s32[64]{0:T(128)}, u32[]{:S(2)}) copy-start(s32[64]{0:T(128)} %param.17) | copy-start | bytes 772
  78.9 9.6 %collective-permute-start.10 = (f32[2,2,64,256]{3,2,1,0:T(8,128)S(1)}, f32[2,2,64,256]{3,2,1,0:T(8,128)S(1)}, u32[]{:S(2)}, u32[]{:S(2)}) collective-permute-start(f32[2,2,64,256]{3,2,1,0:T(8,128)S(1)} %shard_map.95), channel_id=1, source_target_pairs={{0,32},{1,33},{2,34},{3,35},{4,36},{5,37},{6,38},{7,39},{8,40},{9,... | collective-permute-start | bytes 786440 | tf_op jit(solution)/shard_map/ppermute | solution.py:246

commit v6 on v5

--- a/solution.py
+++ b/solution.py
@@ -15,6 +15,7 @@
 SLABS = 16
 T = FR * SLABS
 HALF = C // 2
+LAST = 384
 SHARD = 27 * GW
 EDGE = FR * W
 NY, NC, NZ, NX = 8, 2, 8, 4
@@ -147,7 +148,7 @@
     return start
 
 
-def activate(lengths_ref, gamma_ref, beta_ref, smooth_ref, x_ref, act_ref):
+def activate(lengths_ref, gamma_ref, beta_ref, smooth_ref, x_ref, act_ref, last_ref):
     y, core, s = lax.axis_index("y"), lax.axis_index("core"), lax.axis_index("z") * NX + lax.axis_index("x")
     n = 2 * T
     thirds = x_ref[:, 96:112, :].astype(F32)[:, :8, :128].reshape(n, 128)
@@ -209,6 +210,10 @@
             e = bdot(earlier, v).astype(BF16)
             act_ref[0, r, c] = e[:T]
             act_ref[1, r, c] = e[T:]
+    for r in range(4):
+        for c in range(4):
+            taps = [act_ref[j, r, c + b, :, HALF - 2 * GW :] for j in range(3) for b in range(3)]
+            last_ref[r, c] = jnp.concatenate(taps + [jnp.zeros((T, LAST - 18 * GW), BF16)], axis=1)
 
 
 def convolve(own_columns, act_ref, *refs):
@@ -220,8 +225,18 @@
         j, a, b = tap // 9, tap // 3 % 3, tap % 3
         lhs = act_ref[j, a : a + 2, pl.ds(column + b, 2)].reshape(4 * T, HALF)
         rows = jnp.concatenate([v[i, tap] for v in weights for i in range(2)], axis=0)
-        term = bdot(lhs, rows)
+        term = bdot(lhs[:, : rows.shape[0]], rows)
         total = term if total is None else total + term
+    out_ref[...] = total.reshape(2, 2, T, CO)
+
+
+def complete(last_ref, w_ref, part_ref, out_ref):
+    column = 2 - 2 * lax.axis_index("core")
+    total = part_ref[...].reshape(4 * T, CO)
+    for a in range(3):
+        lhs = last_ref[a : a + 2, pl.ds(column, 2)].reshape(4 * T, LAST)
+        rows = [w_ref[i, 9 * j + 3 * a + b] for j in range(3) for b in range(3) for i in range(2)]
+        total = total + bdot(lhs, jnp.concatenate(rows + [jnp.zeros((LAST - 18 * GW, CO), BF16)], axis=0))
     out_ref[...] = total.reshape(2, 2, T, CO)
 
 
@@ -283,7 +298,8 @@
 
 def call_activate(*args):
     return pl.pallas_call(
-        activate, out_shape=struct((3, 4, 6, T, HALF), BF16), in_specs=[SMEM] + [VMEM] * 4, out_specs=VMEM,
+        activate, out_shape=(struct((3, 4, 6, T, HALF), BF16), struct((4, 4, T, LAST), BF16)),
+        in_specs=[SMEM] + [VMEM] * 4, out_specs=(VMEM, VMEM),
         compiler_params=params(), cost_estimate=cost(2**16, 2**16),
     )(*args)
 
@@ -325,18 +341,20 @@
     columns = lax.all_to_all(windows, ("y", "core"), 0, 0, tiled=True)
     a2, b2 = ring(lax.optimization_barrier((a1, b1))[0]), ring(b1)
     a3, b3 = ring(a2), ring(b2)
-    act = call_activate(lengths, gamma[None], beta[None], smooth[None], columns)
+    act, last = call_activate(lengths, gamma[None], beta[None], smooth[None], columns)
     a4 = ring(a3)
 
 
-    def part(own_columns):
+    def part(kernel, *args):
         return pl.pallas_call(
-            functools.partial(convolve, own_columns), out_shape=struct((2, 2, T, CO), F32),
-            in_specs=[VMEM] * 9, out_specs=VMEM, compiler_params=params(32), cost_estimate=cost(2**30, 2**16),
-        )(act, a0, a1, b1, a2, b2, a3, b3, a4)
-
-    other = other_core(part(False))
-    keep = part(True)
+            kernel, out_shape=struct((2, 2, T, CO), F32), in_specs=[VMEM] * len(args), out_specs=VMEM,
+            compiler_params=params(32), cost_estimate=cost(2**16, 2**16),
+        )(*args)
+
+    pieces = (a0, a1, b1, a2, b2, a3, b3)
+    sent = part(functools.partial(convolve, False), act, *pieces)
+    other = other_core(part(complete, last, a4, sent))
+    keep = part(functools.partial(convolve, True), act, *pieces, a4)
     out = call_finish(order[None], w_scale[None], bias[None], keep, other)
     return out.reshape(SLABS, FR, 2, 2, CO)
 

time: 90.2 us -> 87.5 us (0.970)
  waiting for transfers between devices: 7.64 us -> 3.88 us
    ppermute x11, waiting for transfers between devices: 6.36 us -> 3.81 us  [shift(): return lax.ppermute(value, AXES, pairs)]
    all_to_all x1, waiting for transfers between devices: 1.28 us -> 0.07 us  [local(): columns = lax.all_to_all(windows, ('y', 'core'), 0, 0, tiled=True)]
    ppermute x11, starting transfers between devices: 54.4 us -> 55.3 us  [shift(): return lax.ppermute(value, AXES, pairs)]
    pallas_call x3 -> x4, Pallas kernels: 7.75 us -> 8.46 us  [the longest x3 5.07 us: part(): pl.pallas_call(kernel, out_shape=struct((2, 2, T, CO), F32), in_specs=[VM...]
  transfers between devices with their start and end apart: 13 -> 13, of which waited for: 5 -> 3; matrix products, arithmetic and copies ran while one was open for 1% -> 1% of each run, Pallas kernels for 8% -> 11%
where the time goes in v6:
time: 87.5 us; the launch traced here: 86.8 us
  starting transfers between devices  67.2 us (77%)
  Pallas kernels  13.5 us (15%)
  waiting for transfers between devices  3.88 us (4%)
  other arithmetic  1.01 us (1%)
    ppermute x11, starting transfers between devices, shift(): return lax.ppermute(value, AXES, pairs)  55.3 us
    all_to_all x1, starting transfers between devices, local(): columns = lax.all_to_all(windows, ('y', 'core'), 0, 0, tiled=True)  8.09 us
    pallas_call x3, Pallas kernels, part(): pl.pallas_call(kernel, out_shape=struct((2, 2, T, CO), F32), in_specs=[VM...  5.07 us
    all_to_all x1, starting transfers between devices, local(): gathered = lax.all_to_all(spread, ('z', 'x'), 0, 0, tiled=True)  3.87 us
    ppermute x11, waiting for transfers between devices, shift(): return lax.ppermute(value, AXES, pairs)  3.81 us
    pallas_call x1, Pallas kernels, call_activate(): pl.pallas_call(activate, out_shape=(struct((3, 4, 6, T, HALF), BF16), str...  3.39 us
    pallas_call x1, Pallas kernels, call_prepare(): pl.pallas_call(prepare, out_shape=(struct((NZ * NX, 8, 128), F32), struct...  3.14 us
  transfers between devices with their start and end apart: 13, of which 3 were waited for; matrix products, arithmetic and copies ran while one was open for 1% of the time, Pallas kernels for 11%

profile of v6, /device:TPU:1, one launch (start us, length us, event | category | flops | bytes accessed | tf_op | source)
XLA Modules:
  0.0 86.8 jit_solution(4534264817067364860)
XLA Ops:
  0.0 3.1 %shard_map.91 = (f32[32,8,128]{2,1,0:T(8,128)}, bf16[688,256]{1,0:T(8,128)(2,1)}, bf16[128,512]{1,0:T(8,128)(2,1)}) custom-call(bf16[4,2,32,512]{3,2,1,0:T(8,128)(2,1)} %bitcast.11, bf16[27,16,256]{2,1,0:T(8,128)(2,1)} %bitcast.20), custom_call_target="tpu_custom_call" | custom-call | flops 65536 | bytes 65536 | tf_op jit(solution)/shard_map/pallas_call | solution.py:281
  3.2 3.9 %collective-permute-start = (bf16[688,256]{1,0:T(8,128)(2,1)}, bf16[688,256]{1,0:T(8,128)(2,1)S(1)}, u32[]{:S(2)}, u32[]{:S(2)}) collective-permute-start(bf16[688,256]{1,0:T(8,128)(2,1)} %get-tuple-element.11), channel_id=1, source_target_pairs={{0,31},{1,0},{2,1},{3,2},{4,3},{5,4},{6,5},{7,6},{8,7},{9,8},{10,9... | collective-permute-start | bytes 1056776 | tf_op jit(solution)/shard_map/ppermute | solution.py:261
  7.1 12.8 %collective-permute-start.2 = (bf16[27,16,256]{2,1,0:T(8,128)(2,1)}, bf16[27,16,256]{2,1,0:T(8,128)(2,1)S(1)}, u32[]{:S(2)}, u32[]{:S(2)}) collective-permute-start(bf16[27,16,256]{2,1,0:T(8,128)(2,1)} %bitcast.21), channel_id=1, source_target_pairs={{32,62},{33,63},{34,32},{35,33},{36,34},{37,35},{38,36},{39,37},{4... | collective-permute-start | bytes 663560 | tf_op jit(solution)/shard_map/ppermute | solution.py:261
  20.0 3.9 %all-to-all-start = ((f32[32,8,128]{2,1,0:T(8,128)}), f32[32,8,128]{2,1,0:T(8,128)S(1)}, u32[]{:S(2)}, u32[]{:S(2)}) async-start(f32[32,8,128]{2,1,0:T(8,128)} %get-tuple-element.13), calls=%async_computation | async-start | bytes 262144 | tf_op jit(solution)/shard_map/all_to_all | solution.py:334
  23.8 6.6 %collective-permute-start.1 = (bf16[128,512]{1,0:T(8,128)(2,1)}, bf16[128,512]{1,0:T(8,128)(2,1)S(1)}, u32[]{:S(2)}, u32[]{:S(2)}) collective-permute-start(bf16[128,512]{1,0:T(8,128)(2,1)} %get-tuple-element.12), channel_id=1, source_target_pairs={{0,1},{1,2},{2,3},{3,4},{4,5},{5,6},{6,7},{7,8},{8,9},{9,10},{10,1... | collective-permute-start | bytes 393224 | tf_op jit(solution)/shard_map/ppermute | solution.py:261
  30.4 0.0 copy-start.1
  30.5 0.0 copy-start.2
  30.5 0.0 copy-start.3
  30.5 0.0 copy-start.6
  30.5 1.0 %fusion.refs_0_ = bf16[2,27,16,256]{3,2,1,0:T(8,128)(2,1)S(1)} fusion(bf16[1,27,16,256]{3,2,1,0:T(8,128)(2,1)S(1)} %bitcast.19, bf16[1,27,16,256]{3,2,1,0:T(8,128)(2,1)} %bitcast.22, bf16[1,27,16,256]{3,2,1,0:T(8,128)(2,1)S(1)} %bitcast.23, pred[]{:T(512)S(6)} %eq.3), kind=kLoop, calls=%fused_computation.2 | loop fusion | flops 663552 | bytes 1105921 | tf_op jit(solution)/shard_map/jit(_where)/select_n | solution.py:337
  31.5 1.9 %collective-permute-start.4 = (bf16[2,27,16,256]{3,2,1,0:T(8,128)(2,1)S(1)}, bf16[2,27,16,256]{3,2,1,0:T(8,128)(2,1)S(1)}, u32[]{:S(2)}, u32[]{:S(2)}) collective-permute-start(bf16[2,27,16,256]{3,2,1,0:T(8,128)(2,1)S(1)} %fusion.refs_0_), channel_id=1, source_target_pairs={{0,60},{1,61},{2,62},{3,63},{4,32},{5,33},{6,34},{7,35},{8,36},{9,... | collective-permute-start | bytes 1327112 | tf_op jit(solution)/shard_map/ppermute | solution.py:261
  33.4 3.1 %collective-permute-start.3 = (bf16[2,27,16,256]{3,2,1,0:T(8,128)(2,1)S(1)}, bf16[2,27,16,256]{3,2,1,0:T(8,128)(2,1)S(1)}, u32[]{:S(2)}, u32[]{:S(2)}) collective-permute-start(bf16[2,27,16,256]{3,2,1,0:T(8,128)(2,1)S(1)} %fusion.refs_0_), channel_id=1, source_target_pairs={{0,4},{1,5},{2,6},{3,7},{4,8},{5,9},{6,10},{7,11},{8,12},{9,13},{1... | collective-permute-start | bytes 1327112 | tf_op jit(solution)/shard_map/ppermute | solution.py:261
  36.5 1.7 %shard_map.92 = bf16[16,112,256]{2,1,0:T(8,128)(2,1)} custom-call(bf16[4,2,32,512]{3,2,1,0:T(8,128)(2,1)S(1)} %bitcast.12, bf16[688,256]{1,0:T(8,128)(2,1)S(1)} %collective-permute-done.beside_ref, bf16[128,512]{1,0:T(8,128)(2,1)S(1)} %collective-permute-done.1.edge_ref, f32[32,8,128]{2,1,0:T(8,128)S(1)} %all-to-all-done.sums_ref), custom_call_target="tpu_custom_call" | custom-call | flops 65536 | bytes 65536 | tf_op jit(solution)/shard_map/pallas_call | solution.py:293
  38.3 8.1 %all-to-all-start.1 = ((bf16[16,112,256]{2,1,0:T(8,128)(2,1)}), bf16[16,112,256]{2,1,0:T(8,128)(2,1)S(1)}, u32[]{:S(2)}, u32[]{:S(2)}) async-start(bf16[16,112,256]{2,1,0:T(8,128)(2,1)} %shard_map.92), calls=%async_computation.1 | async-start | bytes 1835008 | tf_op jit(solution)/shard_map/all_to_all | solution.py:341
  46.4 4.3 %collective-permute-start.5 = (bf16[2,27,16,256]{3,2,1,0:T(8,128)(2,1)S(1)}, bf16[2,27,16,256]{3,2,1,0:T(8,128)(2,1)S(1)}, u32[]{:S(2)}, u32[]{:S(2)}) collective-permute-start(bf16[2,27,16,256]{3,2,1,0:T(8,128)(2,1)S(1)} %collective-permute-done.3.refs_1_), channel_id=1, source_target_pairs={{0,4},{1,5},{2,6},{3,7},{4,8},{5,9},{6,10},{7,11},{8,12},{9,13},{1... | collective-permute-start | bytes 1327112 | tf_op jit(solution)/shard_map/ppermute | solution.py:261
  50.6 1.9 %collective-permute-start.6 = (bf16[2,27,16,256]{3,2,1,0:T(8,128)(2,1)S(1)}, bf16[2,27,16,256]{3,2,1,0:T(8,128)(2,1)}, u32[]{:S(2)}, u32[]{:S(2)}) collective-permute-start(bf16[2,27,16,256]{3,2,1,0:T(8,128)(2,1)S(1)} %collective-permute-done.4.refs_2_), channel_id=1, source_target_pairs={{0,4},{1,5},{2,6},{3,7},{4,8},{5,9},{6,10},{7,11},{8,12},{9,13},{1... | collective-permute-start | bytes 1327112 | tf_op jit(solution)/shard_map/ppermute | solution.py:261
  52.6 3.3 %collective-permute-done.5.refs_3_ = bf16[2,27,16,256]{3,2,1,0:T(8,128)(2,1)S(1)} collective-permute-done((bf16[2,27,16,256]{3,2,1,0:T(8,128)(2,1)S(1)}, bf16[2,27,16,256]{3,2,1,0:T(8,128)(2,1)S(1)}, u32[]{:S(2)}, u32[]{:S(2)}) %collective-permute-start.5) | collective-permute-done | bytes 442400 | tf_op jit(solution)/shard_map/ppermute | solution.py:261
  55.9 5.3 %collective-permute-start.7 = (bf16[2,27,16,256]{3,2,1,0:T(8,128)(2,1)S(1)}, bf16[2,27,16,256]{3,2,1,0:T(8,128)(2,1)}, u32[]{:S(2)}, u32[]{:S(2)}) collective-permute-start(bf16[2,27,16,256]{3,2,1,0:T(8,128)(2,1)S(1)} %collective-permute-done.5.refs_3_), channel_id=1, source_target_pairs={{0,4},{1,5},{2,6},{3,7},{4,8},{5,9},{6,10},{7,11},{8,12},{9,13},{1... | collective-permute-start | bytes 1327112 | tf_op jit(solution)/shard_map/ppermute | solution.py:261
  61.2 4.7 %collective-permute-start.8 = (bf16[2,27,16,256]{3,2,1,0:T(8,128)(2,1)}, bf16[2,27,16,256]{3,2,1,0:T(8,128)(2,1)}, u32[]{:S(2)}, u32[]{:S(2)}) collective-permute-start(bf16[2,27,16,256]{3,2,1,0:T(8,128)(2,1)} %collective-permute-done.6.refs_4_), channel_id=1, source_target_pairs={{0,4},{1,5},{2,6},{3,7},{4,8},{5,9},{6,10},{7,11},{8,12},{9,13},{1... | collective-permute-start | bytes 1327112 | tf_op jit(solution)/shard_map/ppermute | solution.py:261
  65.9 0.5 collective-permute-done.7.refs_5_
  66.4 5.2 %collective-permute-start.9 = (bf16[2,27,16,256]{3,2,1,0:T(8,128)(2,1)}, bf16[2,27,16,256]{3,2,1,0:T(8,128)(2,1)S(1)}, u32[]{:S(2)}, u32[]{:S(2)}) collective-permute-start(bf16[2,27,16,256]{3,2,1,0:T(8,128)(2,1)} %collective-permute-done.7.refs_5_), channel_id=1, source_target_pairs={{0,4},{1,5},{2,6},{3,7},{4,8},{5,9},{6,10},{7,11},{8,12},{9,13},{1... | collective-permute-start | bytes 1327112 | tf_op jit(solution)/shard_map/ppermute | solution.py:261
  71.6 0.1 all-to-all-done.1.x_ref
  71.7 3.4 %shard_map.93 = (bf16[3,4,6,64,256]{4,3,2,1,0:T(8,128)(2,1)S(1)}, bf16[4,4,64,384]{3,2,1,0:T(8,128)(2,1)S(1)}) custom-call(s32[10]{0:T(128)S(1)} %copy-done.6, f32[1,512]{1,0:T(1,128)S(1)} %bitcast.13, f32[1,512]{1,0:T(1,128)S(1)} %bitcast.14, f32[1,512]{1,0:T(1,128)S(1)} %bitcast.15, bf16[16,112,256]{2,1,0:T(8,128)(2,1)S(1)} %all-to-all-done.1.x_ref), custom_call_target="tpu_custom_call" | custom-call | flops 65536 | bytes 65536 | tf_op jit(solution)/shard_map/pallas_call | solution.py:300
  75.1 2.4 %shard_map.95.part_ref = f32[2,2,64,256]{3,2,1,0:T(8,128)S(1)} custom-call(bf16[3,4,6,64,256]{4,3,2,1,0:T(8,128)(2,1)S(1)} %get-tuple-element.14.act_ref, bf16[2,27,16,256]{3,2,1,0:T(8,128)(2,1)S(1)} %fusion.refs_0_, bf16[2,27,16,256]{3,2,1,0:T(8,128)(2,1)S(1)} %collective-permute-done.3.refs_1_, ...), custom_call_target="tpu_custom_call" | custom-call | flops 65536 | bytes 65536 | tf_op jit(solution)/shard_map/pallas_call | solution.py:349
  77.4 0.4 shard_map.96
  77.8 0.0 copy-start.4
  77.8 0.0 copy-start.5
  77.8 0.0 copy-start.7
  77.8 5.6 %collective-permute-start.10 = (f32[2,2,64,256]{3,2,1,0:T(8,128)S(1)}, f32[2,2,64,256]{3,2,1,0:T(8,128)S(1)}, u32[]{:S(2)}, u32[]{:S(2)}) collective-permute-start(f32[2,2,64,256]{3,2,1,0:T(8,128)S(1)} %shard_map.96), channel_id=1, source_target_pairs={{0,32},{1,33},{2,34},{3,35},{4,36},{5,37},{6,38},{7,39},{8,40},{9,... | collective-permute-start | bytes 786440 | tf_op jit(solution)/shard_map/ppermute | solution.py:261
  83.4 2.4 %shard_map.94.a_ref = f32[2,2,64,256]{3,2,1,0:T(8,128)S(1)} custom-call(bf16[3,4,6,64,256]{4,3,2,1,0:T(8,128)(2,1)S(1)} %get-tuple-element.14.act_ref, bf16[2,27,16,256]{3,2,1,0:T(8,128)(2,1)S(1)} %fusion.refs_0_, bf16[2,27,16,256]{3,2,1,0:T(8,128)(2,1)S(1)} %collective-permute-done.3.refs_1_, bf16[2,27,16,256]{3,2,1,0:T(8,128)(2,1)S(1)} %collective-permute-done.4.refs_2_, ...), custom_call_target="tpu_custom_call" | custom-call | flops 65536 | bytes 65536 | tf_op jit(solution)/shard_map/pallas_call | solution.py:349
  85.8 0.2 shard_map.97
  86.1 0.7 reshape.7
  (20 shorter events, 0.1 us)
Async XLA Ops:
  0.0 36.5 %copy-start = (bf16[1,4,2,32,512]{4,3,2,1,0:T(8,128)(2,1)S(1)}, bf16[1,4,2,32,512]{4,3,2,1,0:T(8,128)(2,1)}, u32[]{:S(2)}) copy-start(bf16[1,4,2,32,512]{4,3,2,1,0:T(8,128)(2,1)} %param.9) | copy-start | bytes 786436
  3.2 27.2 %collective-permute-start = (bf16[688,256]{1,0:T(8,128)(2,1)}, bf16[688,256]{1,0:T(8,128)(2,1)S(1)}, u32[]{:S(2)}, u32[]{:S(2)}) collective-permute-start(bf16[688,256]{1,0:T(8,128)(2,1)} %get-tuple-element.11), channel_id=1, source_target_pairs={{0,31},{1,0},{2,1},{3,2},{4,3},{5,4},{6,5},{7,6},{8,7},{9,8},{10,9... | collective-permute-start | bytes 1056776 | tf_op jit(solution)/shard_map/ppermute | solution.py:261
  7.1 23.3 %collective-permute-start.2 = (bf16[27,16,256]{2,1,0:T(8,128)(2,1)}, bf16[27,16,256]{2,1,0:T(8,128)(2,1)S(1)}, u32[]{:S(2)}, u32[]{:S(2)}) collective-permute-start(bf16[27,16,256]{2,1,0:T(8,128)(2,1)} %bitcast.21), channel_id=1, source_target_pairs={{32,62},{33,63},{34,32},{35,33},{36,34},{37,35},{38,36},{39,37},{4... | collective-permute-start | bytes 663560 | tf_op jit(solution)/shard_map/ppermute | solution.py:261
  20.0 16.6 %all-to-all-start = ((f32[32,8,128]{2,1,0:T(8,128)}), f32[32,8,128]{2,1,0:T(8,128)S(1)}, u32[]{:S(2)}, u32[]{:S(2)}) async-start(f32[32,8,128]{2,1,0:T(8,128)} %get-tuple-element.13), calls=%async_computation | async-start | bytes 262144 | tf_op jit(solution)/shard_map/all_to_all | solution.py:334
  23.8 12.7 %collective-permute-start.1 = (bf16[128,512]{1,0:T(8,128)(2,1)}, bf16[128,512]{1,0:T(8,128)(2,1)S(1)}, u32[]{:S(2)}, u32[]{:S(2)}) collective-permute-start(bf16[128,512]{1,0:T(8,128)(2,1)} %get-tuple-element.12), channel_id=1, source_target_pairs={{0,1},{1,2},{2,3},{3,4},{4,5},{5,6},{6,7},{7,8},{8,9},{9,10},{10,1... | collective-permute-start | bytes 393224 | tf_op jit(solution)/shard_map/ppermute | solution.py:261
  30.4 41.2 %copy-start.1 = (f32[512]{0:T(512)S(1)}, f32[512]{0:T(512)}, u32[]{:S(2)}) copy-start(f32[512]{0:T(512)} %param.10) | copy-start | bytes 6148
  30.5 41.2 %copy-start.2 = (f32[512]{0:T(512)S(1)}, f32[512]{0:T(512)}, u32[]{:S(2)}) copy-start(f32[512]{0:T(512)} %param.11) | copy-start | bytes 6148
  30.5 41.2 %copy-start.3 = (f32[512]{0:T(512)S(1)}, f32[512]{0:T(512)}, u32[]{:S(2)}) copy-start(f32[512]{0:T(512)} %param.12) | copy-start | bytes 6148
  30.5 41.2 %copy-start.6 = (s32[10]{0:T(128)S(1)}, s32[10]{0:T(128)}, u32[]{:S(2)}) copy-start(s32[10]{0:T(128)} %lengths_ref.1) | copy-start | bytes 124
  31.5 14.8 %collective-permute-start.4 = (bf16[2,27,16,256]{3,2,1,0:T(8,128)(2,1)S(1)}, bf16[2,27,16,256]{3,2,1,0:T(8,128)(2,1)S(1)}, u32[]{:S(2)}, u32[]{:S(2)}) collective-permute-start(bf16[2,27,16,256]{3,2,1,0:T(8,128)(2,1)S(1)} %fusion.refs_0_), channel_id=1, source_target_pairs={{0,60},{1,61},{2,62},{3,63},{4,32},{5,33},{6,34},{7,35},{8,36},{9,... | collective-permute-start | bytes 1327112 | tf_op jit(solution)/shard_map/ppermute | solution.py:261
  33.4 12.9 %collective-permute-start.3 = (bf16[2,27,16,256]{3,2,1,0:T(8,128)(2,1)S(1)}, bf16[2,27,16,256]{3,2,1,0:T(8,128)(2,1)S(1)}, u32[]{:S(2)}, u32[]{:S(2)}) collective-permute-start(bf16[2,27,16,256]{3,2,1,0:T(8,128)(2,1)S(1)} %fusion.refs_0_), channel_id=1, source_target_pairs={{0,4},{1,5},{2,6},{3,7},{4,8},{5,9},{6,10},{7,11},{8,12},{9,13},{1... | collective-permute-start | bytes 1327112 | tf_op jit(solution)/shard_map/ppermute | solution.py:261
  38.3 33.4 %all-to-all-start.1 = ((bf16[16,112,256]{2,1,0:T(8,128)(2,1)}), bf16[16,112,256]{2,1,0:T(8,128)(2,1)S(1)}, u32[]{:S(2)}, u32[]{:S(2)}) async-start(bf16[16,112,256]{2,1,0:T(8,128)(2,1)} %shard_map.92), calls=%async_computation.1 | async-start | bytes 1835008 | tf_op jit(solution)/shard_map/all_to_all | solution.py:341
  46.4 9.5 %collective-permute-start.5 = (bf16[2,27,16,256]{3,2,1,0:T(8,128)(2,1)S(1)}, bf16[2,27,16,256]{3,2,1,0:T(8,128)(2,1)S(1)}, u32[]{:S(2)}, u32[]{:S(2)}) collective-permute-start(bf16[2,27,16,256]{3,2,1,0:T(8,128)(2,1)S(1)} %collective-permute-done.3.refs_1_), channel_id=1, source_target_pairs={{0,4},{1,5},{2,6},{3,7},{4,8},{5,9},{6,10},{7,11},{8,12},{9,13},{1... | collective-permute-start | bytes 1327112 | tf_op jit(solution)/shard_map/ppermute | solution.py:261
  50.6 10.5 %collective-permute-start.6 = (bf16[2,27,16,256]{3,2,1,0:T(8,128)(2,1)S(1)}, bf16[2,27,16,256]{3,2,1,0:T(8,128)(2,1)}, u32[]{:S(2)}, u32[]{:S(2)}) collective-permute-start(bf16[2,27,16,256]{3,2,1,0:T(8,128)(2,1)S(1)} %collective-permute-done.4.refs_2_), channel_id=1, source_target_pairs={{0,4},{1,5},{2,6},{3,7},{4,8},{5,9},{6,10},{7,11},{8,12},{9,13},{1... | collective-permute-start | bytes 1327112 | tf_op jit(solution)/shard_map/ppermute | solution.py:261
  55.9 10.5 %collective-permute-start.7 = (bf16[2,27,16,256]{3,2,1,0:T(8,128)(2,1)S(1)}, bf16[2,27,16,256]{3,2,1,0:T(8,128)(2,1)}, u32[]{:S(2)}, u32[]{:S(2)}) collective-permute-start(bf16[2,27,16,256]{3,2,1,0:T(8,128)(2,1)S(1)} %collective-permute-done.5.refs_3_), channel_id=1, source_target_pairs={{0,4},{1,5},{2,6},{3,7},{4,8},{5,9},{6,10},{7,11},{8,12},{9,13},{1... | collective-permute-start | bytes 1327112 | tf_op jit(solution)/shard_map/ppermute | solution.py:261
  61.2 13.9 %collective-permute-start.8 = (bf16[2,27,16,256]{3,2,1,0:T(8,128)(2,1)}, bf16[2,27,16,256]{3,2,1,0:T(8,128)(2,1)}, u32[]{:S(2)}, u32[]{:S(2)}) collective-permute-start(bf16[2,27,16,256]{3,2,1,0:T(8,128)(2,1)} %collective-permute-done.6.refs_4_), channel_id=1, source_target_pairs={{0,4},{1,5},{2,6},{3,7},{4,8},{5,9},{6,10},{7,11},{8,12},{9,13},{1... | collective-permute-start | bytes 1327112 | tf_op jit(solution)/shard_map/ppermute | solution.py:261
  66.4 11.0 %collective-permute-start.9 = (bf16[2,27,16,256]{3,2,1,0:T(8,128)(2,1)}, bf16[2,27,16,256]{3,2,1,0:T(8,128)(2,1)S(1)}, u32[]{:S(2)}, u32[]{:S(2)}) collective-permute-start(bf16[2,27,16,256]{3,2,1,0:T(8,128)(2,1)} %collective-permute-done.7.refs_5_), channel_id=1, source_target_pairs={{0,4},{1,5},{2,6},{3,7},{4,8},{5,9},{6,10},{7,11},{8,12},{9,13},{1... | collective-permute-start | bytes 1327112 | tf_op jit(solution)/shard_map/ppermute | solution.py:261
  77.8 8.0 %copy-start.4 = (f32[256]{0:T(256)S(1)}, f32[256]{0:T(256)}, u32[]{:S(2)}) copy-start(f32[256]{0:T(256)} %param.14) | copy-start | bytes 3076
  77.8 8.0 %copy-start.5 = (f32[256]{0:T(256)S(1)}, f32[256]{0:T(256)}, u32[]{:S(2)}) copy-start(f32[256]{0:T(256)} %param.15) | copy-start | bytes 3076
  77.8 8.0 %copy-start.7 = (s32[64]{0:T(128)S(1)}, s32[64]{0:T(128)}, u32[]{:S(2)}) copy-start(s32[64]{0:T(128)} %param.17) | copy-start | bytes 772
  77.8 8.0 %collective-permute-start.10 = (f32[2,2,64,256]{3,2,1,0:T(8,128)S(1)}, f32[2,2,64,256]{3,2,1,0:T(8,128)S(1)}, u32[]{:S(2)}, u32[]{:S(2)}) collective-permute-start(f32[2,2,64,256]{3,2,1,0:T(8,128)S(1)} %shard_map.96), channel_id=1, source_target_pairs={{0,32},{1,33},{2,34},{3,35},{4,36},{5,37},{6,38},{7,39},{8,40},{9,... | collective-permute-start | bytes 786440 | tf_op jit(solution)/shard_map/ppermute | solution.py:261

commit v7 on v6

--- a/solution.py
+++ b/solution.py
@@ -148,17 +148,38 @@
     return start
 
 
-def activate(lengths_ref, gamma_ref, beta_ref, smooth_ref, x_ref, act_ref, last_ref):
-    y, core, s = lax.axis_index("y"), lax.axis_index("core"), lax.axis_index("z") * NX + lax.axis_index("x")
+def tables(lengths_ref, gamma_ref, beta_ref, smooth_ref, rows_ref, earlier_ref, means_ref, squares_ref, pick_ref, group_ref, affine_ref):
+    core, s = lax.axis_index("core"), lax.axis_index("z") * NX + lax.axis_index("x")
     n = 2 * T
-    thirds = x_ref[:, 96:112, :].astype(F32)[:, :8, :128].reshape(n, 128)
     rows, columns = iota((n, 1), 0), iota((1, n), 1)
     frame_a, frame_b = (rows >> 3) * FR + (rows & 3), (columns >> 3) * FR + (columns & 3)
     same = starts(lengths_ref, frame_a) == starts(lengths_ref, frame_b)
     means_b = (columns & 4) == 0
-    on_means, on_squares = same & means_b, flag(same & jnp.logical_not(means_b))
+    means_ref[...] = flag(same & means_b)
+    squares_ref[...] = flag(same & jnp.logical_not(means_b))
+    pick_ref[...] = flag((frame_b == iota((T, 1), 0)) & means_b)
+    channels = channel_at(s, core, iota((1, HALF), 1))
+    mine = flag(iota((C, HALF), 0) == channels)
+    third = iota((128, 1), 0)
+    group_ref[...] = flag(((third & (GROUPS - 1)) == (channels >> 4)) & (third < 3 * GROUPS))
+    affine = take(jnp.concatenate([gamma_ref[...], beta_ref[...], smooth_ref[...]], axis=0), mine)
+    affine_ref[...] = jnp.concatenate([affine[:2], 1.0 / affine[2:3], jnp.zeros((5, HALF), F32)], axis=0)
+    m = 16 * 16
+    to = iota((m, 1), 0)
+    row, t = to >> 6, to & (T - 1)
+    rows_ref[...] = flag(iota((m, m), 1) == (t >> 2) * 16 + row * FR + (t & 3))
+    frame, other = iota((T, 1), 0), iota((T, T), 1)
+    start = starts(lengths_ref, frame)
+    earlier = [flag(other == jnp.maximum(frame - back, start)) for back in (2, 1)]
+    earlier_ref[...] = jnp.concatenate(earlier, axis=0)
+
+
+def activate(rows_ref, earlier_ref, means_ref, squares_ref, pick_ref, group_ref, affine_ref, x_ref, act_ref, last_ref):
+    y, s = lax.axis_index("y"), lax.axis_index("z") * NX + lax.axis_index("x")
+    n = 2 * T
+    thirds = x_ref[:, 96:112, :].astype(F32)[:, :8, :128].reshape(n, 128)
+    on_means, on_squares, pick, to_group = means_ref[...], squares_ref[...], pick_ref[...], group_ref[...]
     count = jnp.sum(on_means.astype(F32), axis=1, keepdims=True)
-    on_means = flag(on_means)
 
     def whole(v):
         return v[:, :GROUPS] + v[:, GROUPS : 2 * GROUPS] + v[:, 2 * GROUPS : 3 * GROUPS]
@@ -170,24 +191,12 @@
     off = whole(thirds) - mean
     squares = whole(bdot(on_squares, thirds.astype(BF16))) + FRAME_CELLS * whole(bdot(on_means, parts(off * off)))
     inverse = lax.rsqrt(squares / (count * FRAME_CELLS) + 1e-6)
-    pick = flag((frame_b == iota((T, 1), 0)) & means_b)
-    channels = channel_at(s, core, iota((1, HALF), 1))
-    mine = flag(iota((C, HALF), 0) == channels)
-    third = iota((128, 1), 0)
-    to_group = flag(((third & (GROUPS - 1)) == (channels >> 4)) & (third < 3 * GROUPS))
-    affine = take(jnp.concatenate([gamma_ref[...], beta_ref[...], smooth_ref[...]], axis=0), mine)
-    gamma, beta, unsmooth = affine[0:1], affine[1:2], 1.0 / affine[2:3]
+    gamma, beta, unsmooth = affine_ref[0:1], affine_ref[1:2], affine_ref[2:3]
     mean = bdot(bdot(pick, parts(mean)).astype(BF16), to_group)
     scale = bdot(bdot(pick, parts(inverse)).astype(BF16), to_group) * gamma
 
     m = 16 * 16
-    to = iota((m, 1), 0)
-    row, t = to >> 6, to & (T - 1)
-    by_row = flag(iota((m, m), 1) == (t >> 2) * 16 + row * FR + (t & 3))
-    frame, other = iota((T, 1), 0), iota((T, T), 1)
-    start = starts(lengths_ref, frame)
-    earlier = [flag(other == jnp.maximum(frame - back, start)) for back in (2, 1)]
-    earlier = jnp.concatenate(earlier, axis=0)
+    by_row, earlier = rows_ref[...], earlier_ref[...]
     for c in range(6):
         rows = x_ref[:, 16 * c : 16 * (c + 1), :].reshape(m, HALF)
         values = bdot(by_row, rows)
@@ -296,10 +305,19 @@
     )(*args)
 
 
+def call_tables(*args):
+    shapes = (2 * HALF // 2, HALF), (2 * T, T), (2 * T, 2 * T), (2 * T, 2 * T), (T, 2 * T), (128, HALF)
+    return pl.pallas_call(
+        tables, out_shape=tuple(struct(shape, BF16) for shape in shapes) + (struct((8, HALF), F32),),
+        in_specs=[SMEM] + [VMEM] * 3, out_specs=(VMEM,) * 7, compiler_params=params(16),
+        cost_estimate=cost(2**16, 2**16),
+    )(*args)
+
+
 def call_activate(*args):
     return pl.pallas_call(
         activate, out_shape=(struct((3, 4, 6, T, HALF), BF16), struct((4, 4, T, LAST), BF16)),
-        in_specs=[SMEM] + [VMEM] * 4, out_specs=(VMEM, VMEM),
+        in_specs=[VMEM] * 8, out_specs=(VMEM, VMEM),
         compiler_params=params(), cost_estimate=cost(2**16, 2**16),
     )(*args)
 
@@ -340,8 +358,10 @@
     windows = call_pack(latent, beside, edge, gathered)
     columns = lax.all_to_all(windows, ("y", "core"), 0, 0, tiled=True)
     a2, b2 = ring(lax.optimization_barrier((a1, b1))[0]), ring(b1)
+    known = call_tables(lengths, gamma[None], beta[None], smooth[None])
+    a2, known = lax.optimization_barrier((a2, known))
     a3, b3 = ring(a2), ring(b2)
-    act, last = call_activate(lengths, gamma[None], beta[None], smooth[None], columns)
+    act, last = call_activate(*known, columns)
     a4 = ring(a3)
 
 

time: 87.5 us -> 87.5 us (level)
  transfers between devices with their start and end apart: 13 -> 13, of which waited for: 3 -> 4; matrix products, arithmetic and copies ran while one was open for 1% -> 1% of each run, Pallas kernels for 11% -> 12%
where the time goes in v7:
time: 87.5 us; the launch traced here: 86.8 us
  starting transfers between devices  67.6 us (77%)
  Pallas kernels  13.8 us (16%)
  waiting for transfers between devices  3.29 us (4%)
  other arithmetic  1.01 us (1%)
    ppermute x11, starting transfers between devices, shift(): return lax.ppermute(value, AXES, pairs)  55.6 us
    all_to_all x1, starting transfers between devices, local(): columns = lax.all_to_all(windows, ('y', 'core'), 0, 0, tiled=True)  8.09 us
    pallas_call x3, Pallas kernels, part(): pl.pallas_call(kernel, out_shape=struct((2, 2, T, CO), F32), in_specs=[VM...  5.07 us
    all_to_all x1, starting transfers between devices, local(): gathered = lax.all_to_all(spread, ('z', 'x'), 0, 0, tiled=True)  3.87 us
    ppermute x11, waiting for transfers between devices, shift(): return lax.ppermute(value, AXES, pairs)  3.22 us
    pallas_call x1, Pallas kernels, call_prepare(): pl.pallas_call(prepare, out_shape=(struct((NZ * NX, 8, 128), F32), struct...  3.14 us
    pallas_call x1, Pallas kernels, call_activate(): pl.pallas_call(activate, out_shape=(struct((3, 4, 6, T, HALF), BF16), str...  2.77 us
  transfers between devices with their start and end apart: 13, of which 4 were waited for; matrix products, arithmetic and copies ran while one was open for 1% of the time, Pallas kernels for 12%

profile of v7, /device:TPU:1, one launch (start us, length us, event | category | flops | bytes accessed | tf_op | source)
XLA Modules:
  0.0 86.8 jit_solution(11080193983923637076)
XLA Ops:
  0.0 3.1 %shard_map.91 = (f32[32,8,128]{2,1,0:T(8,128)}, bf16[688,256]{1,0:T(8,128)(2,1)}, bf16[128,512]{1,0:T(8,128)(2,1)}) custom-call(bf16[4,2,32,512]{3,2,1,0:T(8,128)(2,1)} %bitcast.11, bf16[27,16,256]{2,1,0:T(8,128)(2,1)} %bitcast.20), custom_call_target="tpu_custom_call" | custom-call | flops 65536 | bytes 65536 | tf_op jit(solution)/shard_map/pallas_call | solution.py:290
  3.2 3.9 %collective-permute-start = (bf16[688,256]{1,0:T(8,128)(2,1)}, bf16[688,256]{1,0:T(8,128)(2,1)S(1)}, u32[]{:S(2)}, u32[]{:S(2)}) collective-permute-start(bf16[688,256]{1,0:T(8,128)(2,1)} %get-tuple-element.26), channel_id=1, source_target_pairs={{0,31},{1,0},{2,1},{3,2},{4,3},{5,4},{6,5},{7,6},{8,7},{9,8},{10,9... | collective-permute-start | bytes 1056776 | tf_op jit(solution)/shard_map/ppermute | solution.py:270
  7.1 12.8 %collective-permute-start.1 = (bf16[27,16,256]{2,1,0:T(8,128)(2,1)}, bf16[27,16,256]{2,1,0:T(8,128)(2,1)S(1)}, u32[]{:S(2)}, u32[]{:S(2)}) collective-permute-start(bf16[27,16,256]{2,1,0:T(8,128)(2,1)} %bitcast.21), channel_id=1, source_target_pairs={{32,62},{33,63},{34,32},{35,33},{36,34},{37,35},{38,36},{39,37},{4... | collective-permute-start | bytes 663560 | tf_op jit(solution)/shard_map/ppermute | solution.py:270
  20.0 3.9 %all-to-all-start = ((f32[32,8,128]{2,1,0:T(8,128)}), f32[32,8,128]{2,1,0:T(8,128)S(1)}, u32[]{:S(2)}, u32[]{:S(2)}) async-start(f32[32,8,128]{2,1,0:T(8,128)} %get-tuple-element.43), calls=%async_computation | async-start | bytes 262144 | tf_op jit(solution)/shard_map/all_to_all | solution.py:352
  23.8 6.6 %collective-permute-start.5 = (bf16[128,512]{1,0:T(8,128)(2,1)}, bf16[128,512]{1,0:T(8,128)(2,1)S(1)}, u32[]{:S(2)}, u32[]{:S(2)}) collective-permute-start(bf16[128,512]{1,0:T(8,128)(2,1)} %get-tuple-element.42), channel_id=1, source_target_pairs={{0,1},{1,2},{2,3},{3,4},{4,5},{5,6},{6,7},{7,8},{8,9},{9,10},{10,1... | collective-permute-start | bytes 393224 | tf_op jit(solution)/shard_map/ppermute | solution.py:270
  30.4 0.0 copy-start.1
  30.5 0.0 copy-start.2
  30.5 0.0 copy-start.3
  30.5 0.0 copy-start.6
  30.5 1.0 %fusion.refs_0_ = bf16[2,27,16,256]{3,2,1,0:T(8,128)(2,1)S(1)} fusion(bf16[1,27,16,256]{3,2,1,0:T(8,128)(2,1)S(1)} %bitcast.19, bf16[1,27,16,256]{3,2,1,0:T(8,128)(2,1)} %bitcast.22, bf16[1,27,16,256]{3,2,1,0:T(8,128)(2,1)S(1)} %bitcast.23, pred[]{:T(512)S(6)} %eq.3), kind=kLoop, calls=%fused_computation.2 | loop fusion | flops 663552 | bytes 1105921 | tf_op jit(solution)/shard_map/jit(_where)/select_n | solution.py:355
  31.5 1.9 %collective-permute-start.3 = (bf16[2,27,16,256]{3,2,1,0:T(8,128)(2,1)S(1)}, bf16[2,27,16,256]{3,2,1,0:T(8,128)(2,1)S(1)}, u32[]{:S(2)}, u32[]{:S(2)}) collective-permute-start(bf16[2,27,16,256]{3,2,1,0:T(8,128)(2,1)S(1)} %fusion.refs_0_), channel_id=1, source_target_pairs={{0,60},{1,61},{2,62},{3,63},{4,32},{5,33},{6,34},{7,35},{8,36},{9,... | collective-permute-start | bytes 1327112 | tf_op jit(solution)/shard_map/ppermute | solution.py:270
  33.4 3.1 %collective-permute-start.2 = (bf16[2,27,16,256]{3,2,1,0:T(8,128)(2,1)S(1)}, bf16[2,27,16,256]{3,2,1,0:T(8,128)(2,1)S(1)}, u32[]{:S(2)}, u32[]{:S(2)}) collective-permute-start(bf16[2,27,16,256]{3,2,1,0:T(8,128)(2,1)S(1)} %fusion.refs_0_), channel_id=1, source_target_pairs={{0,4},{1,5},{2,6},{3,7},{4,8},{5,9},{6,10},{7,11},{8,12},{9,13},{1... | collective-permute-start | bytes 1327112 | tf_op jit(solution)/shard_map/ppermute | solution.py:270
  36.5 1.7 %shard_map.93 = bf16[16,112,256]{2,1,0:T(8,128)(2,1)} custom-call(bf16[4,2,32,512]{3,2,1,0:T(8,128)(2,1)S(1)} %bitcast.12, bf16[688,256]{1,0:T(8,128)(2,1)S(1)} %collective-permute-done.beside_ref, bf16[128,512]{1,0:T(8,128)(2,1)S(1)} %collective-permute-done.5.edge_ref, f32[32,8,128]{2,1,0:T(8,128)S(1)} %all-to-all-done.sums_ref), custom_call_target="tpu_custom_call" | custom-call | flops 65536 | bytes 65536 | tf_op jit(solution)/shard_map/pallas_call | solution.py:302
  38.3 8.1 %all-to-all-start.1 = ((bf16[16,112,256]{2,1,0:T(8,128)(2,1)}), bf16[16,112,256]{2,1,0:T(8,128)(2,1)S(1)}, u32[]{:S(2)}, u32[]{:S(2)}) async-start(bf16[16,112,256]{2,1,0:T(8,128)(2,1)} %shard_map.93), calls=%async_computation.1 | async-start | bytes 1835008 | tf_op jit(solution)/shard_map/all_to_all | solution.py:359
  46.4 4.3 %collective-permute-start.4 = (bf16[2,27,16,256]{3,2,1,0:T(8,128)(2,1)S(1)}, bf16[2,27,16,256]{3,2,1,0:T(8,128)(2,1)S(1)}, u32[]{:S(2)}, u32[]{:S(2)}) collective-permute-start(bf16[2,27,16,256]{3,2,1,0:T(8,128)(2,1)S(1)} %collective-permute-done.2.refs_1_), channel_id=1, source_target_pairs={{0,4},{1,5},{2,6},{3,7},{4,8},{5,9},{6,10},{7,11},{8,12},{9,13},{1... | collective-permute-start | bytes 1327112 | tf_op jit(solution)/shard_map/ppermute | solution.py:270
  50.7 0.9 shard_map.92
  51.6 1.9 %collective-permute-start.6 = (bf16[2,27,16,256]{3,2,1,0:T(8,128)(2,1)S(1)}, bf16[2,27,16,256]{3,2,1,0:T(8,128)(2,1)}, u32[]{:S(2)}, u32[]{:S(2)}) collective-permute-start(bf16[2,27,16,256]{3,2,1,0:T(8,128)(2,1)S(1)} %collective-permute-done.3.refs_2_), channel_id=1, source_target_pairs={{0,4},{1,5},{2,6},{3,7},{4,8},{5,9},{6,10},{7,11},{8,12},{9,13},{1... | collective-permute-start | bytes 1327112 | tf_op jit(solution)/shard_map/ppermute | solution.py:270
  53.5 2.4 %collective-permute-done.4.refs_3_ = bf16[2,27,16,256]{3,2,1,0:T(8,128)(2,1)S(1)} collective-permute-done((bf16[2,27,16,256]{3,2,1,0:T(8,128)(2,1)S(1)}, bf16[2,27,16,256]{3,2,1,0:T(8,128)(2,1)S(1)}, u32[]{:S(2)}, u32[]{:S(2)}) %collective-permute-start.4) | collective-permute-done | bytes 442400 | tf_op jit(solution)/shard_map/ppermute | solution.py:270
  55.9 5.3 %collective-permute-start.7 = (bf16[2,27,16,256]{3,2,1,0:T(8,128)(2,1)S(1)}, bf16[2,27,16,256]{3,2,1,0:T(8,128)(2,1)}, u32[]{:S(2)}, u32[]{:S(2)}) collective-permute-start(bf16[2,27,16,256]{3,2,1,0:T(8,128)(2,1)S(1)} %collective-permute-done.4.refs_3_), channel_id=1, source_target_pairs={{0,4},{1,5},{2,6},{3,7},{4,8},{5,9},{6,10},{7,11},{8,12},{9,13},{1... | collective-permute-start | bytes 1327112 | tf_op jit(solution)/shard_map/ppermute | solution.py:270
  61.2 4.7 %collective-permute-start.8 = (bf16[2,27,16,256]{3,2,1,0:T(8,128)(2,1)}, bf16[2,27,16,256]{3,2,1,0:T(8,128)(2,1)}, u32[]{:S(2)}, u32[]{:S(2)}) collective-permute-start(bf16[2,27,16,256]{3,2,1,0:T(8,128)(2,1)} %collective-permute-done.6.refs_4_), channel_id=1, source_target_pairs={{0,4},{1,5},{2,6},{3,7},{4,8},{5,9},{6,10},{7,11},{8,12},{9,13},{1... | collective-permute-start | bytes 1327112 | tf_op jit(solution)/shard_map/ppermute | solution.py:270
  65.9 0.5 collective-permute-done.7.refs_5_
  66.4 5.2 %collective-permute-start.9 = (bf16[2,27,16,256]{3,2,1,0:T(8,128)(2,1)}, bf16[2,27,16,256]{3,2,1,0:T(8,128)(2,1)S(1)}, u32[]{:S(2)}, u32[]{:S(2)}) collective-permute-start(bf16[2,27,16,256]{3,2,1,0:T(8,128)(2,1)} %collective-permute-done.7.refs_5_), channel_id=1, source_target_pairs={{0,4},{1,5},{2,6},{3,7},{4,8},{5,9},{6,10},{7,11},{8,12},{9,13},{1... | collective-permute-start | bytes 1327112 | tf_op jit(solution)/shard_map/ppermute | solution.py:270
  71.6 0.1 all-to-all-done.1.x_ref
  71.7 2.8 %shard_map.94 = (bf16[3,4,6,64,256]{4,3,2,1,0:T(8,128)(2,1)S(1)}, bf16[4,4,64,384]{3,2,1,0:T(8,128)(2,1)S(1)}) custom-call(bf16[256,256]{1,0:T(8,128)(2,1)S(1)} %get-tuple-element.35.rows_ref, bf16[128,64]{1,0:T(8,128)(2,1)S(1)} %get-tuple-element.36.earlier_ref, bf16[128,128]{1,0:T(8,128)(2,1)S(1)} %get-tuple-element.37.means_ref, ...), custom_call_target="tpu_custom_call" | custom-call | flops 65536 | bytes 65536 | tf_op jit(solution)/shard_map/pallas_call | solution.py:318
  74.4 2.4 %shard_map.96.part_ref = f32[2,2,64,256]{3,2,1,0:T(8,128)S(1)} custom-call(bf16[3,4,6,64,256]{4,3,2,1,0:T(8,128)(2,1)S(1)} %get-tuple-element.44.act_ref, bf16[2,27,16,256]{3,2,1,0:T(8,128)(2,1)S(1)} %fusion.refs_0_, bf16[2,27,16,256]{3,2,1,0:T(8,128)(2,1)S(1)} %collective-permute-done.2.refs_1_, ...), custom_call_target="tpu_custom_call" | custom-call | flops 65536 | bytes 65536 | tf_op jit(solution)/shard_map/pallas_call | solution.py:369
  76.8 0.3 collective-permute-done.9.refs_7_.w_ref
  77.1 0.3 shard_map.97
  77.5 0.0 copy-start.4
  77.5 5.9 %collective-permute-start.10 = (f32[2,2,64,256]{3,2,1,0:T(8,128)S(1)}, f32[2,2,64,256]{3,2,1,0:T(8,128)S(1)}, u32[]{:S(2)}, u32[]{:S(2)}) collective-permute-start(f32[2,2,64,256]{3,2,1,0:T(8,128)S(1)} %shard_map.97), channel_id=1, source_target_pairs={{0,32},{1,33},{2,34},{3,35},{4,36},{5,37},{6,38},{7,39},{8,40},{9,... | collective-permute-start | bytes 786440 | tf_op jit(solution)/shard_map/ppermute | solution.py:270
  83.4 2.4 %shard_map.95.a_ref = f32[2,2,64,256]{3,2,1,0:T(8,128)S(1)} custom-call(bf16[3,4,6,64,256]{4,3,2,1,0:T(8,128)(2,1)S(1)} %get-tuple-element.44.act_ref, bf16[2,27,16,256]{3,2,1,0:T(8,128)(2,1)S(1)} %fusion.refs_0_, bf16[2,27,16,256]{3,2,1,0:T(8,128)(2,1)S(1)} %collective-permute-done.2.refs_1_, bf16[2,27,16,256]{3,2,1,0:T(8,128)(2,1)S(1)} %collective-permute-done.3.refs_2_, ...), custom_call_target="tpu_custom_call" | custom-call | flops 65536 | bytes 65536 | tf_op jit(solution)/shard_map/pallas_call | solution.py:369
  85.9 0.2 shard_map.98
  86.1 0.7 reshape.7
  (21 shorter events, 0.1 us)
Async XLA Ops:
  0.0 36.5 %copy-start = (bf16[1,4,2,32,512]{4,3,2,1,0:T(8,128)(2,1)S(1)}, bf16[1,4,2,32,512]{4,3,2,1,0:T(8,128)(2,1)}, u32[]{:S(2)}) copy-start(bf16[1,4,2,32,512]{4,3,2,1,0:T(8,128)(2,1)} %param.9) | copy-start | bytes 786436
  3.2 27.2 %collective-permute-start = (bf16[688,256]{1,0:T(8,128)(2,1)}, bf16[688,256]{1,0:T(8,128)(2,1)S(1)}, u32[]{:S(2)}, u32[]{:S(2)}) collective-permute-start(bf16[688,256]{1,0:T(8,128)(2,1)} %get-tuple-element.26), channel_id=1, source_target_pairs={{0,31},{1,0},{2,1},{3,2},{4,3},{5,4},{6,5},{7,6},{8,7},{9,8},{10,9... | collective-permute-start | bytes 1056776 | tf_op jit(solution)/shard_map/ppermute | solution.py:270
  7.1 23.3 %collective-permute-start.1 = (bf16[27,16,256]{2,1,0:T(8,128)(2,1)}, bf16[27,16,256]{2,1,0:T(8,128)(2,1)S(1)}, u32[]{:S(2)}, u32[]{:S(2)}) collective-permute-start(bf16[27,16,256]{2,1,0:T(8,128)(2,1)} %bitcast.21), channel_id=1, source_target_pairs={{32,62},{33,63},{34,32},{35,33},{36,34},{37,35},{38,36},{39,37},{4... | collective-permute-start | bytes 663560 | tf_op jit(solution)/shard_map/ppermute | solution.py:270
  20.0 16.6 %all-to-all-start = ((f32[32,8,128]{2,1,0:T(8,128)}), f32[32,8,128]{2,1,0:T(8,128)S(1)}, u32[]{:S(2)}, u32[]{:S(2)}) async-start(f32[32,8,128]{2,1,0:T(8,128)} %get-tuple-element.43), calls=%async_computation | async-start | bytes 262144 | tf_op jit(solution)/shard_map/all_to_all | solution.py:352
  23.8 12.7 %collective-permute-start.5 = (bf16[128,512]{1,0:T(8,128)(2,1)}, bf16[128,512]{1,0:T(8,128)(2,1)S(1)}, u32[]{:S(2)}, u32[]{:S(2)}) collective-permute-start(bf16[128,512]{1,0:T(8,128)(2,1)} %get-tuple-element.42), channel_id=1, source_target_pairs={{0,1},{1,2},{2,3},{3,4},{4,5},{5,6},{6,7},{7,8},{8,9},{9,10},{10,1... | collective-permute-start | bytes 393224 | tf_op jit(solution)/shard_map/ppermute | solution.py:270
  30.4 20.2 %copy-start.1 = (f32[512]{0:T(512)S(1)}, f32[512]{0:T(512)}, u32[]{:S(2)}) copy-start(f32[512]{0:T(512)} %param.10) | copy-start | bytes 6148
  30.5 20.2 %copy-start.2 = (f32[512]{0:T(512)S(1)}, f32[512]{0:T(512)}, u32[]{:S(2)}) copy-start(f32[512]{0:T(512)} %param.11) | copy-start | bytes 6148
  30.5 20.2 %copy-start.3 = (f32[512]{0:T(512)S(1)}, f32[512]{0:T(512)}, u32[]{:S(2)}) copy-start(f32[512]{0:T(512)} %param.12) | copy-start | bytes 6148
  30.5 20.2 %copy-start.6 = (s32[10]{0:T(128)S(1)}, s32[10]{0:T(128)}, u32[]{:S(2)}) copy-start(s32[10]{0:T(128)} %lengths_ref.1) | copy-start | bytes 124
  31.5 14.9 %collective-permute-start.3 = (bf16[2,27,16,256]{3,2,1,0:T(8,128)(2,1)S(1)}, bf16[2,27,16,256]{3,2,1,0:T(8,128)(2,1)S(1)}, u32[]{:S(2)}, u32[]{:S(2)}) collective-permute-start(bf16[2,27,16,256]{3,2,1,0:T(8,128)(2,1)S(1)} %fusion.refs_0_), channel_id=1, source_target_pairs={{0,60},{1,61},{2,62},{3,63},{4,32},{5,33},{6,34},{7,35},{8,36},{9,... | collective-permute-start | bytes 1327112 | tf_op jit(solution)/shard_map/ppermute | solution.py:270
  33.4 12.9 %collective-permute-start.2 = (bf16[2,27,16,256]{3,2,1,0:T(8,128)(2,1)S(1)}, bf16[2,27,16,256]{3,2,1,0:T(8,128)(2,1)S(1)}, u32[]{:S(2)}, u32[]{:S(2)}) collective-permute-start(bf16[2,27,16,256]{3,2,1,0:T(8,128)(2,1)S(1)} %fusion.refs_0_), channel_id=1, source_target_pairs={{0,4},{1,5},{2,6},{3,7},{4,8},{5,9},{6,10},{7,11},{8,12},{9,13},{1... | collective-permute-start | bytes 1327112 | tf_op jit(solution)/shard_map/ppermute | solution.py:270
  38.3 33.4 %all-to-all-start.1 = ((bf16[16,112,256]{2,1,0:T(8,128)(2,1)}), bf16[16,112,256]{2,1,0:T(8,128)(2,1)S(1)}, u32[]{:S(2)}, u32[]{:S(2)}) async-start(bf16[16,112,256]{2,1,0:T(8,128)(2,1)} %shard_map.93), calls=%async_computation.1 | async-start | bytes 1835008 | tf_op jit(solution)/shard_map/all_to_all | solution.py:359
  46.4 9.5 %collective-permute-start.4 = (bf16[2,27,16,256]{3,2,1,0:T(8,128)(2,1)S(1)}, bf16[2,27,16,256]{3,2,1,0:T(8,128)(2,1)S(1)}, u32[]{:S(2)}, u32[]{:S(2)}) collective-permute-start(bf16[2,27,16,256]{3,2,1,0:T(8,128)(2,1)S(1)} %collective-permute-done.2.refs_1_), channel_id=1, source_target_pairs={{0,4},{1,5},{2,6},{3,7},{4,8},{5,9},{6,10},{7,11},{8,12},{9,13},{1... | collective-permute-start | bytes 1327112 | tf_op jit(solution)/shard_map/ppermute | solution.py:270
  51.6 9.6 %collective-permute-start.6 = (bf16[2,27,16,256]{3,2,1,0:T(8,128)(2,1)S(1)}, bf16[2,27,16,256]{3,2,1,0:T(8,128)(2,1)}, u32[]{:S(2)}, u32[]{:S(2)}) collective-permute-start(bf16[2,27,16,256]{3,2,1,0:T(8,128)(2,1)S(1)} %collective-permute-done.3.refs_2_), channel_id=1, source_target_pairs={{0,4},{1,5},{2,6},{3,7},{4,8},{5,9},{6,10},{7,11},{8,12},{9,13},{1... | collective-permute-start | bytes 1327112 | tf_op jit(solution)/shard_map/ppermute | solution.py:270
  55.9 10.5 %collective-permute-start.7 = (bf16[2,27,16,256]{3,2,1,0:T(8,128)(2,1)S(1)}, bf16[2,27,16,256]{3,2,1,0:T(8,128)(2,1)}, u32[]{:S(2)}, u32[]{:S(2)}) collective-permute-start(bf16[2,27,16,256]{3,2,1,0:T(8,128)(2,1)S(1)} %collective-permute-done.4.refs_3_), channel_id=1, source_target_pairs={{0,4},{1,5},{2,6},{3,7},{4,8},{5,9},{6,10},{7,11},{8,12},{9,13},{1... | collective-permute-start | bytes 1327112 | tf_op jit(solution)/shard_map/ppermute | solution.py:270
  61.2 13.2 %collective-permute-start.8 = (bf16[2,27,16,256]{3,2,1,0:T(8,128)(2,1)}, bf16[2,27,16,256]{3,2,1,0:T(8,128)(2,1)}, u32[]{:S(2)}, u32[]{:S(2)}) collective-permute-start(bf16[2,27,16,256]{3,2,1,0:T(8,128)(2,1)} %collective-permute-done.6.refs_4_), channel_id=1, source_target_pairs={{0,4},{1,5},{2,6},{3,7},{4,8},{5,9},{6,10},{7,11},{8,12},{9,13},{1... | collective-permute-start | bytes 1327112 | tf_op jit(solution)/shard_map/ppermute | solution.py:270
  66.4 10.7 %collective-permute-start.9 = (bf16[2,27,16,256]{3,2,1,0:T(8,128)(2,1)}, bf16[2,27,16,256]{3,2,1,0:T(8,128)(2,1)S(1)}, u32[]{:S(2)}, u32[]{:S(2)}) collective-permute-start(bf16[2,27,16,256]{3,2,1,0:T(8,128)(2,1)} %collective-permute-done.7.refs_5_), channel_id=1, source_target_pairs={{0,4},{1,5},{2,6},{3,7},{4,8},{5,9},{6,10},{7,11},{8,12},{9,13},{1... | collective-permute-start | bytes 1327112 | tf_op jit(solution)/shard_map/ppermute | solution.py:270
  77.5 8.3 %copy-start.4 = (f32[256]{0:T(256)S(1)}, f32[256]{0:T(256)}, u32[]{:S(2)}) copy-start(f32[256]{0:T(256)} %param.14) | copy-start | bytes 3076
  77.5 8.3 %copy-start.5 = (f32[256]{0:T(256)S(1)}, f32[256]{0:T(256)}, u32[]{:S(2)}) copy-start(f32[256]{0:T(256)} %param.15) | copy-start | bytes 3076
  77.5 8.3 %copy-start.7 = (s32[64]{0:T(128)S(1)}, s32[64]{0:T(128)}, u32[]{:S(2)}) copy-start(s32[64]{0:T(128)} %param.17) | copy-start | bytes 772
  77.5 8.3 %collective-permute-start.10 = (f32[2,2,64,256]{3,2,1,0:T(8,128)S(1)}, f32[2,2,64,256]{3,2,1,0:T(8,128)S(1)}, u32[]{:S(2)}, u32[]{:S(2)}) collective-permute-start(f32[2,2,64,256]{3,2,1,0:T(8,128)S(1)} %shard_map.97), channel_id=1, source_target_pairs={{0,32},{1,33},{2,34},{3,35},{4,36},{5,37},{6,38},{7,39},{8,40},{9,... | collective-permute-start | bytes 786440 | tf_op jit(solution)/shard_map/ppermute | solution.py:270

commit v8 on v6

--- a/solution.py
+++ b/solution.py
@@ -332,9 +332,9 @@
 
     beside, second = along(to_beside, 1, -1), along(weights, None, 2)
     gathered = lax.all_to_all(spread, ("z", "x"), 0, 0, tiled=True)
-    edge = along(edge, -1, 1)
     near = beside[:SHARD].reshape(27, GW, CO)
     a0 = jnp.where(core == 0, jnp.stack([weights, near]), jnp.stack([second, near]))
+    edge = along(lax.optimization_barrier((edge, a0))[0], -1, 1)
     a1 = ring(a0)
     b1 = shift(a0, lambda y, core, z, x: (y, 1 - core, z - 1 + 2 * core, x))
     windows = call_pack(latent, beside, edge, gathered)

time: 87.5 us -> 88.3 us (level)
  waiting for transfers between devices: 3.88 us -> 8.41 us
  starting transfers between devices: 67.2 us -> 63.6 us
    ppermute x11, starting transfers between devices: 55.3 us -> 50.8 us  [shift(): return lax.ppermute(value, AXES, pairs)]
    ppermute x11, waiting for transfers between devices: 3.81 us -> 7.49 us  [shift(): return lax.ppermute(value, AXES, pairs)]
  transfers between devices with their start and end apart: 13 -> 13, of which waited for: 3 -> 5; matrix products, arithmetic and copies ran while one was open for 1% -> 1% of each run, Pallas kernels for 11% -> 11%
where the time goes in v8:
time: 88.3 us; the launch traced here: 87.6 us
  starting transfers between devices  63.6 us (72%)
  Pallas kernels  13.5 us (15%)
  waiting for transfers between devices  8.41 us (10%)
  other arithmetic  1.04 us (1%)
    ppermute x11, starting transfers between devices, shift(): return lax.ppermute(value, AXES, pairs)  50.8 us
    all_to_all x1, starting transfers between devices, local(): columns = lax.all_to_all(windows, ('y', 'core'), 0, 0, tiled=True)  8.93 us
    ppermute x11, waiting for transfers between devices, shift(): return lax.ppermute(value, AXES, pairs)  7.49 us
    pallas_call x3, Pallas kernels, part(): pl.pallas_call(kernel, out_shape=struct((2, 2, T, CO), F32), in_specs=[VM...  5.07 us
    all_to_all x1, starting transfers between devices, local(): gathered = lax.all_to_all(spread, ('z', 'x'), 0, 0, tiled=True)  3.87 us
    pallas_call x1, Pallas kernels, call_activate(): pl.pallas_call(activate, out_shape=(struct((3, 4, 6, T, HALF), BF16), str...  3.39 us
    pallas_call x1, Pallas kernels, call_prepare(): pl.pallas_call(prepare, out_shape=(struct((NZ * NX, 8, 128), F32), struct...  3.14 us
  transfers between devices with their start and end apart: 13, of which 5 were waited for; matrix products, arithmetic and copies ran while one was open for 1% of the time, Pallas kernels for 11%

profile of v8, /device:TPU:1, one launch (start us, length us, event | category | flops | bytes accessed | tf_op | source)
XLA Modules:
  0.0 87.6 jit_solution(15971660128459790005)
XLA Ops:
  0.0 3.1 %shard_map.91 = (f32[32,8,128]{2,1,0:T(8,128)}, bf16[688,256]{1,0:T(8,128)(2,1)}, bf16[128,512]{1,0:T(8,128)(2,1)}) custom-call(bf16[4,2,32,512]{3,2,1,0:T(8,128)(2,1)} %bitcast.11, bf16[27,16,256]{2,1,0:T(8,128)(2,1)} %bitcast.20), custom_call_target="tpu_custom_call" | custom-call | flops 65536 | bytes 65536 | tf_op jit(solution)/shard_map/pallas_call | solution.py:281
  3.2 3.9 %collective-permute-start = (bf16[688,256]{1,0:T(8,128)(2,1)}, bf16[688,256]{1,0:T(8,128)(2,1)S(1)}, u32[]{:S(2)}, u32[]{:S(2)}) collective-permute-start(bf16[688,256]{1,0:T(8,128)(2,1)} %get-tuple-element.12), channel_id=1, source_target_pairs={{0,31},{1,0},{2,1},{3,2},{4,3},{5,4},{6,5},{7,6},{8,7},{9,8},{10,9... | collective-permute-start | bytes 1056776 | tf_op jit(solution)/shard_map/ppermute | solution.py:261
  7.1 12.8 %collective-permute-start.1 = (bf16[27,16,256]{2,1,0:T(8,128)(2,1)}, bf16[27,16,256]{2,1,0:T(8,128)(2,1)S(1)}, u32[]{:S(2)}, u32[]{:S(2)}) collective-permute-start(bf16[27,16,256]{2,1,0:T(8,128)(2,1)} %bitcast.21), channel_id=1, source_target_pairs={{32,62},{33,63},{34,32},{35,33},{36,34},{37,35},{38,36},{39,37},{4... | collective-permute-start | bytes 663560 | tf_op jit(solution)/shard_map/ppermute | solution.py:261
  20.0 3.9 %all-to-all-start = ((f32[32,8,128]{2,1,0:T(8,128)}), f32[32,8,128]{2,1,0:T(8,128)S(1)}, u32[]{:S(2)}, u32[]{:S(2)}) async-start(f32[32,8,128]{2,1,0:T(8,128)} %get-tuple-element.15), calls=%async_computation | async-start | bytes 262144 | tf_op jit(solution)/shard_map/all_to_all | solution.py:334
  23.8 0.0 collective-permute-done.beside_ref
  23.9 2.8 %collective-permute-done.1 = bf16[27,16,256]{2,1,0:T(8,128)(2,1)S(1)} collective-permute-done((bf16[27,16,256]{2,1,0:T(8,128)(2,1)}, bf16[27,16,256]{2,1,0:T(8,128)(2,1)S(1)}, u32[]{:S(2)}, u32[]{:S(2)}) %collective-permute-start.1) | collective-permute-done | bytes 221216 | tf_op jit(solution)/shard_map/ppermute | solution.py:261
  26.7 1.0 %fusion.refs_0_ = bf16[2,27,16,256]{3,2,1,0:T(8,128)(2,1)S(1)} fusion(bf16[1,27,16,256]{3,2,1,0:T(8,128)(2,1)S(1)} %bitcast.19, bf16[1,27,16,256]{3,2,1,0:T(8,128)(2,1)} %bitcast.22, bf16[1,27,16,256]{3,2,1,0:T(8,128)(2,1)S(1)} %bitcast.23, pred[]{:T(512)S(6)} %eq.3), kind=kLoop, calls=%fused_computation.2 | loop fusion | flops 663552 | bytes 1105921 | tf_op jit(solution)/shard_map/jit(_where)/select_n | solution.py:336
  27.7 4.6 %collective-permute-start.2 = (bf16[128,512]{1,0:T(8,128)(2,1)}, bf16[128,512]{1,0:T(8,128)(2,1)S(1)}, u32[]{:S(2)}, u32[]{:S(2)}) collective-permute-start(bf16[128,512]{1,0:T(8,128)(2,1)} %get-tuple-element.14), channel_id=1, source_target_pairs={{0,1},{1,2},{2,3},{3,4},{4,5},{5,6},{6,7},{7,8},{8,9},{9,10},{10,1... | collective-permute-start | bytes 393224 | tf_op jit(solution)/shard_map/ppermute | solution.py:261
  32.3 1.9 %collective-permute-start.4 = (bf16[2,27,16,256]{3,2,1,0:T(8,128)(2,1)S(1)}, bf16[2,27,16,256]{3,2,1,0:T(8,128)(2,1)S(1)}, u32[]{:S(2)}, u32[]{:S(2)}) collective-permute-start(bf16[2,27,16,256]{3,2,1,0:T(8,128)(2,1)S(1)} %fusion.refs_0_), channel_id=1, source_target_pairs={{0,60},{1,61},{2,62},{3,63},{4,32},{5,33},{6,34},{7,35},{8,36},{9,... | collective-permute-start | bytes 1327112 | tf_op jit(solution)/shard_map/ppermute | solution.py:261
  34.3 2.2 %collective-permute-start.3 = (bf16[2,27,16,256]{3,2,1,0:T(8,128)(2,1)S(1)}, bf16[2,27,16,256]{3,2,1,0:T(8,128)(2,1)S(1)}, u32[]{:S(2)}, u32[]{:S(2)}) collective-permute-start(bf16[2,27,16,256]{3,2,1,0:T(8,128)(2,1)S(1)} %fusion.refs_0_), channel_id=1, source_target_pairs={{0,4},{1,5},{2,6},{3,7},{4,8},{5,9},{6,10},{7,11},{8,12},{9,13},{1... | collective-permute-start | bytes 1327112 | tf_op jit(solution)/shard_map/ppermute | solution.py:261
  36.5 0.0 all-to-all-done.sums_ref
  36.5 1.7 %shard_map.92 = bf16[16,112,256]{2,1,0:T(8,128)(2,1)} custom-call(bf16[4,2,32,512]{3,2,1,0:T(8,128)(2,1)S(1)} %bitcast.12, bf16[688,256]{1,0:T(8,128)(2,1)S(1)} %collective-permute-done.beside_ref, bf16[128,512]{1,0:T(8,128)(2,1)S(1)} %collective-permute-done.2.edge_ref, f32[32,8,128]{2,1,0:T(8,128)S(1)} %all-to-all-done.sums_ref), custom_call_target="tpu_custom_call" | custom-call | flops 65536 | bytes 65536 | tf_op jit(solution)/shard_map/pallas_call | solution.py:293
  38.3 8.9 %all-to-all-start.1 = ((bf16[16,112,256]{2,1,0:T(8,128)(2,1)}), bf16[16,112,256]{2,1,0:T(8,128)(2,1)S(1)}, u32[]{:S(2)}, u32[]{:S(2)}) async-start(bf16[16,112,256]{2,1,0:T(8,128)(2,1)} %shard_map.92), calls=%async_computation.1 | async-start | bytes 1835008 | tf_op jit(solution)/shard_map/all_to_all | solution.py:341
  47.2 3.4 %collective-permute-start.5 = (bf16[2,27,16,256]{3,2,1,0:T(8,128)(2,1)S(1)}, bf16[2,27,16,256]{3,2,1,0:T(8,128)(2,1)S(1)}, u32[]{:S(2)}, u32[]{:S(2)}) collective-permute-start(bf16[2,27,16,256]{3,2,1,0:T(8,128)(2,1)S(1)} %collective-permute-done.3.refs_1_), channel_id=1, source_target_pairs={{0,4},{1,5},{2,6},{3,7},{4,8},{5,9},{6,10},{7,11},{8,12},{9,13},{1... | collective-permute-start | bytes 1327112 | tf_op jit(solution)/shard_map/ppermute | solution.py:261
  50.6 1.9 %collective-permute-start.6 = (bf16[2,27,16,256]{3,2,1,0:T(8,128)(2,1)S(1)}, bf16[2,27,16,256]{3,2,1,0:T(8,128)(2,1)}, u32[]{:S(2)}, u32[]{:S(2)}) collective-permute-start(bf16[2,27,16,256]{3,2,1,0:T(8,128)(2,1)S(1)} %collective-permute-done.4.refs_2_), channel_id=1, source_target_pairs={{0,4},{1,5},{2,6},{3,7},{4,8},{5,9},{6,10},{7,11},{8,12},{9,13},{1... | collective-permute-start | bytes 1327112 | tf_op jit(solution)/shard_map/ppermute | solution.py:261
  52.6 4.0 %collective-permute-done.5.refs_3_ = bf16[2,27,16,256]{3,2,1,0:T(8,128)(2,1)S(1)} collective-permute-done((bf16[2,27,16,256]{3,2,1,0:T(8,128)(2,1)S(1)}, bf16[2,27,16,256]{3,2,1,0:T(8,128)(2,1)S(1)}, u32[]{:S(2)}, u32[]{:S(2)}) %collective-permute-start.5) | collective-permute-done | bytes 442400 | tf_op jit(solution)/shard_map/ppermute | solution.py:261
  56.5 4.6 %collective-permute-start.7 = (bf16[2,27,16,256]{3,2,1,0:T(8,128)(2,1)S(1)}, bf16[2,27,16,256]{3,2,1,0:T(8,128)(2,1)}, u32[]{:S(2)}, u32[]{:S(2)}) collective-permute-start(bf16[2,27,16,256]{3,2,1,0:T(8,128)(2,1)S(1)} %collective-permute-done.5.refs_3_), channel_id=1, source_target_pairs={{0,4},{1,5},{2,6},{3,7},{4,8},{5,9},{6,10},{7,11},{8,12},{9,13},{1... | collective-permute-start | bytes 1327112 | tf_op jit(solution)/shard_map/ppermute | solution.py:261
  61.2 0.2 collective-permute-done.6.refs_4_
  61.4 4.5 %collective-permute-start.8 = (bf16[2,27,16,256]{3,2,1,0:T(8,128)(2,1)}, bf16[2,27,16,256]{3,2,1,0:T(8,128)(2,1)}, u32[]{:S(2)}, u32[]{:S(2)}) collective-permute-start(bf16[2,27,16,256]{3,2,1,0:T(8,128)(2,1)} %collective-permute-done.6.refs_4_), channel_id=1, source_target_pairs={{0,4},{1,5},{2,6},{3,7},{4,8},{5,9},{6,10},{7,11},{8,12},{9,13},{1... | collective-permute-start | bytes 1327112 | tf_op jit(solution)/shard_map/ppermute | solution.py:261
  65.9 0.5 collective-permute-done.7.refs_5_
  66.4 5.2 %collective-permute-start.9 = (bf16[2,27,16,256]{3,2,1,0:T(8,128)(2,1)}, bf16[2,27,16,256]{3,2,1,0:T(8,128)(2,1)S(1)}, u32[]{:S(2)}, u32[]{:S(2)}) collective-permute-start(bf16[2,27,16,256]{3,2,1,0:T(8,128)(2,1)} %collective-permute-done.7.refs_5_), channel_id=1, source_target_pairs={{0,4},{1,5},{2,6},{3,7},{4,8},{5,9},{6,10},{7,11},{8,12},{9,13},{1... | collective-permute-start | bytes 1327112 | tf_op jit(solution)/shard_map/ppermute | solution.py:261
  71.6 0.9 %all-to-all-done.1.x_ref = bf16[16,112,256]{2,1,0:T(8,128)(2,1)S(1)} async-done(((bf16[16,112,256]{2,1,0:T(8,128)(2,1)}), bf16[16,112,256]{2,1,0:T(8,128)(2,1)S(1)}, u32[]{:S(2)}, u32[]{:S(2)}) %all-to-all-start.1) | async-done | bytes 917536 | tf_op jit(solution)/shard_map/all_to_all | solution.py:341
  72.5 3.4 %shard_map.93 = (bf16[3,4,6,64,256]{4,3,2,1,0:T(8,128)(2,1)S(1)}, bf16[4,4,64,384]{3,2,1,0:T(8,128)(2,1)S(1)}) custom-call(s32[10]{0:T(128)S(1)} %copy-done.6, f32[1,512]{1,0:T(1,128)S(1)} %bitcast.13, f32[1,512]{1,0:T(1,128)S(1)} %bitcast.14, f32[1,512]{1,0:T(1,128)S(1)} %bitcast.15, bf16[16,112,256]{2,1,0:T(8,128)(2,1)S(1)} %all-to-all-done.1.x_ref), custom_call_target="tpu_custom_call" | custom-call | flops 65536 | bytes 65536 | tf_op jit(solution)/shard_map/pallas_call | solution.py:300
  75.9 2.4 %shard_map.95.part_ref = f32[2,2,64,256]{3,2,1,0:T(8,128)S(1)} custom-call(bf16[3,4,6,64,256]{4,3,2,1,0:T(8,128)(2,1)S(1)} %get-tuple-element.16.act_ref, bf16[2,27,16,256]{3,2,1,0:T(8,128)(2,1)S(1)} %fusion.refs_0_, bf16[2,27,16,256]{3,2,1,0:T(8,128)(2,1)S(1)} %collective-permute-done.3.refs_1_, ...), custom_call_target="tpu_custom_call" | custom-call | flops 65536 | bytes 65536 | tf_op jit(solution)/shard_map/pallas_call | solution.py:349
  78.3 0.4 shard_map.96
  78.6 0.0 copy-start.4
  78.7 0.0 copy-start.5
  78.7 0.0 copy-start.7
  78.7 5.6 %collective-permute-start.10 = (f32[2,2,64,256]{3,2,1,0:T(8,128)S(1)}, f32[2,2,64,256]{3,2,1,0:T(8,128)S(1)}, u32[]{:S(2)}, u32[]{:S(2)}) collective-permute-start(f32[2,2,64,256]{3,2,1,0:T(8,128)S(1)} %shard_map.96), channel_id=1, source_target_pairs={{0,32},{1,33},{2,34},{3,35},{4,36},{5,37},{6,38},{7,39},{8,40},{9,... | collective-permute-start | bytes 786440 | tf_op jit(solution)/shard_map/ppermute | solution.py:261
  84.3 2.4 %shard_map.94.a_ref = f32[2,2,64,256]{3,2,1,0:T(8,128)S(1)} custom-call(bf16[3,4,6,64,256]{4,3,2,1,0:T(8,128)(2,1)S(1)} %get-tuple-element.16.act_ref, bf16[2,27,16,256]{3,2,1,0:T(8,128)(2,1)S(1)} %fusion.refs_0_, bf16[2,27,16,256]{3,2,1,0:T(8,128)(2,1)S(1)} %collective-permute-done.3.refs_1_, bf16[2,27,16,256]{3,2,1,0:T(8,128)(2,1)S(1)} %collective-permute-done.4.refs_2_, ...), custom_call_target="tpu_custom_call" | custom-call | flops 65536 | bytes 65536 | tf_op jit(solution)/shard_map/pallas_call | solution.py:349
  86.7 0.2 shard_map.97
  86.9 0.7 reshape.7
  (20 shorter events, 0.1 us)
Async XLA Ops:
  0.0 36.5 %copy-start = (bf16[1,4,2,32,512]{4,3,2,1,0:T(8,128)(2,1)S(1)}, bf16[1,4,2,32,512]{4,3,2,1,0:T(8,128)(2,1)}, u32[]{:S(2)}) copy-start(bf16[1,4,2,32,512]{4,3,2,1,0:T(8,128)(2,1)} %param.9) | copy-start | bytes 786436
  3.2 20.7 %collective-permute-start = (bf16[688,256]{1,0:T(8,128)(2,1)}, bf16[688,256]{1,0:T(8,128)(2,1)S(1)}, u32[]{:S(2)}, u32[]{:S(2)}) collective-permute-start(bf16[688,256]{1,0:T(8,128)(2,1)} %get-tuple-element.12), channel_id=1, source_target_pairs={{0,31},{1,0},{2,1},{3,2},{4,3},{5,4},{6,5},{7,6},{8,7},{9,8},{10,9... | collective-permute-start | bytes 1056776 | tf_op jit(solution)/shard_map/ppermute | solution.py:261
  7.1 19.6 %collective-permute-start.1 = (bf16[27,16,256]{2,1,0:T(8,128)(2,1)}, bf16[27,16,256]{2,1,0:T(8,128)(2,1)S(1)}, u32[]{:S(2)}, u32[]{:S(2)}) collective-permute-start(bf16[27,16,256]{2,1,0:T(8,128)(2,1)} %bitcast.21), channel_id=1, source_target_pairs={{32,62},{33,63},{34,32},{35,33},{36,34},{37,35},{38,36},{39,37},{4... | collective-permute-start | bytes 663560 | tf_op jit(solution)/shard_map/ppermute | solution.py:261
  20.0 16.6 %all-to-all-start = ((f32[32,8,128]{2,1,0:T(8,128)}), f32[32,8,128]{2,1,0:T(8,128)S(1)}, u32[]{:S(2)}, u32[]{:S(2)}) async-start(f32[32,8,128]{2,1,0:T(8,128)} %get-tuple-element.15), calls=%async_computation | async-start | bytes 262144 | tf_op jit(solution)/shard_map/all_to_all | solution.py:334
  26.7 45.8 %copy-start.1 = (f32[512]{0:T(512)S(1)}, f32[512]{0:T(512)}, u32[]{:S(2)}) copy-start(f32[512]{0:T(512)} %param.10) | copy-start | bytes 6148
  26.7 45.8 %copy-start.2 = (f32[512]{0:T(512)S(1)}, f32[512]{0:T(512)}, u32[]{:S(2)}) copy-start(f32[512]{0:T(512)} %param.11) | copy-start | bytes 6148
  26.7 45.8 %copy-start.3 = (f32[512]{0:T(512)S(1)}, f32[512]{0:T(512)}, u32[]{:S(2)}) copy-start(f32[512]{0:T(512)} %param.12) | copy-start | bytes 6148
  26.7 45.8 %copy-start.6 = (s32[10]{0:T(128)S(1)}, s32[10]{0:T(128)}, u32[]{:S(2)}) copy-start(s32[10]{0:T(128)} %lengths_ref.1) | copy-start | bytes 124
  27.7 8.8 %collective-permute-start.2 = (bf16[128,512]{1,0:T(8,128)(2,1)}, bf16[128,512]{1,0:T(8,128)(2,1)S(1)}, u32[]{:S(2)}, u32[]{:S(2)}) collective-permute-start(bf16[128,512]{1,0:T(8,128)(2,1)} %get-tuple-element.14), channel_id=1, source_target_pairs={{0,1},{1,2},{2,3},{3,4},{4,5},{5,6},{6,7},{7,8},{8,9},{9,10},{10,1... | collective-permute-start | bytes 393224 | tf_op jit(solution)/shard_map/ppermute | solution.py:261
  32.3 14.8 %collective-permute-start.4 = (bf16[2,27,16,256]{3,2,1,0:T(8,128)(2,1)S(1)}, bf16[2,27,16,256]{3,2,1,0:T(8,128)(2,1)S(1)}, u32[]{:S(2)}, u32[]{:S(2)}) collective-permute-start(bf16[2,27,16,256]{3,2,1,0:T(8,128)(2,1)S(1)} %fusion.refs_0_), channel_id=1, source_target_pairs={{0,60},{1,61},{2,62},{3,63},{4,32},{5,33},{6,34},{7,35},{8,36},{9,... | collective-permute-start | bytes 1327112 | tf_op jit(solution)/shard_map/ppermute | solution.py:261
  34.3 12.9 %collective-permute-start.3 = (bf16[2,27,16,256]{3,2,1,0:T(8,128)(2,1)S(1)}, bf16[2,27,16,256]{3,2,1,0:T(8,128)(2,1)S(1)}, u32[]{:S(2)}, u32[]{:S(2)}) collective-permute-start(bf16[2,27,16,256]{3,2,1,0:T(8,128)(2,1)S(1)} %fusion.refs_0_), channel_id=1, source_target_pairs={{0,4},{1,5},{2,6},{3,7},{4,8},{5,9},{6,10},{7,11},{8,12},{9,13},{1... | collective-permute-start | bytes 1327112 | tf_op jit(solution)/shard_map/ppermute | solution.py:261
  38.3 34.2 %all-to-all-start.1 = ((bf16[16,112,256]{2,1,0:T(8,128)(2,1)}), bf16[16,112,256]{2,1,0:T(8,128)(2,1)S(1)}, u32[]{:S(2)}, u32[]{:S(2)}) async-start(bf16[16,112,256]{2,1,0:T(8,128)(2,1)} %shard_map.92), calls=%async_computation.1 | async-start | bytes 1835008 | tf_op jit(solution)/shard_map/all_to_all | solution.py:341
  47.2 9.3 %collective-permute-start.5 = (bf16[2,27,16,256]{3,2,1,0:T(8,128)(2,1)S(1)}, bf16[2,27,16,256]{3,2,1,0:T(8,128)(2,1)S(1)}, u32[]{:S(2)}, u32[]{:S(2)}) collective-permute-start(bf16[2,27,16,256]{3,2,1,0:T(8,128)(2,1)S(1)} %collective-permute-done.3.refs_1_), channel_id=1, source_target_pairs={{0,4},{1,5},{2,6},{3,7},{4,8},{5,9},{6,10},{7,11},{8,12},{9,13},{1... | collective-permute-start | bytes 1327112 | tf_op jit(solution)/shard_map/ppermute | solution.py:261
  50.6 10.7 %collective-permute-start.6 = (bf16[2,27,16,256]{3,2,1,0:T(8,128)(2,1)S(1)}, bf16[2,27,16,256]{3,2,1,0:T(8,128)(2,1)}, u32[]{:S(2)}, u32[]{:S(2)}) collective-permute-start(bf16[2,27,16,256]{3,2,1,0:T(8,128)(2,1)S(1)} %collective-permute-done.4.refs_2_), channel_id=1, source_target_pairs={{0,4},{1,5},{2,6},{3,7},{4,8},{5,9},{6,10},{7,11},{8,12},{9,13},{1... | collective-permute-start | bytes 1327112 | tf_op jit(solution)/shard_map/ppermute | solution.py:261
  56.5 9.9 %collective-permute-start.7 = (bf16[2,27,16,256]{3,2,1,0:T(8,128)(2,1)S(1)}, bf16[2,27,16,256]{3,2,1,0:T(8,128)(2,1)}, u32[]{:S(2)}, u32[]{:S(2)}) collective-permute-start(bf16[2,27,16,256]{3,2,1,0:T(8,128)(2,1)S(1)} %collective-permute-done.5.refs_3_), channel_id=1, source_target_pairs={{0,4},{1,5},{2,6},{3,7},{4,8},{5,9},{6,10},{7,11},{8,12},{9,13},{1... | collective-permute-start | bytes 1327112 | tf_op jit(solution)/shard_map/ppermute | solution.py:261
  61.4 14.5 %collective-permute-start.8 = (bf16[2,27,16,256]{3,2,1,0:T(8,128)(2,1)}, bf16[2,27,16,256]{3,2,1,0:T(8,128)(2,1)}, u32[]{:S(2)}, u32[]{:S(2)}) collective-permute-start(bf16[2,27,16,256]{3,2,1,0:T(8,128)(2,1)} %collective-permute-done.6.refs_4_), channel_id=1, source_target_pairs={{0,4},{1,5},{2,6},{3,7},{4,8},{5,9},{6,10},{7,11},{8,12},{9,13},{1... | collective-permute-start | bytes 1327112 | tf_op jit(solution)/shard_map/ppermute | solution.py:261
  66.4 11.9 %collective-permute-start.9 = (bf16[2,27,16,256]{3,2,1,0:T(8,128)(2,1)}, bf16[2,27,16,256]{3,2,1,0:T(8,128)(2,1)S(1)}, u32[]{:S(2)}, u32[]{:S(2)}) collective-permute-start(bf16[2,27,16,256]{3,2,1,0:T(8,128)(2,1)} %collective-permute-done.7.refs_5_), channel_id=1, source_target_pairs={{0,4},{1,5},{2,6},{3,7},{4,8},{5,9},{6,10},{7,11},{8,12},{9,13},{1... | collective-permute-start | bytes 1327112 | tf_op jit(solution)/shard_map/ppermute | solution.py:261
  78.6 8.0 %copy-start.4 = (f32[256]{0:T(256)S(1)}, f32[256]{0:T(256)}, u32[]{:S(2)}) copy-start(f32[256]{0:T(256)} %param.14) | copy-start | bytes 3076
  78.7 8.0 %copy-start.5 = (f32[256]{0:T(256)S(1)}, f32[256]{0:T(256)}, u32[]{:S(2)}) copy-start(f32[256]{0:T(256)} %param.15) | copy-start | bytes 3076
  78.7 8.0 %copy-start.7 = (s32[64]{0:T(128)S(1)}, s32[64]{0:T(128)}, u32[]{:S(2)}) copy-start(s32[64]{0:T(128)} %param.17) | copy-start | bytes 772
  78.7 8.0 %collective-permute-start.10 = (f32[2,2,64,256]{3,2,1,0:T(8,128)S(1)}, f32[2,2,64,256]{3,2,1,0:T(8,128)S(1)}, u32[]{:S(2)}, u32[]{:S(2)}) collective-permute-start(f32[2,2,64,256]{3,2,1,0:T(8,128)S(1)} %shard_map.96), channel_id=1, source_target_pairs={{0,32},{1,33},{2,34},{3,35},{4,36},{5,37},{6,38},{7,39},{8,40},{9,... | collective-permute-start | bytes 786440 | tf_op jit(solution)/shard_map/ppermute | solution.py:261
